TPU v7x, 32 devices: a whole 2x2x4 slice. The times are simulated.
32 devices in a mesh: seg: 2 (over x), ctx: 16 (over z, y, core).
Axes of the slice: x: 2, y: 2, z: 4, core: 2. Of those that a mesh axis runs over, the one named last changes fastest.
Arguments:
- hidden_in: bfloat16 [4096, 1024], P(('seg', 'ctx')), may hold values from -6 to 6
- queries: bfloat16 [4096, 1024], P(('seg', 'ctx')), may hold values from -6 to 6
- key_rows: bfloat16 [4096, 1024], P(('seg', 'ctx')), may hold values from -6 to 6
- values: bfloat16 [4096, 1024], P(('seg', 'ctx')), may hold values from -6 to 6
- norm_gain: float32 [1024], replicated, may hold values from 0.5 to 1.5
- out_proj: bfloat16 [1024, 1024], replicated, may hold values from -0.1875 to 0.1875
- moe_gain: float32 [1024], replicated, may hold values from 0.5 to 1.5
- w_gate: bfloat16 [16, 1024, 896], P('ctx'), may hold values from -0.1875 to 0.1875
- w_up: bfloat16 [16, 1024, 896], P('ctx'), may hold values from -0.1875 to 0.1875
- w_down: bfloat16 [16, 896, 1024], P('ctx'), may hold values from -0.1875 to 0.1875
- expert_ids: int32 [4096, 8], P(('seg', 'ctx')), may hold values from 0 to 15, all different within a row; in each aligned block of 128 rows (0 to 127, 128 to 255, ...) at most 96 rows name the same one
- route_scale: int32 [4096, 8], P(('seg', 'ctx')), may hold values from 1 to 4095
Outputs:
- layer_out: bfloat16 [4096, 1024], P(('seg', 'ctx'))
Inputs may be any that keep to these rules, and one draw needn't show every extreme that they name: `expert_ids`: each row names 8 different experts. Among the rows of one device no expert is named more than 96 times, and in every draw some device names some expert exactly 96 times.
All inputs are finite; a program needn't handle non-finite values.
Results may differ from a plain program's by a relative error of at most 0.0075.
Values may be sent and summed in bfloat16 or wider, within the bound.
No kernel may reach another device: no remote copies, remote signals or barrier semaphores. Data moves between devices by JAX's collectives and lax.ppermute only.
A program may use at most 192 MiB of HBM per device.

v0:
```python
import jax
import jax.numpy as jnp
from jax import lax
from jax.sharding import PartitionSpec as P

HEADS = 8
HEAD = 128
D = 1024
TOP = 8


def prefix(value, axis, join, neutral):
    count, mine = (lax.axis_size(axis), lax.axis_index(axis))
    pieces = lax.all_gather(value, axis)
    so_far = jnp.full_like(value, 0) + jnp.asarray(neutral, value.dtype)

    def hop(position, so_far):
        longer = join(so_far, pieces[position])
        return jnp.where(position < mine, longer, so_far)

    return lax.fori_loop(0, count - 1, hop, so_far)


def rms_scale(rows, gain):
    mean_sq = jnp.mean(rows * rows, axis=1, keepdims=True)
    return rows * lax.rsqrt(mean_sq + 1e-06) * gain[None, :]


def add_states(earlier, later):
    return earlier + later


def expert_rows(arrived, w_gate, w_up, w_down):
    sources, slots = (arrived.shape[0], arrived.shape[1])
    rows = arrived.reshape(sources * slots, D)
    gate = jnp.dot(rows, w_gate[0], preferred_element_type=jnp.float32)
    upper = jnp.dot(rows, w_up[0], preferred_element_type=jnp.float32)
    inner = (jax.nn.silu(gate) * upper).astype(jnp.bfloat16)
    result = jnp.dot(inner, w_down[0], preferred_element_type=jnp.float32).astype(jnp.bfloat16)
    return result.reshape(sources, slots, D)


def body(
    hidden_in,
    queries,
    key_rows,
    values,
    norm_gain,
    out_proj,
    moe_gain,
    w_gate,
    w_up,
    w_down,
    expert_ids,
    route_scale,
):
    ntok = queries.shape[0]
    high = lax.Precision.HIGHEST
    q_loc = queries.astype(jnp.float32).reshape(ntok, HEADS, HEAD)
    k_loc = key_rows.astype(jnp.float32).reshape(ntok, HEADS, HEAD)
    v_loc = values.astype(jnp.float32).reshape(ntok, HEADS, HEAD)
    own_state = jnp.einsum("thd,the->hde", k_loc, v_loc, precision=high)
    empty = jnp.zeros_like(own_state)
    earlier = prefix(own_state, ("seg", "ctx"), add_states, empty)
    causal = jnp.arange(ntok)[:, None] >= jnp.arange(ntok)[None, :]
    scores = jnp.einsum("thd,shd->hts", q_loc, k_loc, precision=high)
    scores = jnp.where(causal[None, :, :], scores, jnp.zeros((), jnp.float32))
    inside = jnp.einsum("hts,she->the", scores, v_loc, precision=high)
    carried = jnp.einsum("thd,hde->the", q_loc, earlier, precision=high)
    attended = (carried + inside).reshape(ntok, D)
    normed = rms_scale(attended, norm_gain).astype(jnp.bfloat16)
    mixed = hidden_in.astype(jnp.float32) + jnp.dot(
        normed, out_proj, preferred_element_type=jnp.float32
    )
    routed = rms_scale(mixed, moe_gain).astype(jnp.bfloat16)
    experts_all = lax.axis_size("ctx") * w_gate.shape[0]
    capacity = min(ntok, 3 * ntok * TOP // (2 * experts_all))
    expert_grid = jnp.arange(experts_all, dtype=jnp.int32)
    chosen = (expert_ids[:, :, None] == expert_grid[None, None, :]).astype(jnp.float32)
    per_token = jnp.sum(chosen, axis=1)
    lower = (jnp.arange(ntok)[:, None] > jnp.arange(ntok)[None, :]).astype(jnp.float32)
    before_tok = jnp.dot(lower, per_token, precision=high)
    position = jnp.sum(chosen * before_tok[:, None, :], axis=2).astype(jnp.int32)
    slot_id = expert_ids * capacity + position
    slot_grid = jnp.arange(experts_all * capacity, dtype=jnp.int32)
    placing = jnp.sum(
        (slot_id[:, :, None] == slot_grid[None, None, :]).astype(jnp.float32), axis=1
    ).astype(jnp.bfloat16)
    outgoing = jnp.einsum("ts,td->sd", placing, routed, preferred_element_type=jnp.float32)
    outgoing = outgoing.astype(jnp.bfloat16).reshape(experts_all, capacity, D)
    came_back = lax.all_to_all(
        expert_rows(
            lax.all_to_all(outgoing, "ctx", split_axis=0, concat_axis=0, tiled=True),
            w_gate,
            w_up,
            w_down,
        ),
        "ctx",
        split_axis=0,
        concat_axis=0,
        tiled=True,
    )
    back_rows = came_back.reshape(experts_all * capacity, D)
    picked = back_rows[slot_id.reshape(-1)].reshape(ntok, TOP, D).astype(jnp.float32)
    scales = route_scale.astype(jnp.float32)
    weight = scales / jnp.sum(scales, axis=1, keepdims=True)
    combined = jnp.sum(weight[:, :, None] * picked, axis=1)
    return (mixed + combined).astype(jnp.bfloat16)


def solution(mesh):
    return jax.shard_map(
        body,
        mesh=mesh,
        in_specs=(
            P(("seg", "ctx"), None),
            P(("seg", "ctx"), None),
            P(("seg", "ctx"), None),
            P(("seg", "ctx"), None),
            P(),
            P(),
            P(),
            P("ctx", None, None),
            P("ctx", None, None),
            P("ctx", None, None),
            P(("seg", "ctx"), None),
            P(("seg", "ctx"), None),
        ),
        out_specs=P(("seg", "ctx"), None),
        check_vma=False,
    )
```

profile of v0, /device:TPU:13, one launch (start us, length us, event | category | flops | bytes accessed | tf_op | source)
XLA Modules:
  0.0 355.3 jit_solution(13173482439660077862)
XLA Ops:
  6.5 0.0 copy-start
  6.5 1.3 copy.55
  7.8 2.1 fusion.12
  9.9 0.0 all-gather.3.cloned.1.call-update
  9.9 0.7 convert_reduce_fusion.1
  10.6 0.1 fusion.21
  10.8 0.8 select_reduce_fusion
  11.5 0.7 convert_add_fusion
  12.2 0.1 copy.52
  12.4 3.9 %convert_reduce_fusion = bf16[128,1536]{1,0:T(8,128)(2,1)} fusion(s32[128,8]{1,0:T(8,128)S(1)} %copy.52), kind=kLoop, calls=%fused_computation.2 | loop fusion | flops 4521984 | bytes 397312 | tf_op jit(solution)/shard_map/reduce_sum | solution.py:86
  16.2 1.3 convolution_select_fusion
  17.6 0.7 convolution_bitcast_fusion
  18.3 107.4 %all-gather.3.cloned.1.call-done = f32[256,128,128]{2,1,0:T(8,128)} async-done(((f32[8,128,128]{2,1,0:T(8,128)}), f32[256,128,128]{2,1,0:T(8,128)}) %all-gather.3.cloned.1.call-update) | async-done | bytes 16777232 | tf_op jit(solution)/shard_map/all_gather | solution.py:14
  125.6 38.8 %while.14 = (s32[]{:T(128)}, f32[8,128,128]{2,1,0:T(8,128)S(1)}, s32[]{:T(128)}, f32[32,8,128,128]{3,2,1,0:T(8,128)}, s32[]{:T(128)}, /*index=5*/s32[]{:T(128)}) while((s32[]{:T(128)}, f32[8,128,128]{2,1,0:T(8,128)S(1)}, s32[]{:T(128)}, f32[32,8,128,128]{3,2,1,0:T(8,128)}, s32[]{:T(128)}, /*index=5*/s32[]{:T(128)}) %tuple.39), condition=%wide.region_1.2_spmd.clone, body=%wide.region_0.1_spmd.clone.sunk | while | flops 393220 | bytes 1572957 | solution.py:21
  125.6 1.3 add_select_fusion.2
  126.9 1.2 add_select_fusion.2
  128.2 1.2 add_select_fusion.2
  129.4 1.2 add_select_fusion.2
  130.7 1.2 add_select_fusion.2
  131.9 1.2 add_select_fusion.2
  133.2 1.2 add_select_fusion.2
  134.4 1.2 add_select_fusion.2
  135.7 1.2 add_select_fusion.2
  136.9 1.2 add_select_fusion.2
  138.2 1.2 add_select_fusion.2
  139.4 1.2 add_select_fusion.2
  140.7 1.2 add_select_fusion.2
  141.9 1.2 add_select_fusion.2
  143.2 1.2 add_select_fusion.2
  144.4 1.2 add_select_fusion.2
  145.7 1.2 add_select_fusion.2
  146.9 1.2 add_select_fusion.2
  148.2 1.2 add_select_fusion.2
  149.4 1.2 add_select_fusion.2
  150.7 1.2 add_select_fusion.2
  151.9 1.2 add_select_fusion.2
  153.2 1.2 add_select_fusion.2
  154.4 1.2 add_select_fusion.2
  155.7 1.2 add_select_fusion.2
  156.9 1.2 add_select_fusion.2
  158.2 1.2 add_select_fusion.2
  159.4 1.2 add_select_fusion.2
  160.7 1.2 add_select_fusion.2
  161.9 1.2 add_select_fusion.2
  163.2 1.2 add_select_fusion.2
  164.4 0.0 copy-start.2
  164.4 0.0 copy-start.6
  164.5 0.6 multiply_reduce_fusion.1
  165.1 0.0 copy-done.5
  165.1 0.2 fusion.8
  165.3 1.5 multiply_reduce_fusion
  166.8 1.0 convolution_convert_fusion
  167.9 0.0 copy-start.7
  167.9 74.9 %all_to_all.10 = bf16[16,96,1024]{2,1,0:T(8,128)(2,1)S(1)} all-to-all(bf16[16,96,1024]{2,1,0:T(8,128)(2,1)S(1)} %bitcast.72), channel_id=1, replica_groups=mesh['seg'=2,'ctx'=16] {'ctx'}, dimensions={0} | all-to-all | bytes 6291456 | tf_op jit(solution)/shard_map/all_to_all | solution.py:93
  242.8 1.7 copy-done.1
  244.5 5.1 %fusion.4 = f32[1536,896]{1,0:T(8,128)} fusion(bf16[1536,1024]{1,0:T(8,128)(2,1)S(1)} %bitcast.74, bf16[1,1024,896]{2,1,0:T(8,128)(2,1)S(1)} %copy-done.7), kind=kOutput, calls=%fused_computation.11 | convolution fusion | flops 2818572288 | bytes 10485760 | tf_op jit(solution)/shard_map/dot_general | solution.py:36
  249.7 11.4 %convolution_convert_fusion.1 = bf16[1536,1024]{1,0:T(8,128)(2,1)} fusion(f32[1536,896]{1,0:T(8,128)} %fusion.4, bf16[1536,1024]{1,0:T(8,128)(2,1)} %bitcast.75, bf16[1,896,1024]{2,1,0:T(8,128)(2,1)} %param.23, bf16[1,1024,896]{2,1,0:T(8,128)(2,1)} %param.22), kind=kOutput, calls=%fused_computation.8 | convolution fusion | flops 5646974976 | bytes 15466496 | tf_op jit(solution)/shard_map/dot_general | solution.py:39
  261.1 5.3 %all-to-all-start.1 = ((bf16[16,96,1024]{2,1,0:T(8,128)(2,1)}), bf16[16,96,1024]{2,1,0:T(8,128)(2,1)}, u32[]{:S(2)}, u32[]{:S(2)}) async-start(bf16[16,96,1024]{2,1,0:T(8,128)(2,1)} %bitcast.73), calls=%async_computation.1 | async-start | bytes 6291456 | tf_op jit(solution)/shard_map/all_to_all | solution.py:91
  266.4 0.1 reshape.101
  266.6 0.1 copy.51
  266.7 69.7 %all-to-all-done.1 = bf16[16,96,1024]{2,1,0:T(8,128)(2,1)} async-done(((bf16[16,96,1024]{2,1,0:T(8,128)(2,1)}), bf16[16,96,1024]{2,1,0:T(8,128)(2,1)}, u32[]{:S(2)}, u32[]{:S(2)}) %all-to-all-start.1) | async-done | bytes 3145760 | tf_op jit(solution)/shard_map/all_to_all | solution.py:91
  336.4 8.3 %gather_fusion = bf16[1024,1024]{1,0:T(8,128)(2,1)} fusion(bf16[1536,1024]{1,0:T(8,128)(2,1)} %bitcast.10, s32[1024]{0:T(1024)S(1)} %broadcast_clamp_fusion), kind=kCustom, calls=%fused_computation | custom fusion | bytes 4198400 | tf_op jit(solution)/shard_map/gather | solution.py:104
  344.8 2.9 fusion
  347.7 0.8 add_convert_fusion
  (19 shorter events, 0.1 us)
Async XLA Ops:
  6.5 158.8 %copy-start = (bf16[1024,1024]{1,0:T(8,128)(2,1)S(1)}, bf16[1024,1024]{1,0:T(8,128)(2,1)}, u32[]{:S(2)}) copy-start(bf16[1024,1024]{1,0:T(8,128)(2,1)} %param.19) | copy-start | bytes 6291460
  6.5 119.1 %all-gather.3.cloned.1.call-start = ((), (), s32[]{:S(2)}) async-start(), calls=%async_computation.2 | async-start | bytes 17301504 | tf_op jit(solution)/shard_map/all_gather | solution.py:14
  125.6 38.8 %copy-start.3 = (bf16[128,1024]{1,0:T(8,128)(2,1)S(1)}, bf16[128,1024]{1,0:T(8,128)(2,1)}, u32[]{:S(2)}) copy-start(bf16[128,1024]{1,0:T(8,128)(2,1)} %param.15) | copy-start | bytes 786436
  125.6 39.5 %copy-start.5 = (f32[1024]{0:T(1024)S(1)}, f32[1024]{0:T(1024)}, u32[]{:S(2)}) copy-start(f32[1024]{0:T(1024)} %param.18) | copy-start | bytes 12292
  164.4 2.4 copy-start.2
  164.4 2.4 copy-start.6
  167.9 76.6 %copy-start.7 = (bf16[1,1024,896]{2,1,0:T(8,128)(2,1)S(1)}, bf16[1,1024,896]{2,1,0:T(8,128)(2,1)}, u32[]{:S(2)}) copy-start(bf16[1,1024,896]{2,1,0:T(8,128)(2,1)} %param.21) | copy-start | bytes 5505028
  242.8 1.7 copy-start.1
  261.1 5.4 %copy-start.4 = (s32[128,8]{0,1:T(8,128)S(1)}, s32[128,8]{0,1:T(8,128)}, u32[]{:S(2)}) copy-start(s32[128,8]{0,1:T(8,128)} %param.25) | copy-start | bytes 12292
  261.1 75.3 %all-to-all-start.1 = ((bf16[16,96,1024]{2,1,0:T(8,128)(2,1)}), bf16[16,96,1024]{2,1,0:T(8,128)(2,1)}, u32[]{:S(2)}, u32[]{:S(2)}) async-start(bf16[16,96,1024]{2,1,0:T(8,128)(2,1)} %bitcast.73), calls=%async_computation.1 | async-start | bytes 6291456 | tf_op jit(solution)/shard_map/all_to_all | solution.py:91
Sparse Core Ops, SparseCore 0:
  10.2 115.3 all-gather.2
where the time goes:
time: 357 us; the launch traced here: 355 us
  waiting for transfers between devices  177 us (50%)
  blocking collectives  74.9 us (21%)
  other arithmetic  48.1 us (13%)
  matrix products  23.9 us (7%)
  between operations  13.6 us (4%)
  local copies, waits for them, and re-layouts  11.7 us (3%)
  starting transfers between devices  5.33 us (1%)
    all_gather x1, waiting for transfers between devices, prefix(): pieces = lax.all_gather(value, axis)  107 us
    all_to_all x1, blocking collectives, body(): lax.all_to_all(outgoing, 'ctx', split_axis=0, concat_axis=0, tiled=True)  74.9 us
    all_to_all x1, waiting for transfers between devices, body(): lax.all_to_all(expert_rows(lax.all_to_all(outgoing, 'ctx', split_axis=0,...  69.7 us
    select_n x31, other arithmetic, hop(): return jnp.where(position < mine, longer, so_far)  38.1 us
    dot_general x1, matrix products, expert_rows(): jnp.dot(inner, w_down[0], preferred_element_type=jnp.float32)  11.4 us
    gather x1, local copies, waits for them, and re-layouts, body(): back_rows[slot_id.reshape(-1)].reshape(ntok, TOP, D).astype(jnp.float32)  8.34 us
  transfers between devices with their start and end apart: 2, of which 2 were waited for; matrix products, arithmetic and copies ran while one was open for 2% of the time, Pallas kernels for 0%

commit v1 on v0

v1 whole, which is shorter than its diff:
```python
import functools

import jax
import jax.numpy as jnp
from jax import lax
from jax.experimental import pallas as pl
from jax.experimental.pallas import tpu as pltpu
from jax.sharding import PartitionSpec as P

HEADS = 8
HEAD = 128
BOTH = ("seg", "ctx")
F32 = jnp.float32
BF16 = jnp.bfloat16


def rms_scale(rows, gain):
    mean_sq = jnp.mean(rows * rows, axis=1, keepdims=True)
    return rows * lax.rsqrt(mean_sq + 1e-06) * gain[None, :]


def chip_order(chips):
    return list(range(0, chips, 2)) + list(range(1, chips, 2))[::-1]


def ring_perm(chips, shift):
    order = chip_order(chips)
    pairs = []
    for place, chip in enumerate(order):
        target = order[(place + shift) % chips]
        pairs += [(chip * 2 + core, target * 2 + core) for core in range(2)]
    return pairs


def core_perm(chips):
    return [(dev, dev ^ 1) for dev in range(2 * chips)]


def scan_and_weights(own_state, dense):
    heads, rows, cols = own_state.shape
    ntok, owners = dense.shape
    segs, devices = lax.axis_size("seg"), lax.axis_size(BOTH)
    share = heads * rows // devices
    top = dense.astype(BF16)
    rest = (dense - top.astype(F32)).astype(BF16)
    split = jnp.stack([top.T, rest.T], axis=1).reshape(owners, 2 * ntok // cols, cols)
    split = jnp.broadcast_to(split[None], (segs,) + split.shape).reshape((devices,) + split.shape[1:])
    pieces = own_state.astype(BF16).reshape(devices, share, cols)
    pieces = jnp.concatenate([pieces, split], axis=1)
    pieces = lax.all_to_all(pieces, BOTH, split_axis=0, concat_axis=0, tiled=True)
    split = lax.dynamic_slice_in_dim(pieces[:, share:], lax.axis_index("seg") * owners, owners)
    split = split.reshape(owners, 2, ntok).astype(F32)
    mine = (split[:, 0] + split[:, 1]).T
    earlier = jnp.arange(devices)[:, None] > jnp.arange(devices)[None, :]
    sums = jnp.dot(
        earlier.astype(BF16),
        pieces[:, :share].reshape(devices, share * cols),
        preferred_element_type=F32,
    )
    sums = sums.astype(BF16).reshape(devices, share, cols)
    sums = lax.all_to_all(sums, BOTH, split_axis=0, concat_axis=0, tiled=True)
    return sums.reshape(heads, rows, cols), mine


def expert_kernel(count, sources, dense, w_gate, w_up, w_down, *refs):
    ntok = refs[0].shape[0]
    rows = jnp.concatenate([refs[i][...] for i in range(count)])
    gate = jnp.dot(rows, w_gate[0], preferred_element_type=F32)
    upper = jnp.dot(rows, w_up[0], preferred_element_type=F32)
    inner = (gate / (1.0 + jnp.exp(-gate)) * upper).astype(BF16)
    result = jnp.dot(inner, w_down[0], preferred_element_type=F32)
    table = dense[...]
    lane = lax.broadcasted_iota(jnp.int32, table.shape, 1)
    for i in range(count):
        picked = jnp.where(lane == sources[i], table, 0.0)
        scale = jnp.sum(picked, axis=1, keepdims=True)
        refs[count + i][...] = (result[i * ntok : (i + 1) * ntok] * scale).astype(BF16)


def expert(shards, sources, dense, w_gate, w_up, w_down):
    count, (ntok, width) = len(shards), shards[0].shape
    whole = pl.BlockSpec(memory_space=pltpu.VMEM)
    hidden = w_gate.shape[2]
    return pl.pallas_call(
        functools.partial(expert_kernel, count),
        out_shape=[jax.ShapeDtypeStruct((ntok, width), BF16)] * count,
        in_specs=[pl.BlockSpec(memory_space=pltpu.SMEM)] + [whole] * (4 + count),
        out_specs=[whole] * count,
        compiler_params=pltpu.CompilerParams(vmem_limit_bytes=32 * 1024 * 1024),
        cost_estimate=pl.CostEstimate(
            flops=6 * count * ntok * width * hidden, bytes_accessed=0, transcendentals=0
        ),
    )(jnp.stack(sources), dense, w_gate, w_up, w_down, *shards)


def body(
    hidden_in,
    queries,
    key_rows,
    values,
    norm_gain,
    out_proj,
    moe_gain,
    w_gate,
    w_up,
    w_down,
    expert_ids,
    route_scale,
):
    ntok, width = queries.shape
    owners = lax.axis_size("ctx")
    chips = owners // 2
    me = lax.axis_index("ctx")

    scales = route_scale.astype(F32)
    weight = scales / jnp.sum(scales, axis=1, keepdims=True)
    grid = jnp.arange(owners, dtype=jnp.int32)
    dense = jnp.sum(
        jnp.where(expert_ids[:, :, None] == grid[None, None, :], weight[:, :, None], 0.0), axis=1
    )

    q_loc = queries.reshape(ntok, HEADS, HEAD)
    k_loc = key_rows.reshape(ntok, HEADS, HEAD)
    v_loc = values.reshape(ntok, HEADS, HEAD)
    own_state = jnp.einsum("thd,the->hde", k_loc, v_loc, preferred_element_type=F32)
    earlier, mine_dense = scan_and_weights(own_state, dense)
    causal = jnp.arange(ntok)[:, None] >= jnp.arange(ntok)[None, :]
    scores = jnp.einsum("thd,shd->hts", q_loc, k_loc, preferred_element_type=F32)
    scores = jnp.where(causal[None, :, :], scores, 0.0).astype(BF16)
    inside = jnp.einsum("hts,she->the", scores, v_loc, preferred_element_type=F32)
    carried = jnp.einsum("thd,hde->the", q_loc, earlier, preferred_element_type=F32)
    attended = (carried + inside).reshape(ntok, width)
    normed = rms_scale(attended, norm_gain).astype(BF16)
    mixed = hidden_in.astype(F32) + jnp.dot(normed, out_proj, preferred_element_type=F32)
    routed = rms_scale(mixed, moe_gain).astype(BF16)

    half = chips // 2
    cut = ntok // 2
    order = chip_order(chips)
    place_of = [order.index(chip) for chip in range(chips)]
    place = jnp.asarray(place_of, jnp.int32)[me // 2]
    up, down, swap = ring_perm(chips, 1), ring_perm(chips, -1), core_perm(chips)

    from_below, from_above = [routed], [routed]
    for step in range(1, half):
        from_below.append(lax.ppermute(from_below[-1], "ctx", up))
        from_above.append(lax.ppermute(from_above[-1], "ctx", down))
    far = jnp.concatenate(
        [
            lax.ppermute(from_below[-1][:cut], "ctx", up),
            lax.ppermute(from_above[-1][cut:], "ctx", down),
        ]
    )
    shards = {0: routed, half: far}
    for step in range(1, half):
        shards[-step] = from_below[step]
        shards[step] = from_above[step]

    parts = {}
    for step in range(half + 1):
        offsets = [step] if step in (0, half) else [step, -step]
        group, sources = [], []
        for offset in offsets:
            chip = jnp.asarray(order, jnp.int32)[(place + offset) % chips]
            source = chip * 2 + me % 2
            group += [shards[offset], lax.ppermute(shards[offset], "ctx", swap)]
            sources += [source, source ^ 1]
        results = expert(group, sources, mine_dense, w_gate, w_up, w_down)
        for i, offset in enumerate(offsets):
            partner = lax.ppermute(results[2 * i + 1], "ctx", swap)
            parts[offset] = results[2 * i].astype(F32) + partner.astype(F32)

    far = parts[half].astype(BF16)
    going_up = lax.ppermute(far[:cut], "ctx", up).astype(F32)
    going_down = lax.ppermute(far[cut:], "ctx", down).astype(F32)
    blank = jnp.zeros((ntok - cut, width), F32)
    going_up = jnp.concatenate([going_up, blank])
    going_down = jnp.concatenate([blank[:cut], going_down])
    for step in range(half - 1, 0, -1):
        going_up = lax.ppermute((parts[step] + going_up).astype(BF16), "ctx", up).astype(F32)
        going_down = lax.ppermute((parts[-step] + going_down).astype(BF16), "ctx", down).astype(F32)
    return (mixed + parts[0] + going_up + going_down).astype(BF16)


def solution(mesh):
    rows = P(BOTH, None)
    expert_spec = P("ctx", None, None)
    return jax.shard_map(
        body,
        mesh=mesh,
        in_specs=(rows,) * 4 + (P(),) * 3 + (expert_spec,) * 3 + (rows,) * 2,
        out_specs=rows,
        check_vma=False,
    )
```

time: 357 us -> 129 us (0.36)
  the two profiles are of different devices: /device:TPU:13 before, /device:TPU:0 now
where the time goes in v1:
time: 129 us; the launch traced here: 128 us
  waiting for transfers between devices  36 us (28%)
  starting transfers between devices  22.5 us (17%)
  blocking collectives  18.9 us (15%)
  Pallas kernels  17.3 us (13%)
  local copies, waits for them, and re-layouts  12.9 us (10%)
  between operations  11.4 us (9%)
  matrix products  4.85 us (4%)
  other arithmetic  4.68 us (4%)
    all_to_all x1, blocking collectives, scan_and_weights(): lax.all_to_all(pieces, BOTH, split_axis=0, concat_axis=0, tiled=True)  18.9 us
    pallas_call x5, Pallas kernels, expert(): pl.pallas_call(functools.partial(expert_kernel, count), out_shape=[jax.Sh...  17.3 us
    ppermute x3, waiting for transfers between devices, body(): lax.ppermute((parts[step] + going_up).astype(BF16), 'ctx', up).astype(F32)  12.2 us
    all_to_all x1, waiting for transfers between devices, scan_and_weights(): sums = lax.all_to_all(sums, BOTH, split_axis=0, concat_axis=0, tiled=True)  8.79 us
    ppermute x3, waiting for transfers between devices, body(): from_below.append(lax.ppermute(from_below[-1], 'ctx', up))  8.42 us
    unnamed x37, local copies, waits for them, and re-layouts  6.35 us
    ppermute x3, starting transfers between devices, body(): from_above.append(lax.ppermute(from_above[-1], 'ctx', down))  4.46 us
    ppermute x3, starting transfers between devices, body(): lax.ppermute((parts[-step] + going_down).astype(BF16), 'ctx', down)  3.78 us
  transfers between devices with their start and end apart: 33, of which 12 were waited for; matrix products, arithmetic and copies ran while one was open for 6% of the time, Pallas kernels for 13%

profile of v1, /device:TPU:0, one launch (start us, length us, event | category | flops | bytes accessed | tf_op | source)
XLA Modules:
  0.0 128.4 jit_solution(16389065753054756131)
XLA Ops:
  0.0 0.9 convert_reduce_fusion
  0.9 0.7 convert_divide_fusion
  1.5 0.7 select_reduce_fusion
  2.3 1.1 copy.61
  3.5 1.3 %convolution_convert_fusion.1 = bf16[8,128,128]{2,1,0:T(8,128)(2,1)S(1)} fusion(bf16[128,8,128]{0,2,1:T(8,128)(2,1)S(1)} %bitcast.102, bf16[128,1024]{1,0:T(8,128)(2,1)} %param.23), kind=kOutput, calls=%fused_computation.7 | convolution fusion | flops 33685504 | bytes 786432 | tf_op jit(solution)/shard_map/thd,the->hde/dot_general | solution.py:125
  4.9 18.9 %all_to_all.10 = bf16[32,34,128]{2,1,0:T(8,128)(2,1)} all-to-all(bf16[32,34,128]{2,1,0:T(8,128)(2,1)S(1)} %pad_maximum_fusion), channel_id=1, replica_groups=mesh['seg'=2,'ctx'=16] {'seg','ctx'}, dimensions={0} | all-to-all | bytes 557056 | tf_op jit(solution)/shard_map/all_to_all | solution.py:50
  23.7 1.0 slice.32
  24.7 0.2 fusion.2
  24.9 0.7 copy.65
  25.7 2.6 %all-to-all-start.1 = ((bf16[32,32,128]{2,1,0:T(8,128)(2,1)}), bf16[32,32,128]{2,1,0:T(8,128)(2,1)S(1)}, u32[]{:S(2)}, u32[]{:S(2)}) async-start(bf16[32,32,128]{2,1,0:T(8,128)(2,1)} %bitcast.45), calls=%async_computation.1 | async-start | bytes 524288 | tf_op jit(solution)/shard_map/all_to_all | solution.py:61
  28.3 1.4 %convolution_bitcast_fusion = f32[128,8,128]{0,2,1:T(8,128)S(1)} fusion(bf16[128,8,128]{0,2,1:T(8,128)(2,1)S(1)} %bitcast.103, pred[128,128]{1,0:T(8,128)(4,1)S(1)} %iota_compare_fusion, bf16[128,1024]{1,0:T(8,128)(2,1)} %param.22, bf16[128,1024]{1,0:T(8,128)(2,1)S(1)} %copy-done.11), kind=kOutput, calls=%fused_computation.1 | convolution fusion | flops 67371008 | bytes 1327104 | tf_op jit(solution)/shard_map/hts,she->the/dot_general | solution.py:130
  29.8 8.8 %all-to-all-done.1 = bf16[32,32,128]{2,1,0:T(8,128)(2,1)S(1)} async-done(((bf16[32,32,128]{2,1,0:T(8,128)(2,1)}), bf16[32,32,128]{2,1,0:T(8,128)(2,1)S(1)}, u32[]{:S(2)}, u32[]{:S(2)}) %all-to-all-start.1) | async-done | bytes 262176 | tf_op jit(solution)/shard_map/all_to_all | solution.py:61
  38.6 1.3 %multiply_reduce_fusion.1 = (f32[128]{0:T(128)S(1)}, f32[128,8,128]{0,2,1:T(8,128)S(1)}) fusion(f32[128,8,128]{0,2,1:T(8,128)S(1)} %convolution_bitcast_fusion, bf16[8,128,128]{2,1,0:T(8,128)(2,1)S(1)} %bitcast.106, bf16[128,1024]{1,0:T(8,128)(2,1)} %param.22), kind=kOutput, calls=%fused_computation.22 | convolution fusion | flops 33947520 | bytes 1573376 | tf_op jit(solution)/shard_map/thd,hde->the/dot_general | solution.py:131
  40.1 0.6 multiply_reduce_fusion
  40.8 1.2 collective-permute-start.4
  42.0 0.9 collective-permute-start.2
  42.9 6.5 %collective-permute-done.4.refs_2_ = bf16[128,1024]{1,0:T(8,128)(2,1)S(1)} collective-permute-done((bf16[128,1024]{1,0:T(8,128)(2,1)S(1)}, bf16[128,1024]{1,0:T(8,128)(2,1)S(1)}, u32[]{:S(2)}, u32[]{:S(2)}) %collective-permute-start.4) | collective-permute-done | bytes 262176 | tf_op jit(solution)/shard_map/ppermute | solution.py:146
  49.4 0.3 collective-permute-start.9
  49.7 1.8 %collective-permute-start.7 = (bf16[128,1024]{1,0:T(8,128)(2,1)S(1)}, bf16[128,1024]{1,0:T(8,128)(2,1)}, u32[]{:S(2)}, u32[]{:S(2)}) collective-permute-start(bf16[128,1024]{1,0:T(8,128)(2,1)S(1)} %collective-permute-done.2.refs_0_), channel_id=1, source_target_pairs={{0,2},{1,3},{4,0},{5,1},{8,4},{9,5},{12,8},{13,9},{14,12},{15,13},... | collective-permute-start | bytes 786440 | tf_op jit(solution)/shard_map/ppermute | solution.py:147
  51.5 0.6 dynamic_slice.30
  57.9 0.7 fusion.27
  59.2 0.3 collective-permute-start.14
  60.4 1.8 %collective-permute-start.12 = (bf16[128,1024]{1,0:T(8,128)(2,1)}, bf16[128,1024]{1,0:T(8,128)(2,1)S(1)}, u32[]{:S(2)}, u32[]{:S(2)}) collective-permute-start(bf16[128,1024]{1,0:T(8,128)(2,1)} %collective-permute-done.7.refs_0_), channel_id=1, source_target_pairs={{0,2},{1,3},{4,0},{5,1},{8,4},{9,5},{12,8},{13,9},{14,12},{15,13},... | collective-permute-start | bytes 786440 | tf_op jit(solution)/shard_map/ppermute | solution.py:147
  64.8 1.9 %collective-permute-done.14.refs_2_ = bf16[128,1024]{1,0:T(8,128)(2,1)S(1)} collective-permute-done((bf16[128,1024]{1,0:T(8,128)(2,1)}, bf16[128,1024]{1,0:T(8,128)(2,1)S(1)}, u32[]{:S(2)}, u32[]{:S(2)}) %collective-permute-start.14) | collective-permute-done | bytes 262176 | tf_op jit(solution)/shard_map/ppermute | solution.py:146
  66.7 0.7 slice.36
  67.3 0.3 collective-permute-start.17
  69.1 0.7 slice.37
  69.7 1.7 %collective-permute-start.18 = (bf16[64,1024]{1,0:T(8,128)(2,1)}, bf16[64,1024]{1,0:T(8,128)(2,1)}, u32[]{:S(2)}, u32[]{:S(2)}) collective-permute-start(bf16[64,1024]{1,0:T(8,128)(2,1)} %slice.37), channel_id=1, source_target_pairs={{0,2},{1,3},{4,0},{5,1},{8,4},{9,5},{12,8},{13,9},{14,12},{15,13},... | collective-permute-start | bytes 393224 | tf_op jit(solution)/shard_map/ppermute | solution.py:151
  71.5 0.9 slice.33
  72.4 0.2 collective-permute-done.17
  72.6 0.9 constant_dynamic-update-slice_fusion.1
  73.5 1.5 %collective-permute-done.18 = bf16[64,1024]{1,0:T(8,128)(2,1)} collective-permute-done((bf16[64,1024]{1,0:T(8,128)(2,1)}, bf16[64,1024]{1,0:T(8,128)(2,1)}, u32[]{:S(2)}, u32[]{:S(2)}) %collective-permute-start.18) | collective-permute-done | bytes 131104 | tf_op jit(solution)/shard_map/ppermute | solution.py:151
  75.0 0.9 constant_dynamic-update-slice_fusion.refs_0_
  76.2 0.5 collective-permute-start.13
  76.8 0.5 collective-permute-start
  77.5 0.3 collective-permute-start.10
  77.8 1.5 %copy-done.1 = bf16[1,1024,896]{2,1,0:T(8,128)(2,1)S(1)} copy-done((bf16[1,1024,896]{2,1,0:T(8,128)(2,1)S(1)}, bf16[1,1024,896]{2,1,0:T(8,128)(2,1)}, u32[]{:S(2)}) %copy-start.1) | copy-done | bytes 1835032
  79.3 1.5 %copy-done.3 = bf16[1,1024,896]{2,1,0:T(8,128)(2,1)S(1)} copy-done((bf16[1,1024,896]{2,1,0:T(8,128)(2,1)S(1)}, bf16[1,1024,896]{2,1,0:T(8,128)(2,1)}, u32[]{:S(2)}) %copy-start.3) | copy-done | bytes 1835032
  80.8 1.5 %copy-done.4 = bf16[1,896,1024]{2,1,0:T(8,128)(2,1)S(1)} copy-done((bf16[1,896,1024]{2,1,0:T(8,128)(2,1)S(1)}, bf16[1,896,1024]{2,1,0:T(8,128)(2,1)}, u32[]{:S(2)}) %copy-start.4) | copy-done | bytes 1835032
  82.3 2.3 %shard_map.203 = (bf16[128,1024]{1,0:T(8,128)(2,1)S(1)}, bf16[128,1024]{1,0:T(8,128)(2,1)S(1)}) custom-call(s32[2]{0:T(128)S(1)} %pad_add_fusion.4.sources, f32[128,16]{1,0:T(8,128)S(1)} %fusion.21.dense, bf16[1,1024,896]{2,1,0:T(8,128)(2,1)S(1)} %copy-done.1, bf16[1,1024,896]{2,1,0:T(8,128)(2,1)S(1)} %copy-done.3, bf16[1,896,1024]{2,1,0:T(8,128)(2,1)S(1)} %copy-done.4, ...), custom_call_target="tpu_custom_call" | custom-call | flops 1409286144 | tf_op jit(solution)/shard_map/pallas_call | solution.py:84
  84.7 0.3 collective-permute-start.8
  85.0 0.3 collective-permute-start.20
  85.3 4.0 %shard_map.202 = (bf16[128,1024]{1,0:T(8,128)(2,1)S(1)}, bf16[128,1024]{1,0:T(8,128)(2,1)S(1)}, bf16[128,1024]{1,0:T(8,128)(2,1)S(1)}, bf16[128,1024]{1,0:T(8,128)(2,1)S(1)}) custom-call(s32[4]{0:T(128)S(1)} %pad_add_fusion.3.sources, f32[128,16]{1,0:T(8,128)S(1)} %fusion.21.dense, bf16[1,1024,896]{2,1,0:T(8,128)(2,1)S(1)} %copy-done.2, ...), custom_call_target="tpu_custom_call" | custom-call | flops 2818572288 | tf_op jit(solution)/shard_map/pallas_call | solution.py:84
  89.3 0.3 collective-permute-start.16
  89.7 0.4 collective-permute-start.27
  90.1 0.3 collective-permute-start.21
  90.4 4.5 %shard_map.201 = (bf16[128,1024]{1,0:T(8,128)(2,1)S(1)}, bf16[128,1024]{1,0:T(8,128)(2,1)S(1)}, bf16[128,1024]{1,0:T(8,128)(2,1)S(1)}, bf16[128,1024]{1,0:T(8,128)(2,1)S(1)}) custom-call(s32[4]{0:T(128)S(1)} %pad_add_fusion.2.sources, f32[128,16]{1,0:T(8,128)S(1)} %fusion.21.dense, bf16[1,1024,896]{2,1,0:T(8,128)(2,1)S(1)} %copy-done.2, ...), custom_call_target="tpu_custom_call" | custom-call | flops 2818572288 | tf_op jit(solution)/shard_map/pallas_call | solution.py:84
  95.0 0.7 collective-permute-done.21
  95.7 1.7 %collective-permute-start.28 = (bf16[64,1024]{1,0:T(8,128)(2,1)S(1)}, bf16[64,1024]{1,0:T(8,128)(2,1)S(1)}, u32[]{:S(2)}, u32[]{:S(2)}) collective-permute-start(bf16[64,1024]{1,0:T(8,128)(2,1)S(1)} %get-tuple-element.38), channel_id=1, source_target_pairs={{0,2},{1,3},{4,0},{5,1},{8,4},{9,5},{12,8},{13,9},{14,12},{15,13},... | collective-permute-start | bytes 393224 | tf_op jit(solution)/shard_map/ppermute | solution.py:175
  97.6 3.3 %collective-permute-done.28 = bf16[64,1024]{1,0:T(8,128)(2,1)S(1)} collective-permute-done((bf16[64,1024]{1,0:T(8,128)(2,1)S(1)}, bf16[64,1024]{1,0:T(8,128)(2,1)S(1)}, u32[]{:S(2)}, u32[]{:S(2)}) %collective-permute-start.28) | collective-permute-done | bytes 131104 | tf_op jit(solution)/shard_map/ppermute | solution.py:175
  101.0 0.9 collective-permute-start.22
  101.9 1.2 collective-permute-start.29
  103.1 4.0 %shard_map.200 = (bf16[128,1024]{1,0:T(8,128)(2,1)S(1)}, bf16[128,1024]{1,0:T(8,128)(2,1)S(1)}, bf16[128,1024]{1,0:T(8,128)(2,1)S(1)}, bf16[128,1024]{1,0:T(8,128)(2,1)S(1)}) custom-call(s32[4]{0:T(128)S(1)} %pad_add_fusion.1.sources, f32[128,16]{1,0:T(8,128)S(1)} %fusion.21.dense, bf16[1,1024,896]{2,1,0:T(8,128)(2,1)S(1)} %copy-done.2, ...), custom_call_target="tpu_custom_call" | custom-call | flops 2818572288 | tf_op jit(solution)/shard_map/pallas_call | solution.py:84
  107.1 0.3 collective-permute-start.6
  107.4 2.4 %collective-permute-done.22 = bf16[128,1024]{1,0:T(8,128)(2,1)S(1)} collective-permute-done((bf16[128,1024]{1,0:T(8,128)(2,1)S(1)}, bf16[128,1024]{1,0:T(8,128)(2,1)S(1)}, u32[]{:S(2)}, u32[]{:S(2)}) %collective-permute-start.22) | collective-permute-done | bytes 262176 | tf_op jit(solution)/shard_map/ppermute | solution.py:180
  109.9 0.9 collective-permute-start.23
  110.9 1.3 collective-permute-start.30
  112.2 2.3 %shard_map.199 = (bf16[128,1024]{1,0:T(8,128)(2,1)S(1)}, bf16[128,1024]{1,0:T(8,128)(2,1)S(1)}) custom-call(s32[2]{0:T(128)S(1)} %pad_add_fusion.sources, f32[128,16]{1,0:T(8,128)S(1)} %fusion.21.dense, bf16[1,1024,896]{2,1,0:T(8,128)(2,1)S(1)} %copy-done.2, bf16[1,1024,896]{2,1,0:T(8,128)(2,1)S(1)} %copy-done.3, bf16[1,896,1024]{2,1,0:T(8,128)(2,1)S(1)} %copy-done.4, ...), custom_call_target="tpu_custom_call" | custom-call | flops 1409286144 | tf_op jit(solution)/shard_map/pallas_call | solution.py:84
  114.7 4.0 %collective-permute-done.23 = bf16[128,1024]{1,0:T(8,128)(2,1)S(1)} collective-permute-done((bf16[128,1024]{1,0:T(8,128)(2,1)S(1)}, bf16[128,1024]{1,0:T(8,128)(2,1)S(1)}, u32[]{:S(2)}, u32[]{:S(2)}) %collective-permute-start.23) | collective-permute-done | bytes 262176 | tf_op jit(solution)/shard_map/ppermute | solution.py:180
  118.8 0.9 collective-permute-start.24
  119.8 1.3 collective-permute-start.31
  121.1 5.7 %collective-permute-done.24 = bf16[128,1024]{1,0:T(8,128)(2,1)S(1)} collective-permute-done((bf16[128,1024]{1,0:T(8,128)(2,1)S(1)}, bf16[128,1024]{1,0:T(8,128)(2,1)S(1)}, u32[]{:S(2)}, u32[]{:S(2)}) %collective-permute-start.24) | collective-permute-done | bytes 262176 | tf_op jit(solution)/shard_map/ppermute | solution.py:180
  126.8 0.7 collective-permute-done.31
  127.5 0.9 add_convert_fusion
  (89 shorter events, 2.4 us)
Async XLA Ops:
  0.0 40.1 %copy-start = (bf16[1024,1024]{1,0:T(8,128)(2,1)S(1)}, bf16[1024,1024]{1,0:T(8,128)(2,1)}, u32[]{:S(2)}) copy-start(bf16[1024,1024]{1,0:T(8,128)(2,1)} %param.26) | copy-start | bytes 6291460
  3.4 24.9 %copy-start.11 = (bf16[128,1024]{1,0:T(8,128)(2,1)S(1)}, bf16[128,1024]{1,0:T(8,128)(2,1)}, u32[]{:S(2)}) copy-start(bf16[128,1024]{1,0:T(8,128)(2,1)} %param.23) | copy-start | bytes 786436
  24.9 14.9 %copy-start.14 = (f32[1024]{0:T(1024)S(1)}, f32[1024]{0:T(1024)}, u32[]{:S(2)}) copy-start(f32[1024]{0:T(1024)} %param.25) | copy-start | bytes 12292
  25.7 12.9 %all-to-all-start.1 = ((bf16[32,32,128]{2,1,0:T(8,128)(2,1)}), bf16[32,32,128]{2,1,0:T(8,128)(2,1)S(1)}, u32[]{:S(2)}, u32[]{:S(2)}) async-start(bf16[32,32,128]{2,1,0:T(8,128)(2,1)} %bitcast.45), calls=%async_computation.1 | async-start | bytes 524288 | tf_op jit(solution)/shard_map/all_to_all | solution.py:61
  29.8 10.3 %copy-start.12 = (bf16[128,1024]{1,0:T(8,128)(2,1)S(1)}, bf16[128,1024]{1,0:T(8,128)(2,1)}, u32[]{:S(2)}) copy-start(bf16[128,1024]{1,0:T(8,128)(2,1)} %param.21) | copy-start | bytes 786436
  39.9 0.9 copy-start.15
  40.1 11.4 %copy-start.16 = (s32[8]{0:T(128)S(1)}, s32[8]{0:T(128)}, u32[]{:S(2)}) copy-start(s32[8]{0:T(128)} %constant.124.clone) | copy-start | bytes 100
  40.1 17.8 %copy-start.13 = (s32[8]{0:T(128)S(1)}, s32[8]{0:T(128)}, u32[]{:S(2)}) copy-start(s32[8]{0:T(128)} %constant.125.clone) | copy-start | bytes 100
  40.7 9.0 %copy-start.9 = (f32[128,1024]{1,0:T(8,128)}, f32[128,1024]{1,0:T(8,128)S(1)}, u32[]{:S(2)}) copy-start(f32[128,1024]{1,0:T(8,128)S(1)} %get-tuple-element.50) | copy-start | bytes 1572868
  40.8 8.6 %collective-permute-start.4 = (bf16[128,1024]{1,0:T(8,128)(2,1)S(1)}, bf16[128,1024]{1,0:T(8,128)(2,1)S(1)}, u32[]{:S(2)}, u32[]{:S(2)}) collective-permute-start(bf16[128,1024]{1,0:T(8,128)(2,1)S(1)} %multiply_convert_fusion.refs_0_), channel_id=1, source_target_pairs={{0,4},{1,5},{4,8},{5,9},{8,12},{9,13},{12,14},{13,15},{14,10},{15,... | collective-permute-start | bytes 786440 | tf_op jit(solution)/shard_map/ppermute | solution.py:146
  42.0 7.7 %collective-permute-start.2 = (bf16[128,1024]{1,0:T(8,128)(2,1)S(1)}, bf16[128,1024]{1,0:T(8,128)(2,1)S(1)}, u32[]{:S(2)}, u32[]{:S(2)}) collective-permute-start(bf16[128,1024]{1,0:T(8,128)(2,1)S(1)} %multiply_convert_fusion.refs_0_), channel_id=1, source_target_pairs={{0,2},{1,3},{4,0},{5,1},{8,4},{9,5},{12,8},{13,9},{14,12},{15,13},... | collective-permute-start | bytes 786440 | tf_op jit(solution)/shard_map/ppermute | solution.py:147
  49.4 23.0 %copy-start.5 = (bf16[128,1024]{1,0:T(8,128)(2,1)}, bf16[128,1024]{1,0:T(8,128)(2,1)S(1)}, u32[]{:S(2)}) copy-start(bf16[128,1024]{1,0:T(8,128)(2,1)S(1)} %collective-permute-done.4.refs_2_) | copy-start | bytes 786436
  49.4 9.8 %collective-permute-start.9 = (bf16[128,1024]{1,0:T(8,128)(2,1)S(1)}, bf16[128,1024]{1,0:T(8,128)(2,1)}, u32[]{:S(2)}, u32[]{:S(2)}) collective-permute-start(bf16[128,1024]{1,0:T(8,128)(2,1)S(1)} %collective-permute-done.4.refs_2_), channel_id=1, source_target_pairs={{0,4},{1,5},{4,8},{5,9},{8,12},{9,13},{12,14},{13,15},{14,10},{15,... | collective-permute-start | bytes 786440 | tf_op jit(solution)/shard_map/ppermute | solution.py:146
  49.7 25.3 %copy-start.7 = (bf16[128,1024]{1,0:T(8,128)(2,1)}, bf16[128,1024]{1,0:T(8,128)(2,1)S(1)}, u32[]{:S(2)}) copy-start(bf16[128,1024]{1,0:T(8,128)(2,1)S(1)} %collective-permute-done.2.refs_0_) | copy-start | bytes 786436
  49.7 10.7 %collective-permute-start.7 = (bf16[128,1024]{1,0:T(8,128)(2,1)S(1)}, bf16[128,1024]{1,0:T(8,128)(2,1)}, u32[]{:S(2)}, u32[]{:S(2)}) collective-permute-start(bf16[128,1024]{1,0:T(8,128)(2,1)S(1)} %collective-permute-done.2.refs_0_), channel_id=1, source_target_pairs={{0,2},{1,3},{4,0},{5,1},{8,4},{9,5},{12,8},{13,9},{14,12},{15,13},... | collective-permute-start | bytes 786440 | tf_op jit(solution)/shard_map/ppermute | solution.py:147
  59.2 7.4 %collective-permute-start.14 = (bf16[128,1024]{1,0:T(8,128)(2,1)}, bf16[128,1024]{1,0:T(8,128)(2,1)S(1)}, u32[]{:S(2)}, u32[]{:S(2)}) collective-permute-start(bf16[128,1024]{1,0:T(8,128)(2,1)} %collective-permute-done.9.refs_2_), channel_id=1, source_target_pairs={{0,4},{1,5},{4,8},{5,9},{8,12},{9,13},{12,14},{13,15},{14,10},{15,... | collective-permute-start | bytes 786440 | tf_op jit(solution)/shard_map/ppermute | solution.py:146
  60.4 8.7 %collective-permute-start.12 = (bf16[128,1024]{1,0:T(8,128)(2,1)}, bf16[128,1024]{1,0:T(8,128)(2,1)S(1)}, u32[]{:S(2)}, u32[]{:S(2)}) collective-permute-start(bf16[128,1024]{1,0:T(8,128)(2,1)} %collective-permute-done.7.refs_0_), channel_id=1, source_target_pairs={{0,2},{1,3},{4,0},{5,1},{8,4},{9,5},{12,8},{13,9},{14,12},{15,13},... | collective-permute-start | bytes 786440 | tf_op jit(solution)/shard_map/ppermute | solution.py:147
  67.3 5.3 %collective-permute-start.17 = (bf16[64,1024]{1,0:T(8,128)(2,1)}, bf16[64,1024]{1,0:T(8,128)(2,1)}, u32[]{:S(2)}, u32[]{:S(2)}) collective-permute-start(bf16[64,1024]{1,0:T(8,128)(2,1)} %slice.36), channel_id=1, source_target_pairs={{0,4},{1,5},{4,8},{5,9},{8,12},{9,13},{12,14},{13,15},{14,10},{15,... | collective-permute-start | bytes 393224 | tf_op jit(solution)/shard_map/ppermute | solution.py:150
  69.7 5.3 %collective-permute-start.18 = (bf16[64,1024]{1,0:T(8,128)(2,1)}, bf16[64,1024]{1,0:T(8,128)(2,1)}, u32[]{:S(2)}, u32[]{:S(2)}) collective-permute-start(bf16[64,1024]{1,0:T(8,128)(2,1)} %slice.37), channel_id=1, source_target_pairs={{0,2},{1,3},{4,0},{5,1},{8,4},{9,5},{12,8},{13,9},{14,12},{15,13},... | collective-permute-start | bytes 393224 | tf_op jit(solution)/shard_map/ppermute | solution.py:151
  75.9 1.6 %collective-permute-start.19 = (bf16[128,1024]{1,0:T(8,128)(2,1)S(1)}, bf16[128,1024]{1,0:T(8,128)(2,1)S(1)}, u32[]{:S(2)}, u32[]{:S(2)}) collective-permute-start(bf16[128,1024]{1,0:T(8,128)(2,1)S(1)} %constant_dynamic-update-slice_fusion.refs_0_), channel_id=1, source_target_pairs={{0,1},{1,0},{2,3},{3,2},{4,5},{5,4},{6,7},{7,6},{8,9},{9,8},{10,11... | collective-permute-start | bytes 786440 | tf_op jit(solution)/shard_map/ppermute | solution.py:166
  76.2 8.5 %collective-permute-start.13 = (bf16[128,1024]{1,0:T(8,128)(2,1)S(1)}, bf16[128,1024]{1,0:T(8,128)(2,1)S(1)}, u32[]{:S(2)}, u32[]{:S(2)}) collective-permute-start(bf16[128,1024]{1,0:T(8,128)(2,1)S(1)} %collective-permute-done.12.refs_0_), channel_id=1, source_target_pairs={{0,1},{1,0},{2,3},{3,2},{4,5},{5,4},{6,7},{7,6},{8,9},{9,8},{10,11... | collective-permute-start | bytes 786440 | tf_op jit(solution)/shard_map/ppermute | solution.py:166
  76.7 8.2 %collective-permute-start.15 = (bf16[128,1024]{1,0:T(8,128)(2,1)S(1)}, bf16[128,1024]{1,0:T(8,128)(2,1)S(1)}, u32[]{:S(2)}, u32[]{:S(2)}) collective-permute-start(bf16[128,1024]{1,0:T(8,128)(2,1)S(1)} %collective-permute-done.14.refs_2_), channel_id=1, source_target_pairs={{0,1},{1,0},{2,3},{3,2},{4,5},{5,4},{6,7},{7,6},{8,9},{9,8},{10,11... | collective-permute-start | bytes 786440 | tf_op jit(solution)/shard_map/ppermute | solution.py:166
  76.8 35.4 %collective-permute-start = (bf16[128,1024]{1,0:T(8,128)(2,1)S(1)}, bf16[128,1024]{1,0:T(8,128)(2,1)S(1)}, u32[]{:S(2)}, u32[]{:S(2)}) collective-permute-start(bf16[128,1024]{1,0:T(8,128)(2,1)S(1)} %multiply_convert_fusion.refs_0_), channel_id=1, source_target_pairs={{0,1},{1,0},{2,3},{3,2},{4,5},{5,4},{6,7},{7,6},{8,9},{9,8},{10,11... | collective-permute-start | bytes 786440 | tf_op jit(solution)/shard_map/ppermute | solution.py:166
  77.3 23.7 %collective-permute-start.3 = (bf16[128,1024]{1,0:T(8,128)(2,1)}, bf16[128,1024]{1,0:T(8,128)(2,1)S(1)}, u32[]{:S(2)}, u32[]{:S(2)}) collective-permute-start(bf16[128,1024]{1,0:T(8,128)(2,1)} %copy-done.7), channel_id=1, source_target_pairs={{0,1},{1,0},{2,3},{3,2},{4,5},{5,4},{6,7},{7,6},{8,9},{9,8},{10,11... | collective-permute-start | bytes 786440 | tf_op jit(solution)/shard_map/ppermute | solution.py:166
  77.5 12.2 %collective-permute-start.10 = (bf16[128,1024]{1,0:T(8,128)(2,1)}, bf16[128,1024]{1,0:T(8,128)(2,1)S(1)}, u32[]{:S(2)}, u32[]{:S(2)}) collective-permute-start(bf16[128,1024]{1,0:T(8,128)(2,1)} %collective-permute-done.9.refs_2_), channel_id=1, source_target_pairs={{0,1},{1,0},{2,3},{3,2},{4,5},{5,4},{6,7},{7,6},{8,9},{9,8},{10,11... | collective-permute-start | bytes 786440 | tf_op jit(solution)/shard_map/ppermute | solution.py:166
  77.8 1.5 %copy-start.1 = (bf16[1,1024,896]{2,1,0:T(8,128)(2,1)S(1)}, bf16[1,1024,896]{2,1,0:T(8,128)(2,1)}, u32[]{:S(2)}) copy-start(bf16[1,1024,896]{2,1,0:T(8,128)(2,1)} %w_gate.9) | copy-start | bytes 5505028
  79.3 1.5 %copy-start.3 = (bf16[1,1024,896]{2,1,0:T(8,128)(2,1)S(1)}, bf16[1,1024,896]{2,1,0:T(8,128)(2,1)}, u32[]{:S(2)}) copy-start(bf16[1,1024,896]{2,1,0:T(8,128)(2,1)} %w_up.9) | copy-start | bytes 5505028
  80.8 1.5 %copy-start.4 = (bf16[1,896,1024]{2,1,0:T(8,128)(2,1)S(1)}, bf16[1,896,1024]{2,1,0:T(8,128)(2,1)}, u32[]{:S(2)}) copy-start(bf16[1,896,1024]{2,1,0:T(8,128)(2,1)} %w_down.9) | copy-start | bytes 5505028
  82.3 2.9 %copy-start.2 = (bf16[1,1024,896]{2,1,0:T(8,128)(2,1)S(1)}, bf16[1,1024,896]{2,1,0:T(8,128)(2,1)}, u32[]{:S(2)}) copy-start(bf16[1,1024,896]{2,1,0:T(8,128)(2,1)} %w_gate.9) | copy-start | bytes 5505028
  84.7 5.4 %collective-permute-start.8 = (bf16[128,1024]{1,0:T(8,128)(2,1)}, bf16[128,1024]{1,0:T(8,128)(2,1)S(1)}, u32[]{:S(2)}, u32[]{:S(2)}) collective-permute-start(bf16[128,1024]{1,0:T(8,128)(2,1)} %collective-permute-done.7.refs_0_), channel_id=1, source_target_pairs={{0,1},{1,0},{2,3},{3,2},{4,5},{5,4},{6,7},{7,6},{8,9},{9,8},{10,11... | collective-permute-start | bytes 786440 | tf_op jit(solution)/shard_map/ppermute | solution.py:166
  85.0 4.3 %collective-permute-start.20 = (bf16[128,1024]{1,0:T(8,128)(2,1)S(1)}, bf16[128,1024]{1,0:T(8,128)(2,1)S(1)}, u32[]{:S(2)}, u32[]{:S(2)}) collective-permute-start(bf16[128,1024]{1,0:T(8,128)(2,1)S(1)} %get-tuple-element.30), channel_id=1, source_target_pairs={{0,1},{1,0},{2,3},{3,2},{4,5},{5,4},{6,7},{7,6},{8,9},{9,8},{10,11... | collective-permute-start | bytes 786440 | tf_op jit(solution)/shard_map/ppermute | solution.py:170
  89.3 5.6 %collective-permute-start.16 = (bf16[128,1024]{1,0:T(8,128)(2,1)S(1)}, bf16[128,1024]{1,0:T(8,128)(2,1)S(1)}, u32[]{:S(2)}, u32[]{:S(2)}) collective-permute-start(bf16[128,1024]{1,0:T(8,128)(2,1)S(1)} %get-tuple-element.28), channel_id=1, source_target_pairs={{0,1},{1,0},{2,3},{3,2},{4,5},{5,4},{6,7},{7,6},{8,9},{9,8},{10,11... | collective-permute-start | bytes 786440 | tf_op jit(solution)/shard_map/ppermute | solution.py:170
  89.7 7.8 %collective-permute-start.27 = (bf16[128,1024]{1,0:T(8,128)(2,1)S(1)}, bf16[128,1024]{1,0:T(8,128)(2,1)S(1)}, u32[]{:S(2)}, u32[]{:S(2)}) collective-permute-start(bf16[128,1024]{1,0:T(8,128)(2,1)S(1)} %get-tuple-element.36), channel_id=1, source_target_pairs={{0,1},{1,0},{2,3},{3,2},{4,5},{5,4},{6,7},{7,6},{8,9},{9,8},{10,11... | collective-permute-start | bytes 786440 | tf_op jit(solution)/shard_map/ppermute | solution.py:170
  90.1 4.8 %copy-start.6 = (bf16[128,1024]{1,0:T(8,128)(2,1)S(1)}, bf16[128,1024]{1,0:T(8,128)(2,1)}, u32[]{:S(2)}) copy-start(bf16[128,1024]{1,0:T(8,128)(2,1)} %copy-done.5) | copy-start | bytes 786436
  90.1 13.0 %copy-start.8 = (bf16[128,1024]{1,0:T(8,128)(2,1)S(1)}, bf16[128,1024]{1,0:T(8,128)(2,1)}, u32[]{:S(2)}) copy-start(bf16[128,1024]{1,0:T(8,128)(2,1)} %copy-done.7) | copy-start | bytes 786436
  90.1 5.6 %collective-permute-start.21 = (bf16[64,1024]{1,0:T(8,128)(2,1)S(1)}, bf16[64,1024]{1,0:T(8,128)(2,1)S(1)}, u32[]{:S(2)}, u32[]{:S(2)}) collective-permute-start(bf16[64,1024]{1,0:T(8,128)(2,1)S(1)} %get-tuple-element.37), channel_id=1, source_target_pairs={{0,4},{1,5},{4,8},{5,9},{8,12},{9,13},{12,14},{13,15},{14,10},{15,... | collective-permute-start | bytes 393224 | tf_op jit(solution)/shard_map/ppermute | solution.py:174
  94.9 6.9 %collective-permute-start.5 = (bf16[128,1024]{1,0:T(8,128)(2,1)S(1)}, bf16[128,1024]{1,0:T(8,128)(2,1)S(1)}, u32[]{:S(2)}, u32[]{:S(2)}) collective-permute-start(bf16[128,1024]{1,0:T(8,128)(2,1)S(1)} %copy-done.6), channel_id=1, source_target_pairs={{0,1},{1,0},{2,3},{3,2},{4,5},{5,4},{6,7},{7,6},{8,9},{9,8},{10,11... | collective-permute-start | bytes 786440 | tf_op jit(solution)/shard_map/ppermute | solution.py:166
  95.7 5.2 %collective-permute-start.28 = (bf16[64,1024]{1,0:T(8,128)(2,1)S(1)}, bf16[64,1024]{1,0:T(8,128)(2,1)S(1)}, u32[]{:S(2)}, u32[]{:S(2)}) collective-permute-start(bf16[64,1024]{1,0:T(8,128)(2,1)S(1)} %get-tuple-element.38), channel_id=1, source_target_pairs={{0,2},{1,3},{4,0},{5,1},{8,4},{9,5},{12,8},{13,9},{14,12},{15,13},... | collective-permute-start | bytes 393224 | tf_op jit(solution)/shard_map/ppermute | solution.py:175
  97.5 9.6 %collective-permute-start.11 = (bf16[128,1024]{1,0:T(8,128)(2,1)S(1)}, bf16[128,1024]{1,0:T(8,128)(2,1)S(1)}, u32[]{:S(2)}, u32[]{:S(2)}) collective-permute-start(bf16[128,1024]{1,0:T(8,128)(2,1)S(1)} %get-tuple-element.26), channel_id=1, source_target_pairs={{0,1},{1,0},{2,3},{3,2},{4,5},{5,4},{6,7},{7,6},{8,9},{9,8},{10,11... | collective-permute-start | bytes 786440 | tf_op jit(solution)/shard_map/ppermute | solution.py:170
  100.9 9.0 %collective-permute-start.26 = (bf16[128,1024]{1,0:T(8,128)(2,1)S(1)}, bf16[128,1024]{1,0:T(8,128)(2,1)S(1)}, u32[]{:S(2)}, u32[]{:S(2)}) collective-permute-start(bf16[128,1024]{1,0:T(8,128)(2,1)S(1)} %get-tuple-element.34), channel_id=1, source_target_pairs={{0,1},{1,0},{2,3},{3,2},{4,5},{5,4},{6,7},{7,6},{8,9},{9,8},{10,11... | collective-permute-start | bytes 786440 | tf_op jit(solution)/shard_map/ppermute | solution.py:170
  101.0 8.8 %collective-permute-start.22 = (bf16[128,1024]{1,0:T(8,128)(2,1)S(1)}, bf16[128,1024]{1,0:T(8,128)(2,1)S(1)}, u32[]{:S(2)}, u32[]{:S(2)}) collective-permute-start(bf16[128,1024]{1,0:T(8,128)(2,1)S(1)} %add_convert_fusion.6), channel_id=1, source_target_pairs={{0,4},{1,5},{4,8},{5,9},{8,12},{9,13},{12,14},{13,15},{14,10},{15,... | collective-permute-start | bytes 786440 | tf_op jit(solution)/shard_map/ppermute | solution.py:180
  101.9 8.9 %collective-permute-start.29 = (bf16[128,1024]{1,0:T(8,128)(2,1)S(1)}, bf16[128,1024]{1,0:T(8,128)(2,1)S(1)}, u32[]{:S(2)}, u32[]{:S(2)}) collective-permute-start(bf16[128,1024]{1,0:T(8,128)(2,1)S(1)} %add_convert_fusion.3), channel_id=1, source_target_pairs={{0,2},{1,3},{4,0},{5,1},{8,4},{9,5},{12,8},{13,9},{14,12},{15,13},... | collective-permute-start | bytes 786440 | tf_op jit(solution)/shard_map/ppermute | solution.py:181
  107.1 7.5 %collective-permute-start.6 = (bf16[128,1024]{1,0:T(8,128)(2,1)S(1)}, bf16[128,1024]{1,0:T(8,128)(2,1)S(1)}, u32[]{:S(2)}, u32[]{:S(2)}) collective-permute-start(bf16[128,1024]{1,0:T(8,128)(2,1)S(1)} %get-tuple-element.24), channel_id=1, source_target_pairs={{0,1},{1,0},{2,3},{3,2},{4,5},{5,4},{6,7},{7,6},{8,9},{9,8},{10,11... | collective-permute-start | bytes 786440 | tf_op jit(solution)/shard_map/ppermute | solution.py:170
  109.8 9.9 %collective-permute-start.25 = (bf16[128,1024]{1,0:T(8,128)(2,1)S(1)}, bf16[128,1024]{1,0:T(8,128)(2,1)S(1)}, u32[]{:S(2)}, u32[]{:S(2)}) collective-permute-start(bf16[128,1024]{1,0:T(8,128)(2,1)S(1)} %get-tuple-element.32), channel_id=1, source_target_pairs={{0,1},{1,0},{2,3},{3,2},{4,5},{5,4},{6,7},{7,6},{8,9},{9,8},{10,11... | collective-permute-start | bytes 786440 | tf_op jit(solution)/shard_map/ppermute | solution.py:170
  109.9 8.8 %collective-permute-start.23 = (bf16[128,1024]{1,0:T(8,128)(2,1)S(1)}, bf16[128,1024]{1,0:T(8,128)(2,1)S(1)}, u32[]{:S(2)}, u32[]{:S(2)}) collective-permute-start(bf16[128,1024]{1,0:T(8,128)(2,1)S(1)} %add_convert_fusion.5), channel_id=1, source_target_pairs={{0,4},{1,5},{4,8},{5,9},{8,12},{9,13},{12,14},{13,15},{14,10},{15,... | collective-permute-start | bytes 786440 | tf_op jit(solution)/shard_map/ppermute | solution.py:180
  110.9 8.8 %collective-permute-start.30 = (bf16[128,1024]{1,0:T(8,128)(2,1)S(1)}, bf16[128,1024]{1,0:T(8,128)(2,1)S(1)}, u32[]{:S(2)}, u32[]{:S(2)}) collective-permute-start(bf16[128,1024]{1,0:T(8,128)(2,1)S(1)} %add_convert_fusion.2), channel_id=1, source_target_pairs={{0,2},{1,3},{4,0},{5,1},{8,4},{9,5},{12,8},{13,9},{14,12},{15,13},... | collective-permute-start | bytes 786440 | tf_op jit(solution)/shard_map/ppermute | solution.py:181
  114.6 13.0 %copy-start.10 = (f32[128,1024]{1,0:T(8,128)S(1)}, f32[128,1024]{1,0:T(8,128)}, u32[]{:S(2)}) copy-start(f32[128,1024]{1,0:T(8,128)} %copy-done.9) | copy-start | bytes 1572868
  114.6 6.5 %collective-permute-start.1 = (bf16[128,1024]{1,0:T(8,128)(2,1)S(1)}, bf16[128,1024]{1,0:T(8,128)(2,1)S(1)}, u32[]{:S(2)}, u32[]{:S(2)}) collective-permute-start(bf16[128,1024]{1,0:T(8,128)(2,1)S(1)} %get-tuple-element.22), channel_id=1, source_target_pairs={{0,1},{1,0},{2,3},{3,2},{4,5},{5,4},{6,7},{7,6},{8,9},{9,8},{10,11... | collective-permute-start | bytes 786440 | tf_op jit(solution)/shard_map/ppermute | solution.py:170
  118.8 8.0 %collective-permute-start.24 = (bf16[128,1024]{1,0:T(8,128)(2,1)S(1)}, bf16[128,1024]{1,0:T(8,128)(2,1)S(1)}, u32[]{:S(2)}, u32[]{:S(2)}) collective-permute-start(bf16[128,1024]{1,0:T(8,128)(2,1)S(1)} %add_convert_fusion.4), channel_id=1, source_target_pairs={{0,4},{1,5},{4,8},{5,9},{8,12},{9,13},{12,14},{13,15},{14,10},{15,... | collective-permute-start | bytes 786440 | tf_op jit(solution)/shard_map/ppermute | solution.py:180
  119.8 7.7 %collective-permute-start.31 = (bf16[128,1024]{1,0:T(8,128)(2,1)S(1)}, bf16[128,1024]{1,0:T(8,128)(2,1)S(1)}, u32[]{:S(2)}, u32[]{:S(2)}) collective-permute-start(bf16[128,1024]{1,0:T(8,128)(2,1)S(1)} %add_convert_fusion.1), channel_id=1, source_target_pairs={{0,2},{1,3},{4,0},{5,1},{8,4},{9,5},{12,8},{13,9},{14,12},{15,13},... | collective-permute-start | bytes 786440 | tf_op jit(solution)/shard_map/ppermute | solution.py:181

commit v2 on v1

v2 whole, which is shorter than its diff:
```python
import functools

import jax
import jax.numpy as jnp
from jax import lax
from jax.experimental import pallas as pl
from jax.experimental.pallas import tpu as pltpu
from jax.sharding import PartitionSpec as P

HEADS = 8
HEAD = 128
HALVES = 2
BOTH = ("seg", "ctx")
F32 = jnp.float32
BF16 = jnp.bfloat16
VMEM = pl.BlockSpec(memory_space=pltpu.VMEM)
HBM = pl.BlockSpec(memory_space=pltpu.HBM)
LIMIT = 16 * 1024 * 1024


def call(kernel, out_shape, in_specs, flops, *operands):
    many = isinstance(out_shape, list)
    return pl.pallas_call(
        kernel,
        out_shape=out_shape,
        in_specs=in_specs,
        out_specs=[VMEM] * len(out_shape) if many else VMEM,
        compiler_params=pltpu.CompilerParams(vmem_limit_bytes=LIMIT),
        cost_estimate=pl.CostEstimate(flops=flops, bytes_accessed=0, transcendentals=0),
    )(*operands)


def in_hbm(array):
    return pltpu.with_memory_space_constraint(array, pltpu.HBM)


def copies_of(sources, targets, sems):
    copies = [
        pltpu.make_async_copy(source, target, sems.at[i])
        for i, (source, target) in enumerate(zip(sources, targets))
    ]
    for copy in copies:
        copy.start()
    return copies


def chip_order(chips):
    return list(range(0, chips, 2)) + list(range(1, chips, 2))[::-1]


def ring_perm(chips):
    order = chip_order(chips)
    pairs = []
    for place, chip in enumerate(order):
        pairs.append((chip * 2, order[(place + 1) % chips] * 2))
        pairs.append((chip * 2 + 1, order[(place - 1) % chips] * 2 + 1))
    return pairs


def core_perm(chips):
    return [(dev, dev ^ 1) for dev in range(2 * chips)]


def state_kernel(k_hbm, v_hbm, out_ref, k_ref, v_ref, sems):
    for copy in copies_of([k_hbm, v_hbm], [k_ref, v_ref], sems):
        copy.wait()
    for head in range(HEADS):
        cols = pl.ds(head * HEAD, HEAD)
        state = lax.dot_general(
            k_ref[:, cols], v_ref[:, cols], (((0,), (0,)), ((), ())), preferred_element_type=F32
        )
        out_ref[cols, :] = state.astype(BF16)


def inside_kernel(count, *refs):
    q_ref, k_ref, v_ref = refs[count + 1 : count + 4]
    out_ref, sems = refs[2 * count + 1], refs[-1]
    copies = copies_of(refs[:count], refs[count + 1 : 2 * count + 1], sems)
    for copy in copies[:3]:
        copy.wait()
    ntok = q_ref.shape[0]
    causal = lax.broadcasted_iota(jnp.int32, (ntok, ntok), 0) >= lax.broadcasted_iota(
        jnp.int32, (ntok, ntok), 1
    )
    for head in range(HEADS):
        cols = pl.ds(head * HEAD, HEAD)
        scores = lax.dot_general(
            q_ref[:, cols], k_ref[:, cols], (((1,), (1,)), ((), ())), preferred_element_type=F32
        )
        scores = jnp.where(causal, scores, 0.0).astype(BF16)
        out_ref[:, cols] = jnp.dot(scores, v_ref[:, cols], preferred_element_type=F32)
    for copy in copies[3:]:
        copy.wait()


def attend_inside(arrays, after):
    count = len(arrays)
    outs = [pltpu.VMEM(a.shape, a.dtype) for a in arrays]
    outs.append(pltpu.VMEM(arrays[0].shape, F32))
    return pl.pallas_call(
        functools.partial(inside_kernel, count),
        out_shape=outs,
        in_specs=[HBM] * count + [pl.BlockSpec(memory_space=pl.ANY)],
        out_specs=[VMEM] * (count + 1),
        scratch_shapes=[pltpu.SemaphoreType.DMA((count,))],
        compiler_params=pltpu.CompilerParams(vmem_limit_bytes=LIMIT),
    )(*[in_hbm(a) for a in arrays], after)


def prefix_kernel(pieces_ref, extra_ref, out_ref):
    devices, share, cols = pieces_ref.shape
    owners = extra_ref.shape[0]
    total = jnp.zeros((share, cols), F32)
    for dev in range(devices):
        rows = jnp.concatenate([total, extra_ref[dev % owners]])
        out_ref[dev] = rows.astype(BF16)
        total += pieces_ref[dev].astype(F32)


def scan_states(states, dense):
    rows, cols = states.shape
    ntok, owners = dense.shape
    devices = lax.axis_size(BOTH)
    share = rows // devices
    top = dense.astype(BF16).astype(F32)
    extra = jnp.concatenate([top, dense - top]).T.reshape(owners, 2 * ntok // cols, cols)
    used = extra.shape[1]
    extra = jnp.pad(extra, ((0, 0), (0, -used % 8), (0, 0)))
    pieces = states.reshape(devices, share, cols)
    pieces = lax.all_to_all(pieces, BOTH, split_axis=0, concat_axis=0, tiled=True)
    whole_tiles = share % 16 == 0
    if whole_tiles:
        out = jax.ShapeDtypeStruct((devices, share + extra.shape[1], cols), BF16)
        sums = call(prefix_kernel, out, [VMEM] * 2, 0, pieces, extra)
    else:
        earlier = jnp.arange(devices)[:, None] > jnp.arange(devices)[None, :]
        sums = jnp.dot(
            earlier.astype(BF16),
            pieces.reshape(devices, share * cols),
            preferred_element_type=F32,
        ).reshape(devices, share, cols)
        extra_all = jnp.concatenate([extra] * (devices // owners))
        sums = jnp.concatenate([sums, extra_all], axis=1).astype(BF16)
    sums = lax.all_to_all(sums, BOTH, split_axis=0, concat_axis=0, tiled=True)
    split = lax.dynamic_slice_in_dim(
        sums[:, share : share + used], lax.axis_index("seg") * owners, owners
    )
    split = split.reshape(owners, 2, ntok).astype(F32)
    mine = (split[:, 0] + split[:, 1]).T
    if not whole_tiles:
        sums = sums[:, :share].reshape(rows // HEAD, HEAD, cols)
        share = HEAD
    return sums, share, mine


def rms(rows, gain):
    mean_sq = jnp.mean(rows * rows, axis=1, keepdims=True)
    return rows * lax.rsqrt(mean_sq + 1e-06) * gain


def route_kernel(
    share, q_ref, sums_ref, inside_ref, hidden_ref, gain_ref, proj_ref, moe_gain_ref, *outs
):
    ntok, width = q_ref.shape
    slabs = HEAD // share
    attended = []
    for head in range(HEADS):
        cols = pl.ds(head * HEAD, HEAD)
        earlier = jnp.concatenate(
            [sums_ref[head * slabs + i, pl.ds(0, share), :] for i in range(slabs)]
        )
        carried = jnp.dot(q_ref[:, cols], earlier, preferred_element_type=F32)
        attended.append(carried + inside_ref[:, cols])
    attended = jnp.concatenate(attended, axis=1)
    normed = rms(attended, gain_ref[...]).astype(BF16)
    mixed = hidden_ref[...].astype(F32) + jnp.dot(
        normed, proj_ref[...], preferred_element_type=F32
    )
    outs[0][...] = mixed
    routed = rms(mixed, moe_gain_ref[...]).astype(BF16)
    cut = ntok // HALVES
    for half in range(HALVES):
        outs[1 + half][...] = routed[half * cut : (half + 1) * cut]


def expert_kernel(
    chips, step, first, pair, dense, w_gate, w_up, w_down, here_ref, there_ref, *outs
):
    copies = []
    if pair:
        outs[4][...] = outs[0][...].astype(F32) + outs[1][...].astype(F32)
        outs = outs[2:4]
    elif len(outs) > 2:
        staged = outs[2:5]
        copies = copies_of([w_gate, w_up, w_down], staged, outs[5])
        w_gate, w_up, w_down = staged
    me = lax.axis_index("ctx")
    core, chip = me % 2, me // 2
    place = jnp.where(chip % 2 == 0, chip // 2, chips - 1 - chip // 2)
    way = 1 - 2 * core

    def device_at(offset, plane):
        spot = (place + offset + chips) % chips
        return jnp.where(2 * spot < chips, 2 * spot, 2 * (chips - spot) - 1) * 2 + plane

    planes = [core] if step in (0, chips // 2) else [core, 1 - core]
    sources = [device_at(-way * step, plane) for plane in planes]
    sources += [device_at(way * step, 1 - plane) for plane in planes]
    rows = jnp.concatenate([here_ref[...], there_ref[...]])
    count = here_ref.shape[0]
    for copy in copies[:2]:
        copy.wait()
    gate = jnp.dot(rows, w_gate[0], preferred_element_type=F32)
    upper = jnp.dot(rows, w_up[0], preferred_element_type=F32)
    inner = (gate / (1.0 + jnp.exp(-gate)) * upper).astype(BF16)
    for copy in copies[2:]:
        copy.wait()
    result = jnp.dot(inner, w_down[0], preferred_element_type=F32)
    block = len(sources)
    cut = 2 * count // block
    table = dense[pl.ds(first, cut), :]
    lane = lax.broadcasted_iota(jnp.int32, table.shape, 1)
    scales = [
        jnp.sum(jnp.where(lane == source, table, 0.0), axis=1, keepdims=True) for source in sources
    ]
    result = (result * jnp.concatenate(scales)).astype(BF16)
    outs[0][...] = result[:count]
    outs[1][...] = result[count:]


def expert(here, there, chips, step, first, dense, weights, staging, pair):
    outs = [jax.ShapeDtypeStruct(here.shape, BF16)] * 2
    specs, scratch = [VMEM] * 3, []
    if staging:
        outs += [pltpu.VMEM(w.shape, w.dtype) for w in weights]
        specs, scratch = [HBM] * 3, [pltpu.SemaphoreType.DMA((3,))]
        weights = [in_hbm(w) for w in weights]
    if pair:
        outs.append(jax.ShapeDtypeStruct(pair[0].shape, F32))
    return pl.pallas_call(
        functools.partial(expert_kernel, chips, step, first, len(pair)),
        out_shape=outs,
        in_specs=[VMEM] + specs + [VMEM] * (2 + len(pair)),
        out_specs=[VMEM] * len(outs),
        scratch_shapes=scratch,
        compiler_params=pltpu.CompilerParams(vmem_limit_bytes=LIMIT),
        cost_estimate=pl.CostEstimate(
            flops=12 * here.size * weights[0].shape[2], bytes_accessed=0, transcendentals=0
        ),
    )(dense, *weights, here, there, *pair)


def body(
    hidden_in,
    queries,
    key_rows,
    values,
    norm_gain,
    out_proj,
    moe_gain,
    w_gate,
    w_up,
    w_down,
    expert_ids,
    route_scale,
):
    ntok, width = queries.shape
    owners = lax.axis_size("ctx")
    chips = owners // 2
    out = jax.ShapeDtypeStruct((HEADS * HEAD, HEAD), BF16)
    states = pl.pallas_call(
        state_kernel,
        out_shape=out,
        in_specs=[pl.BlockSpec(memory_space=pltpu.HBM)] * 2,
        out_specs=VMEM,
        scratch_shapes=[pltpu.VMEM((ntok, width), BF16)] * 2 + [pltpu.SemaphoreType.DMA((2,))],
        compiler_params=pltpu.CompilerParams(vmem_limit_bytes=LIMIT),
    )(in_hbm(key_rows), in_hbm(values))
    scales = route_scale.astype(F32)
    weight = scales / jnp.sum(scales, axis=1, keepdims=True)
    grid = jnp.arange(owners, dtype=jnp.int32)
    dense = jnp.sum(
        jnp.where(expert_ids[:, :, None] == grid[None, None, :], weight[:, :, None], 0.0), axis=1
    )
    sums, share, dense = scan_states(states, dense)

    out = jax.ShapeDtypeStruct((ntok, width), F32)
    arrays = [queries, key_rows, values, hidden_in, norm_gain[None, :], out_proj, moe_gain[None, :]]
    queries, _, _, hidden_in, norm_gain, out_proj, moe_gain, inside = attend_inside(arrays, states)
    cut = ntok // HALVES
    outs = [out] + [jax.ShapeDtypeStruct((cut, width), BF16)] * HALVES
    mixed, *routed = call(
        functools.partial(route_kernel, share),
        outs,
        [VMEM] * 7,
        2 * ntok * width * (HEAD + width),
        queries,
        sums,
        inside,
        hidden_in,
        norm_gain,
        out_proj,
        moe_gain,
    )

    far = chips // 2
    ring, swap = ring_perm(chips), core_perm(chips)

    def send(rows):
        return lax.ppermute(rows, "ctx", ring)

    def cross(rows):
        return lax.ppermute(rows, "ctx", swap)

    weights = [w_gate, w_up, w_down]
    kept, partner, here, there, summed, done = {}, {}, {}, {}, {}, {}

    def work(half, step):
        nonlocal weights
        pair = [] if step < 2 else [kept[half, step - 1], partner[half, step - 1]]
        arrived, kept[half, step], *more = expert(
            here[half, step],
            there[half, step],
            chips,
            step,
            half * cut,
            dense,
            weights,
            half == step == 0,
            pair,
        )
        if half == step == 0:
            weights = more
        if pair:
            summed[half, step - 1] = more[0]
        done[half, step] = kept[half, step]
        partner[half, step] = arrived if step == 0 else cross(arrived)

    for half in range(HALVES):
        here[half, 0], there[half, 0] = routed[half], cross(routed[half])
        chunk = jnp.concatenate([here[half, 0], there[half, 0]])
        here[half, 1] = send(chunk)
    for half in range(HALVES):
        work(half, 0)
    for step in range(1, far + 1):
        for half in range(HALVES):
            before = done[max(half, 2 - step), step - 1]
            chunk = lax.optimization_barrier((here[half, step], before))[0]
            there[half, step] = cross(chunk)
            if step < far:
                here[half, step + 1] = send(chunk if step + 1 < far else chunk[:cut])
            work(half, step)

    rows = []
    for half in range(HALVES):
        moving = None
        for step in range(far, 0, -1):
            if step < far:
                total = summed[half, step]
            else:
                total = kept[half, step].astype(F32) + partner[half, step].astype(F32)
            if moving is not None:
                if moving.shape[0] < total.shape[0]:
                    moving = jnp.concatenate([moving, jnp.zeros_like(moving)])
                total = total + moving.astype(F32)
            moving = send(total.astype(BF16))
        if moving.shape[0] < 2 * cut:
            moving = jnp.concatenate([moving, jnp.zeros_like(moving)])
        moving = moving.astype(F32)
        home = cross((moving[:cut] + kept[half, 0].astype(F32)).astype(BF16))
        rows.append(
            mixed[half * cut : (half + 1) * cut]
            + (moving[cut:] + partner[half, 0].astype(F32) + home.astype(F32))
        )
    return jnp.concatenate(rows).astype(BF16)


def solution(mesh):
    rows = P(BOTH, None)
    expert_spec = P("ctx", None, None)
    return jax.shard_map(
        body,
        mesh=mesh,
        in_specs=(rows,) * 4 + (P(),) * 3 + (expert_spec,) * 3 + (rows,) * 2,
        out_specs=rows,
        check_vma=False,
    )
```

time: 129 us -> 104 us (0.81)
  blocking collectives: 18.9 us -> 0 us
  between operations: 11.4 us -> 0.41 us
  local copies, waits for them, and re-layouts: 12.9 us -> 3.68 us
  Pallas kernels: 17.3 us -> 24.6 us
  waiting for transfers between devices: 36 us -> 42.7 us
  starting transfers between devices: 22.5 us -> 28.5 us
  matrix products: 4.85 us -> 0 us
    all_to_all x1 -> x0, blocking collectives: 18.9 us -> none  [scan_and_weights(): lax.all_to_all(pieces, BOTH, split_axis=0, concat_axis=0, tiled=True)]
    pallas_call x5 -> x14, Pallas kernels: 17.3 us -> 24.6 us  [the longest x10 17.6 us: expert(): pl.pallas_call(functools.partial(expert_kernel, chips, step, first, len(p...]
    all_to_all x1 -> x2, starting transfers between devices: 2.59 us -> 9.89 us  [the longest x1 7.3 us: scan_states(): lax.all_to_all(pieces, BOTH, split_axis=0, concat_axis=0, tiled=True)]
    all_to_all x1 -> x2, waiting for transfers between devices: 8.79 us -> 15 us  [the longest x1 8.12 us: scan_states(): lax.all_to_all(pieces, BOTH, split_axis=0, concat_axis=0, tiled=True)]
    dot_general x5 -> x0, matrix products: 4.85 us -> none  [the longest x1 1.44 us: body(): jnp.einsum('hts,she->the', scores, v_loc, preferred_element_type=F32)]
    slice x5 -> x3, local copies, waits for them, and re-layouts: 3.16 us -> 0.03 us  [the longest x2 0.02 us: body(): here[half, step + 1] = send(chunk if step + 1 < far else chunk[:cut])]
    unnamed x37 -> x9, local copies, waits for them, and re-layouts: 6.35 us -> 3.61 us
    convert_element_type x11 -> x14, other arithmetic: 1.96 us -> 0.52 us  [the longest x8 0.37 us: body(): moving = send(total.astype(BF16))]
  transfers between devices with their start and end apart: 33 -> 38, of which waited for: 12 -> 19; matrix products, arithmetic and copies ran while one was open for 6% -> 3% of each run, Pallas kernels for 13% -> 20%
where the time goes in v2:
time: 104 us; the launch traced here: 103 us
  waiting for transfers between devices  42.7 us (41%)
  starting transfers between devices  28.5 us (27%)
  Pallas kernels  24.6 us (24%)
  local copies, waits for them, and re-layouts  3.68 us (4%)
  other arithmetic  3.52 us (3%)
    ppermute x16, waiting for transfers between devices, send(): return lax.ppermute(rows, 'ctx', ring)  25.6 us
    pallas_call x10, Pallas kernels, expert(): pl.pallas_call(functools.partial(expert_kernel, chips, step, first, len(p...  17.6 us
    ppermute x16, starting transfers between devices, send(): return lax.ppermute(rows, 'ctx', ring)  14.1 us
    all_to_all x1, waiting for transfers between devices, scan_states(): lax.all_to_all(pieces, BOTH, split_axis=0, concat_axis=0, tiled=True)  8.12 us
    all_to_all x1, starting transfers between devices, scan_states(): lax.all_to_all(pieces, BOTH, split_axis=0, concat_axis=0, tiled=True)  7.3 us
    all_to_all x1, waiting for transfers between devices, scan_states(): sums = lax.all_to_all(sums, BOTH, split_axis=0, concat_axis=0, tiled=True)  6.85 us
    ppermute x20, starting transfers between devices, cross(): return lax.ppermute(rows, 'ctx', swap)  4.59 us
    unnamed x9, local copies, waits for them, and re-layouts  3.61 us
  transfers between devices with their start and end apart: 38, of which 19 were waited for; matrix products, arithmetic and copies ran while one was open for 3% of the time, Pallas kernels for 20%

profile of v2, /device:TPU:0, one launch (start us, length us, event | category | flops | bytes accessed | tf_op | source)
XLA Modules:
  0.0 103.4 jit_solution(987545589980658086)
XLA Ops:
  0.0 2.0 %shard_map.118.refs_7_ = bf16[1024,128]{1,0:T(8,128)(2,1)} custom-call(bf16[128,1024]{1,0:T(8,128)(2,1)} %refs_1_.1, bf16[128,1024]{1,0:T(8,128)(2,1)} %refs_2_.1), custom_call_target="tpu_custom_call" | custom-call | tf_op jit(solution)/shard_map/pallas_call | solution.py:271
  2.0 7.3 %all-to-all-start = ((bf16[32,32,128]{2,1,0:T(8,128)(2,1)}), bf16[32,32,128]{2,1,0:T(8,128)(2,1)S(1)}, u32[]{:S(2)}, u32[]{:S(2)}) async-start(bf16[32,32,128]{2,1,0:T(8,128)(2,1)} %bitcast.2), calls=%async_computation | async-start | bytes 524288 | tf_op jit(solution)/shard_map/all_to_all | solution.py:130
  9.3 0.7 convert_reduce_fusion
  10.0 0.7 convert_divide_fusion
  10.7 0.7 select_reduce_fusion
  11.5 8.1 %all-to-all-done.pieces_ref = bf16[32,32,128]{2,1,0:T(8,128)(2,1)S(1)} async-done(((bf16[32,32,128]{2,1,0:T(8,128)(2,1)}), bf16[32,32,128]{2,1,0:T(8,128)(2,1)S(1)}, u32[]{:S(2)}, u32[]{:S(2)}) %all-to-all-start) | async-done | bytes 262176 | tf_op jit(solution)/shard_map/all_to_all | solution.py:130
  19.6 0.8 shard_map.120
  20.4 2.6 %all-to-all-start.1 = ((bf16[32,40,128]{2,1,0:T(8,128)(2,1)}), bf16[32,40,128]{2,1,0:T(8,128)(2,1)S(1)}, u32[]{:S(2)}, u32[]{:S(2)}) async-start(bf16[32,40,128]{2,1,0:T(8,128)(2,1)} %shard_map.120), calls=%async_computation.1 | async-start | bytes 655360 | tf_op jit(solution)/shard_map/all_to_all | solution.py:144
  23.0 3.3 %shard_map.119 = (bf16[128,1024]{1,0:T(8,128)(2,1)S(1)}, bf16[128,1024]{1,0:T(8,128)(2,1)}, bf16[128,1024]{1,0:T(8,128)(2,1)}, bf16[128,1024]{1,0:T(8,128)(2,1)S...) custom-call(bf16[128,1024]{1,0:T(8,128)(2,1)} %refs_0_.1, ...), custom_call_target="tpu_custom_call" | custom-call | tf_op jit(solution)/shard_map/pallas_call | solution.py:100
  26.3 0.8 copy-done
  27.1 0.7 copy-done.2
  27.8 6.8 %all-to-all-done.1.sums_ref = bf16[32,40,128]{2,1,0:T(8,128)(2,1)S(1)} async-done(((bf16[32,40,128]{2,1,0:T(8,128)(2,1)}), bf16[32,40,128]{2,1,0:T(8,128)(2,1)S(1)}, u32[]{:S(2)}, u32[]{:S(2)}) %all-to-all-start.1) | async-done | bytes 327712 | tf_op jit(solution)/shard_map/all_to_all | solution.py:144
  34.7 1.0 %copy-done.1 = f32[128,1024]{1,0:T(8,128)S(1)} copy-done((f32[128,1024]{1,0:T(8,128)S(1)}, f32[128,1024]{1,0:T(8,128)}, u32[]{:S(2)}) %copy-start.1) | copy-done | bytes 524312
  35.7 0.9 copy-done.3
  36.7 0.8 shard_map.121
  37.8 0.6 collective-permute-start.2
  38.3 0.6 collective-permute-done.there_ref
  38.9 1.1 %collective-permute-start.1 = (bf16[128,1024]{1,0:T(8,128)(2,1)S(1)}, bf16[128,1024]{1,0:T(8,128)(2,1)S(1)}, u32[]{:S(2)}, u32[]{:S(2)}) collective-permute-start(bf16[128,1024]{1,0:T(8,128)(2,1)S(1)} %pad_maximum_fusion), channel_id=1, source_target_pairs={{0,4},{1,3},{4,8},{5,1},{8,12},{9,5},{12,14},{13,9},{14,10},{15,13... | collective-permute-start | bytes 786440 | tf_op jit(solution)/shard_map/ppermute | solution.py:310
  40.1 0.5 collective-permute-start.19
  40.6 3.3 %shard_map.122 = (bf16[64,1024]{1,0:T(8,128)(2,1)S(1)}, bf16[64,1024]{1,0:T(8,128)(2,1)S(1)}, bf16[1,1024,896]{2,1,0:T(8,128)(2,1)S(1)}, bf16[1,1024,896]{2,1,0:T(8,128)(2,1)S(1)}, bf16[1,896,1024]{2,1,0:T(8,128)(2,1)S(1)}) custom-call(f32[128,16]{1,0:T(8,128)S(1)} %fusion.8.dense, bf16[1,1024,896]{2,1,0:T(8,128)(2,1)} %w_gate.1, ...), custom_call_target="tpu_custom_call" | custom-call | flops 704643072 | tf_op jit(solution)/shard_map/pallas_call | solution.py:240
  43.9 1.1 %shard_map.123 = (bf16[64,1024]{1,0:T(8,128)(2,1)S(1)}, bf16[64,1024]{1,0:T(8,128)(2,1)S(1)}) custom-call(f32[128,16]{1,0:T(8,128)S(1)} %fusion.8.dense, bf16[1,1024,896]{2,1,0:T(8,128)(2,1)S(1)} %get-tuple-element.59.w_gate, bf16[1,1024,896]{2,1,0:T(8,128)(2,1)S(1)} %get-tuple-element.60.w_up, bf16[1,896,1024]{2,1,0:T(8,128)(2,1)S(1)} %get-tuple-element.61.w_down, ...), custom_call_target="tpu_custom_call" | custom-call | flops 704643072 | tf_op jit(solution)/shard_map/pallas_call | solution.py:240
  45.4 1.2 %collective-permute-start.3 = (bf16[128,1024]{1,0:T(8,128)(2,1)S(1)}, bf16[128,1024]{1,0:T(8,128)(2,1)S(1)}, u32[]{:S(2)}, u32[]{:S(2)}) collective-permute-start(bf16[128,1024]{1,0:T(8,128)(2,1)S(1)} %collective-permute-done.1.here_ref), channel_id=1, source_target_pairs={{0,4},{1,3},{4,8},{5,1},{8,12},{9,5},{12,14},{13,9},{14,10},{15,13... | collective-permute-start | bytes 786440 | tf_op jit(solution)/shard_map/ppermute | solution.py:310
  46.6 1.5 %collective-permute-done.19.here_ref = bf16[128,1024]{1,0:T(8,128)(2,1)S(1)} collective-permute-done((bf16[128,1024]{1,0:T(8,128)(2,1)S(1)}, bf16[128,1024]{1,0:T(8,128)(2,1)S(1)}, u32[]{:S(2)}, u32[]{:S(2)}) %collective-permute-start.19) | collective-permute-done | bytes 262176 | tf_op jit(solution)/shard_map/ppermute | solution.py:310
  48.2 1.1 %collective-permute-start.20 = (bf16[128,1024]{1,0:T(8,128)(2,1)S(1)}, bf16[128,1024]{1,0:T(8,128)(2,1)S(1)}, u32[]{:S(2)}, u32[]{:S(2)}) collective-permute-start(bf16[128,1024]{1,0:T(8,128)(2,1)S(1)} %collective-permute-done.19.here_ref), channel_id=1, source_target_pairs={{0,4},{1,3},{4,8},{5,1},{8,12},{9,5},{12,14},{13,9},{14,10},{15,13... | collective-permute-start | bytes 786440 | tf_op jit(solution)/shard_map/ppermute | solution.py:310
  49.2 1.8 %shard_map.124 = (bf16[128,1024]{1,0:T(8,128)(2,1)S(1)}, bf16[128,1024]{1,0:T(8,128)(2,1)S(1)}) custom-call(f32[128,16]{1,0:T(8,128)S(1)} %fusion.8.dense, bf16[1,1024,896]{2,1,0:T(8,128)(2,1)S(1)} %get-tuple-element.59.w_gate, bf16[1,1024,896]{2,1,0:T(8,128)(2,1)S(1)} %get-tuple-element.60.w_up, bf16[1,896,1024]{2,1,0:T(8,128)(2,1)S(1)} %get-tuple-element.61.w_down, ...), custom_call_target="tpu_custom_call" | custom-call | flops 1409286144 | tf_op jit(solution)/shard_map/pallas_call | solution.py:240
  51.1 0.7 collective-permute-done.3.here_ref
  51.8 0.5 collective-permute-start.6
  52.3 1.2 %collective-permute-start.7 = (bf16[128,1024]{1,0:T(8,128)(2,1)S(1)}, bf16[128,1024]{1,0:T(8,128)(2,1)S(1)}, u32[]{:S(2)}, u32[]{:S(2)}) collective-permute-start(bf16[128,1024]{1,0:T(8,128)(2,1)S(1)} %collective-permute-done.3.here_ref), channel_id=1, source_target_pairs={{0,4},{1,3},{4,8},{5,1},{8,12},{9,5},{12,14},{13,9},{14,10},{15,13... | collective-permute-start | bytes 786440 | tf_op jit(solution)/shard_map/ppermute | solution.py:310
  53.5 1.8 %shard_map.128 = (bf16[128,1024]{1,0:T(8,128)(2,1)S(1)}, bf16[128,1024]{1,0:T(8,128)(2,1)S(1)}) custom-call(f32[128,16]{1,0:T(8,128)S(1)} %fusion.8.dense, bf16[1,1024,896]{2,1,0:T(8,128)(2,1)S(1)} %get-tuple-element.59.w_gate, bf16[1,1024,896]{2,1,0:T(8,128)(2,1)S(1)} %get-tuple-element.60.w_up, bf16[1,896,1024]{2,1,0:T(8,128)(2,1)S(1)} %get-tuple-element.61.w_down, ...), custom_call_target="tpu_custom_call" | custom-call | flops 1409286144 | tf_op jit(solution)/shard_map/pallas_call | solution.py:240
  55.4 0.5 collective-permute-start.23
  55.9 0.7 collective-permute-start.24
  56.6 1.9 %shard_map.125 = (bf16[128,1024]{1,0:T(8,128)(2,1)S(1)}, bf16[128,1024]{1,0:T(8,128)(2,1)S(1)}, f32[128,1024]{1,0:T(8,128)S(1)}) custom-call(f32[128,16]{1,0:T(8,128)S(1)} %fusion.8.dense, bf16[1,1024,896]{2,1,0:T(8,128)(2,1)S(1)} %get-tuple-element.59.w_gate, bf16[1,1024,896]{2,1,0:T(8,128)(2,1)S(1)} %get-tuple-element.60.w_up, ...), custom_call_target="tpu_custom_call" | custom-call | flops 1409286144 | tf_op jit(solution)/shard_map/pallas_call | solution.py:240
  58.6 0.5 collective-permute-start.9
  59.2 1.9 %shard_map.129 = (bf16[128,1024]{1,0:T(8,128)(2,1)S(1)}, bf16[128,1024]{1,0:T(8,128)(2,1)S(1)}, f32[128,1024]{1,0:T(8,128)S(1)}) custom-call(f32[128,16]{1,0:T(8,128)S(1)} %fusion.8.dense, bf16[1,1024,896]{2,1,0:T(8,128)(2,1)S(1)} %get-tuple-element.59.w_gate, bf16[1,1024,896]{2,1,0:T(8,128)(2,1)S(1)} %get-tuple-element.60.w_up, ...), custom_call_target="tpu_custom_call" | custom-call | flops 1409286144 | tf_op jit(solution)/shard_map/pallas_call | solution.py:240
  61.0 1.3 %collective-permute-done.24.here_ref = bf16[128,1024]{1,0:T(8,128)(2,1)S(1)} collective-permute-done((bf16[128,1024]{1,0:T(8,128)(2,1)S(1)}, bf16[128,1024]{1,0:T(8,128)(2,1)S(1)}, u32[]{:S(2)}, u32[]{:S(2)}) %collective-permute-start.24) | collective-permute-done | bytes 262176 | tf_op jit(solution)/shard_map/ppermute | solution.py:310
  62.3 0.5 collective-permute-start.26
  62.8 0.8 collective-permute-start.10
  63.6 1.0 collective-permute-start.27
  64.6 1.9 %shard_map.126 = (bf16[128,1024]{1,0:T(8,128)(2,1)S(1)}, bf16[128,1024]{1,0:T(8,128)(2,1)S(1)}, f32[128,1024]{1,0:T(8,128)S(1)}) custom-call(f32[128,16]{1,0:T(8,128)S(1)} %fusion.8.dense, bf16[1,1024,896]{2,1,0:T(8,128)(2,1)S(1)} %get-tuple-element.59.w_gate, bf16[1,1024,896]{2,1,0:T(8,128)(2,1)S(1)} %get-tuple-element.60.w_up, ...), custom_call_target="tpu_custom_call" | custom-call | flops 1409286144 | tf_op jit(solution)/shard_map/pallas_call | solution.py:240
  66.5 1.3 %collective-permute-done.10.here_ref = bf16[64,1024]{1,0:T(8,128)(2,1)S(1)} collective-permute-done((bf16[64,1024]{1,0:T(8,128)(2,1)S(1)}, bf16[64,1024]{1,0:T(8,128)(2,1)S(1)}, u32[]{:S(2)}, u32[]{:S(2)}) %collective-permute-start.10) | collective-permute-done | bytes 131104 | tf_op jit(solution)/shard_map/ppermute | solution.py:310
  67.9 0.5 collective-permute-start.12
  68.4 1.9 %shard_map.130 = (bf16[128,1024]{1,0:T(8,128)(2,1)S(1)}, bf16[128,1024]{1,0:T(8,128)(2,1)S(1)}, f32[128,1024]{1,0:T(8,128)S(1)}) custom-call(f32[128,16]{1,0:T(8,128)S(1)} %fusion.8.dense, bf16[1,1024,896]{2,1,0:T(8,128)(2,1)S(1)} %get-tuple-element.59.w_gate, bf16[1,1024,896]{2,1,0:T(8,128)(2,1)S(1)} %get-tuple-element.60.w_up, ...), custom_call_target="tpu_custom_call" | custom-call | flops 1409286144 | tf_op jit(solution)/shard_map/pallas_call | solution.py:240
  70.3 0.5 collective-permute-start.28
  70.8 1.1 %shard_map.127 = (bf16[64,1024]{1,0:T(8,128)(2,1)S(1)}, bf16[64,1024]{1,0:T(8,128)(2,1)S(1)}, f32[128,1024]{1,0:T(8,128)S(1)}) custom-call(f32[128,16]{1,0:T(8,128)S(1)} %fusion.8.dense, bf16[1,1024,896]{2,1,0:T(8,128)(2,1)S(1)} %get-tuple-element.59.w_gate, bf16[1,1024,896]{2,1,0:T(8,128)(2,1)S(1)} %get-tuple-element.60.w_up, ...), custom_call_target="tpu_custom_call" | custom-call | flops 704643072 | tf_op jit(solution)/shard_map/pallas_call | solution.py:240
  72.1 1.1 %shard_map.131 = (bf16[64,1024]{1,0:T(8,128)(2,1)S(1)}, bf16[64,1024]{1,0:T(8,128)(2,1)S(1)}, f32[128,1024]{1,0:T(8,128)S(1)}) custom-call(f32[128,16]{1,0:T(8,128)S(1)} %fusion.8.dense, bf16[1,1024,896]{2,1,0:T(8,128)(2,1)S(1)} %get-tuple-element.59.w_gate, bf16[1,1024,896]{2,1,0:T(8,128)(2,1)S(1)} %get-tuple-element.60.w_up, ...), custom_call_target="tpu_custom_call" | custom-call | flops 704643072 | tf_op jit(solution)/shard_map/pallas_call | solution.py:240
  73.2 0.5 collective-permute-start.30
  73.8 0.8 collective-permute-start.14
  74.8 0.9 collective-permute-start.31
  75.7 3.1 %collective-permute-done.14 = bf16[64,1024]{1,0:T(8,128)(2,1)S(1)} collective-permute-done((bf16[64,1024]{1,0:T(8,128)(2,1)S(1)}, bf16[64,1024]{1,0:T(8,128)(2,1)S(1)}, u32[]{:S(2)}, u32[]{:S(2)}) %collective-permute-start.14) | collective-permute-done | bytes 131104 | tf_op jit(solution)/shard_map/ppermute | solution.py:310
  78.8 0.8 collective-permute-start.15
  79.6 0.6 collective-permute-done.31
  80.3 0.8 collective-permute-start.32
  81.0 4.2 %collective-permute-done.15 = bf16[128,1024]{1,0:T(8,128)(2,1)S(1)} collective-permute-done((bf16[128,1024]{1,0:T(8,128)(2,1)S(1)}, bf16[128,1024]{1,0:T(8,128)(2,1)S(1)}, u32[]{:S(2)}, u32[]{:S(2)}) %collective-permute-start.15) | collective-permute-done | bytes 262176 | tf_op jit(solution)/shard_map/ppermute | solution.py:310
  85.3 0.8 collective-permute-start.16
  86.1 2.0 %collective-permute-done.32 = bf16[128,1024]{1,0:T(8,128)(2,1)S(1)} collective-permute-done((bf16[128,1024]{1,0:T(8,128)(2,1)S(1)}, bf16[128,1024]{1,0:T(8,128)(2,1)S(1)}, u32[]{:S(2)}, u32[]{:S(2)}) %collective-permute-start.32) | collective-permute-done | bytes 262176 | tf_op jit(solution)/shard_map/ppermute | solution.py:310
  88.2 0.8 collective-permute-start.33
  88.9 2.8 %collective-permute-done.16 = bf16[128,1024]{1,0:T(8,128)(2,1)S(1)} collective-permute-done((bf16[128,1024]{1,0:T(8,128)(2,1)S(1)}, bf16[128,1024]{1,0:T(8,128)(2,1)S(1)}, u32[]{:S(2)}, u32[]{:S(2)}) %collective-permute-start.16) | collective-permute-done | bytes 262176 | tf_op jit(solution)/shard_map/ppermute | solution.py:310
  91.8 0.8 collective-permute-start.17
  92.6 2.0 %collective-permute-done.33 = bf16[128,1024]{1,0:T(8,128)(2,1)S(1)} collective-permute-done((bf16[128,1024]{1,0:T(8,128)(2,1)S(1)}, bf16[128,1024]{1,0:T(8,128)(2,1)S(1)}, u32[]{:S(2)}, u32[]{:S(2)}) %collective-permute-start.33) | collective-permute-done | bytes 262176 | tf_op jit(solution)/shard_map/ppermute | solution.py:310
  94.6 0.8 collective-permute-start.34
  95.4 2.8 %collective-permute-done.17 = bf16[128,1024]{1,0:T(8,128)(2,1)S(1)} collective-permute-done((bf16[128,1024]{1,0:T(8,128)(2,1)S(1)}, bf16[128,1024]{1,0:T(8,128)(2,1)S(1)}, u32[]{:S(2)}, u32[]{:S(2)}) %collective-permute-start.17) | collective-permute-done | bytes 262176 | tf_op jit(solution)/shard_map/ppermute | solution.py:310
  98.4 2.7 %collective-permute-done.34 = bf16[128,1024]{1,0:T(8,128)(2,1)S(1)} collective-permute-done((bf16[128,1024]{1,0:T(8,128)(2,1)S(1)}, bf16[128,1024]{1,0:T(8,128)(2,1)S(1)}, u32[]{:S(2)}, u32[]{:S(2)}) %collective-permute-start.34) | collective-permute-done | bytes 262176 | tf_op jit(solution)/shard_map/ppermute | solution.py:310
  101.2 1.3 %collective-permute-done.35 = bf16[64,1024]{1,0:T(8,128)(2,1)S(1)} collective-permute-done((bf16[64,1024]{1,0:T(8,128)(2,1)S(1)}, bf16[64,1024]{1,0:T(8,128)(2,1)S(1)}, u32[]{:S(2)}, u32[]{:S(2)}) %collective-permute-start.35) | collective-permute-done | bytes 131104 | tf_op jit(solution)/shard_map/ppermute | solution.py:313
  102.7 0.7 pad_maximum_fusion.2
  (64 shorter events, 2.2 us)
Async XLA Ops:
  2.0 17.6 %all-to-all-start = ((bf16[32,32,128]{2,1,0:T(8,128)(2,1)}), bf16[32,32,128]{2,1,0:T(8,128)(2,1)S(1)}, u32[]{:S(2)}, u32[]{:S(2)}) async-start(bf16[32,32,128]{2,1,0:T(8,128)(2,1)} %bitcast.2), calls=%async_computation | async-start | bytes 524288 | tf_op jit(solution)/shard_map/all_to_all | solution.py:130
  20.4 14.3 %all-to-all-start.1 = ((bf16[32,40,128]{2,1,0:T(8,128)(2,1)}), bf16[32,40,128]{2,1,0:T(8,128)(2,1)S(1)}, u32[]{:S(2)}, u32[]{:S(2)}) async-start(bf16[32,40,128]{2,1,0:T(8,128)(2,1)} %shard_map.120), calls=%async_computation.1 | async-start | bytes 655360 | tf_op jit(solution)/shard_map/all_to_all | solution.py:144
  26.3 0.8 copy-start
  27.1 0.7 copy-start.2
  34.7 1.0 %copy-start.1 = (f32[128,1024]{1,0:T(8,128)S(1)}, f32[128,1024]{1,0:T(8,128)}, u32[]{:S(2)}) copy-start(f32[128,1024]{1,0:T(8,128)} %copy-done) | copy-start | bytes 1572868
  35.7 0.9 copy-start.3
  37.5 1.4 %collective-permute-start = (bf16[64,1024]{1,0:T(8,128)(2,1)S(1)}, bf16[64,1024]{1,0:T(8,128)(2,1)S(1)}, u32[]{:S(2)}, u32[]{:S(2)}) collective-permute-start(bf16[64,1024]{1,0:T(8,128)(2,1)S(1)} %get-tuple-element.58.here_ref), channel_id=1, source_target_pairs={{0,1},{1,0},{2,3},{3,2},{4,5},{5,4},{6,7},{7,6},{8,9},{9,8},{10,11... | collective-permute-start | bytes 393224 | tf_op jit(solution)/shard_map/ppermute | solution.py:313
  37.8 2.3 %collective-permute-start.2 = (bf16[64,1024]{1,0:T(8,128)(2,1)S(1)}, bf16[64,1024]{1,0:T(8,128)(2,1)S(1)}, u32[]{:S(2)}, u32[]{:S(2)}) collective-permute-start(bf16[64,1024]{1,0:T(8,128)(2,1)S(1)} %get-tuple-element.62.here_ref), channel_id=1, source_target_pairs={{0,1},{1,0},{2,3},{3,2},{4,5},{5,4},{6,7},{7,6},{8,9},{9,8},{10,11... | collective-permute-start | bytes 393224 | tf_op jit(solution)/shard_map/ppermute | solution.py:313
  38.9 6.4 %collective-permute-start.1 = (bf16[128,1024]{1,0:T(8,128)(2,1)S(1)}, bf16[128,1024]{1,0:T(8,128)(2,1)S(1)}, u32[]{:S(2)}, u32[]{:S(2)}) collective-permute-start(bf16[128,1024]{1,0:T(8,128)(2,1)S(1)} %pad_maximum_fusion), channel_id=1, source_target_pairs={{0,4},{1,3},{4,8},{5,1},{8,12},{9,5},{12,14},{13,9},{14,10},{15,13... | collective-permute-start | bytes 786440 | tf_op jit(solution)/shard_map/ppermute | solution.py:310
  40.1 8.1 %collective-permute-start.19 = (bf16[128,1024]{1,0:T(8,128)(2,1)S(1)}, bf16[128,1024]{1,0:T(8,128)(2,1)S(1)}, u32[]{:S(2)}, u32[]{:S(2)}) collective-permute-start(bf16[128,1024]{1,0:T(8,128)(2,1)S(1)} %pad_maximum_fusion.1), channel_id=1, source_target_pairs={{0,4},{1,3},{4,8},{5,1},{8,12},{9,5},{12,14},{13,9},{14,10},{15,13... | collective-permute-start | bytes 786440 | tf_op jit(solution)/shard_map/ppermute | solution.py:310
  45.4 3.9 %collective-permute-start.4 = (bf16[128,1024]{1,0:T(8,128)(2,1)S(1)}, bf16[128,1024]{1,0:T(8,128)(2,1)S(1)}, u32[]{:S(2)}, u32[]{:S(2)}) collective-permute-start(bf16[128,1024]{1,0:T(8,128)(2,1)S(1)} %collective-permute-done.1.here_ref), channel_id=1, source_target_pairs={{0,1},{1,0},{2,3},{3,2},{4,5},{5,4},{6,7},{7,6},{8,9},{9,8},{10,11... | collective-permute-start | bytes 786440 | tf_op jit(solution)/shard_map/ppermute | solution.py:313
  45.4 6.4 %collective-permute-start.3 = (bf16[128,1024]{1,0:T(8,128)(2,1)S(1)}, bf16[128,1024]{1,0:T(8,128)(2,1)S(1)}, u32[]{:S(2)}, u32[]{:S(2)}) collective-permute-start(bf16[128,1024]{1,0:T(8,128)(2,1)S(1)} %collective-permute-done.1.here_ref), channel_id=1, source_target_pairs={{0,4},{1,3},{4,8},{5,1},{8,12},{9,5},{12,14},{13,9},{14,10},{15,13... | collective-permute-start | bytes 786440 | tf_op jit(solution)/shard_map/ppermute | solution.py:310
  48.2 5.3 %collective-permute-start.21 = (bf16[128,1024]{1,0:T(8,128)(2,1)S(1)}, bf16[128,1024]{1,0:T(8,128)(2,1)S(1)}, u32[]{:S(2)}, u32[]{:S(2)}) collective-permute-start(bf16[128,1024]{1,0:T(8,128)(2,1)S(1)} %collective-permute-done.19.here_ref), channel_id=1, source_target_pairs={{0,1},{1,0},{2,3},{3,2},{4,5},{5,4},{6,7},{7,6},{8,9},{9,8},{10,11... | collective-permute-start | bytes 786440 | tf_op jit(solution)/shard_map/ppermute | solution.py:313
  48.2 7.2 %collective-permute-start.20 = (bf16[128,1024]{1,0:T(8,128)(2,1)S(1)}, bf16[128,1024]{1,0:T(8,128)(2,1)S(1)}, u32[]{:S(2)}, u32[]{:S(2)}) collective-permute-start(bf16[128,1024]{1,0:T(8,128)(2,1)S(1)} %collective-permute-done.19.here_ref), channel_id=1, source_target_pairs={{0,4},{1,3},{4,8},{5,1},{8,12},{9,5},{12,14},{13,9},{14,10},{15,13... | collective-permute-start | bytes 786440 | tf_op jit(solution)/shard_map/ppermute | solution.py:310
  51.8 4.2 %collective-permute-start.5 = (bf16[128,1024]{1,0:T(8,128)(2,1)S(1)}, bf16[128,1024]{1,0:T(8,128)(2,1)S(1)}, u32[]{:S(2)}, u32[]{:S(2)}) collective-permute-start(bf16[128,1024]{1,0:T(8,128)(2,1)S(1)} %collective-permute-done.3.here_ref), channel_id=1, source_target_pairs={{0,1},{1,0},{2,3},{3,2},{4,5},{5,4},{6,7},{7,6},{8,9},{9,8},{10,11... | collective-permute-start | bytes 786440 | tf_op jit(solution)/shard_map/ppermute | solution.py:313
  51.8 4.8 %collective-permute-start.6 = (bf16[128,1024]{1,0:T(8,128)(2,1)S(1)}, bf16[128,1024]{1,0:T(8,128)(2,1)S(1)}, u32[]{:S(2)}, u32[]{:S(2)}) collective-permute-start(bf16[128,1024]{1,0:T(8,128)(2,1)S(1)} %get-tuple-element.67), channel_id=1, source_target_pairs={{0,1},{1,0},{2,3},{3,2},{4,5},{5,4},{6,7},{7,6},{8,9},{9,8},{10,11... | collective-permute-start | bytes 786440 | tf_op jit(solution)/shard_map/ppermute | solution.py:313
  52.3 6.4 %collective-permute-start.7 = (bf16[128,1024]{1,0:T(8,128)(2,1)S(1)}, bf16[128,1024]{1,0:T(8,128)(2,1)S(1)}, u32[]{:S(2)}, u32[]{:S(2)}) collective-permute-start(bf16[128,1024]{1,0:T(8,128)(2,1)S(1)} %collective-permute-done.3.here_ref), channel_id=1, source_target_pairs={{0,4},{1,3},{4,8},{5,1},{8,12},{9,5},{12,14},{13,9},{14,10},{15,13... | collective-permute-start | bytes 786440 | tf_op jit(solution)/shard_map/ppermute | solution.py:310
  55.3 3.8 %collective-permute-start.22 = (bf16[128,1024]{1,0:T(8,128)(2,1)S(1)}, bf16[128,1024]{1,0:T(8,128)(2,1)S(1)}, u32[]{:S(2)}, u32[]{:S(2)}) collective-permute-start(bf16[128,1024]{1,0:T(8,128)(2,1)S(1)} %collective-permute-done.20.here_ref), channel_id=1, source_target_pairs={{0,1},{1,0},{2,3},{3,2},{4,5},{5,4},{6,7},{7,6},{8,9},{9,8},{10,11... | collective-permute-start | bytes 786440 | tf_op jit(solution)/shard_map/ppermute | solution.py:313
  55.4 3.7 %collective-permute-start.23 = (bf16[128,1024]{1,0:T(8,128)(2,1)S(1)}, bf16[128,1024]{1,0:T(8,128)(2,1)S(1)}, u32[]{:S(2)}, u32[]{:S(2)}) collective-permute-start(bf16[128,1024]{1,0:T(8,128)(2,1)S(1)} %get-tuple-element.84), channel_id=1, source_target_pairs={{0,1},{1,0},{2,3},{3,2},{4,5},{5,4},{6,7},{7,6},{8,9},{9,8},{10,11... | collective-permute-start | bytes 786440 | tf_op jit(solution)/shard_map/ppermute | solution.py:313
  55.9 6.4 %collective-permute-start.24 = (bf16[128,1024]{1,0:T(8,128)(2,1)S(1)}, bf16[128,1024]{1,0:T(8,128)(2,1)S(1)}, u32[]{:S(2)}, u32[]{:S(2)}) collective-permute-start(bf16[128,1024]{1,0:T(8,128)(2,1)S(1)} %collective-permute-done.20.here_ref), channel_id=1, source_target_pairs={{0,4},{1,3},{4,8},{5,1},{8,12},{9,5},{12,14},{13,9},{14,10},{15,13... | collective-permute-start | bytes 786440 | tf_op jit(solution)/shard_map/ppermute | solution.py:310
  58.6 5.0 %collective-permute-start.8 = (bf16[128,1024]{1,0:T(8,128)(2,1)S(1)}, bf16[128,1024]{1,0:T(8,128)(2,1)S(1)}, u32[]{:S(2)}, u32[]{:S(2)}) collective-permute-start(bf16[128,1024]{1,0:T(8,128)(2,1)S(1)} %collective-permute-done.7.here_ref), channel_id=1, source_target_pairs={{0,1},{1,0},{2,3},{3,2},{4,5},{5,4},{6,7},{7,6},{8,9},{9,8},{10,11... | collective-permute-start | bytes 786440 | tf_op jit(solution)/shard_map/ppermute | solution.py:313
  58.6 6.0 %collective-permute-start.9 = (bf16[128,1024]{1,0:T(8,128)(2,1)S(1)}, bf16[128,1024]{1,0:T(8,128)(2,1)S(1)}, u32[]{:S(2)}, u32[]{:S(2)}) collective-permute-start(bf16[128,1024]{1,0:T(8,128)(2,1)S(1)} %get-tuple-element.71), channel_id=1, source_target_pairs={{0,1},{1,0},{2,3},{3,2},{4,5},{5,4},{6,7},{7,6},{8,9},{9,8},{10,11... | collective-permute-start | bytes 786440 | tf_op jit(solution)/shard_map/ppermute | solution.py:313
  62.3 6.1 %collective-permute-start.25 = (bf16[128,1024]{1,0:T(8,128)(2,1)S(1)}, bf16[128,1024]{1,0:T(8,128)(2,1)S(1)}, u32[]{:S(2)}, u32[]{:S(2)}) collective-permute-start(bf16[128,1024]{1,0:T(8,128)(2,1)S(1)} %collective-permute-done.24.here_ref), channel_id=1, source_target_pairs={{0,1},{1,0},{2,3},{3,2},{4,5},{5,4},{6,7},{7,6},{8,9},{9,8},{10,11... | collective-permute-start | bytes 786440 | tf_op jit(solution)/shard_map/ppermute | solution.py:313
  62.3 6.1 %collective-permute-start.26 = (bf16[128,1024]{1,0:T(8,128)(2,1)S(1)}, bf16[128,1024]{1,0:T(8,128)(2,1)S(1)}, u32[]{:S(2)}, u32[]{:S(2)}) collective-permute-start(bf16[128,1024]{1,0:T(8,128)(2,1)S(1)} %get-tuple-element.88), channel_id=1, source_target_pairs={{0,1},{1,0},{2,3},{3,2},{4,5},{5,4},{6,7},{7,6},{8,9},{9,8},{10,11... | collective-permute-start | bytes 786440 | tf_op jit(solution)/shard_map/ppermute | solution.py:313
  62.8 5.0 %collective-permute-start.10 = (bf16[64,1024]{1,0:T(8,128)(2,1)S(1)}, bf16[64,1024]{1,0:T(8,128)(2,1)S(1)}, u32[]{:S(2)}, u32[]{:S(2)}) collective-permute-start(bf16[64,1024]{1,0:T(8,128)(2,1)S(1)} %slice.37), channel_id=1, source_target_pairs={{0,4},{1,3},{4,8},{5,1},{8,12},{9,5},{12,14},{13,9},{14,10},{15,13... | collective-permute-start | bytes 393224 | tf_op jit(solution)/shard_map/ppermute | solution.py:310
  63.6 6.7 %collective-permute-start.27 = (bf16[64,1024]{1,0:T(8,128)(2,1)S(1)}, bf16[64,1024]{1,0:T(8,128)(2,1)S(1)}, u32[]{:S(2)}, u32[]{:S(2)}) collective-permute-start(bf16[64,1024]{1,0:T(8,128)(2,1)S(1)} %slice.41), channel_id=1, source_target_pairs={{0,4},{1,3},{4,8},{5,1},{8,12},{9,5},{12,14},{13,9},{14,10},{15,13... | collective-permute-start | bytes 393224 | tf_op jit(solution)/shard_map/ppermute | solution.py:310
  67.9 3.0 %collective-permute-start.11 = (bf16[64,1024]{1,0:T(8,128)(2,1)S(1)}, bf16[64,1024]{1,0:T(8,128)(2,1)S(1)}, u32[]{:S(2)}, u32[]{:S(2)}) collective-permute-start(bf16[64,1024]{1,0:T(8,128)(2,1)S(1)} %collective-permute-done.10.here_ref), channel_id=1, source_target_pairs={{0,1},{1,0},{2,3},{3,2},{4,5},{5,4},{6,7},{7,6},{8,9},{9,8},{10,11... | collective-permute-start | bytes 393224 | tf_op jit(solution)/shard_map/ppermute | solution.py:313
  67.9 3.0 %collective-permute-start.12 = (bf16[128,1024]{1,0:T(8,128)(2,1)S(1)}, bf16[128,1024]{1,0:T(8,128)(2,1)S(1)}, u32[]{:S(2)}, u32[]{:S(2)}) collective-permute-start(bf16[128,1024]{1,0:T(8,128)(2,1)S(1)} %get-tuple-element.75), channel_id=1, source_target_pairs={{0,1},{1,0},{2,3},{3,2},{4,5},{5,4},{6,7},{7,6},{8,9},{9,8},{10,11... | collective-permute-start | bytes 786440 | tf_op jit(solution)/shard_map/ppermute | solution.py:313
  70.2 1.9 %collective-permute-start.29 = (bf16[128,1024]{1,0:T(8,128)(2,1)S(1)}, bf16[128,1024]{1,0:T(8,128)(2,1)S(1)}, u32[]{:S(2)}, u32[]{:S(2)}) collective-permute-start(bf16[128,1024]{1,0:T(8,128)(2,1)S(1)} %get-tuple-element.92), channel_id=1, source_target_pairs={{0,1},{1,0},{2,3},{3,2},{4,5},{5,4},{6,7},{7,6},{8,9},{9,8},{10,11... | collective-permute-start | bytes 786440 | tf_op jit(solution)/shard_map/ppermute | solution.py:313
  70.3 1.8 %collective-permute-start.28 = (bf16[64,1024]{1,0:T(8,128)(2,1)S(1)}, bf16[64,1024]{1,0:T(8,128)(2,1)S(1)}, u32[]{:S(2)}, u32[]{:S(2)}) collective-permute-start(bf16[64,1024]{1,0:T(8,128)(2,1)S(1)} %collective-permute-done.27.here_ref), channel_id=1, source_target_pairs={{0,1},{1,0},{2,3},{3,2},{4,5},{5,4},{6,7},{7,6},{8,9},{9,8},{10,11... | collective-permute-start | bytes 393224 | tf_op jit(solution)/shard_map/ppermute | solution.py:313
  72.0 1.8 %collective-permute-start.13 = (bf16[64,1024]{1,0:T(8,128)(2,1)S(1)}, bf16[64,1024]{1,0:T(8,128)(2,1)S(1)}, u32[]{:S(2)}, u32[]{:S(2)}) collective-permute-start(bf16[64,1024]{1,0:T(8,128)(2,1)S(1)} %get-tuple-element.78), channel_id=1, source_target_pairs={{0,1},{1,0},{2,3},{3,2},{4,5},{5,4},{6,7},{7,6},{8,9},{9,8},{10,11... | collective-permute-start | bytes 393224 | tf_op jit(solution)/shard_map/ppermute | solution.py:313
  73.2 1.5 %collective-permute-start.30 = (bf16[64,1024]{1,0:T(8,128)(2,1)S(1)}, bf16[64,1024]{1,0:T(8,128)(2,1)S(1)}, u32[]{:S(2)}, u32[]{:S(2)}) collective-permute-start(bf16[64,1024]{1,0:T(8,128)(2,1)S(1)} %get-tuple-element.95), channel_id=1, source_target_pairs={{0,1},{1,0},{2,3},{3,2},{4,5},{5,4},{6,7},{7,6},{8,9},{9,8},{10,11... | collective-permute-start | bytes 393224 | tf_op jit(solution)/shard_map/ppermute | solution.py:313
  73.8 5.0 %collective-permute-start.14 = (bf16[64,1024]{1,0:T(8,128)(2,1)S(1)}, bf16[64,1024]{1,0:T(8,128)(2,1)S(1)}, u32[]{:S(2)}, u32[]{:S(2)}) collective-permute-start(bf16[64,1024]{1,0:T(8,128)(2,1)S(1)} %add_convert_fusion.7), channel_id=1, source_target_pairs={{0,4},{1,3},{4,8},{5,1},{8,12},{9,5},{12,14},{13,9},{14,10},{15,13... | collective-permute-start | bytes 393224 | tf_op jit(solution)/shard_map/ppermute | solution.py:310
  74.8 5.4 %collective-permute-start.31 = (bf16[64,1024]{1,0:T(8,128)(2,1)S(1)}, bf16[64,1024]{1,0:T(8,128)(2,1)S(1)}, u32[]{:S(2)}, u32[]{:S(2)}) collective-permute-start(bf16[64,1024]{1,0:T(8,128)(2,1)S(1)} %add_convert_fusion.6), channel_id=1, source_target_pairs={{0,4},{1,3},{4,8},{5,1},{8,12},{9,5},{12,14},{13,9},{14,10},{15,13... | collective-permute-start | bytes 393224 | tf_op jit(solution)/shard_map/ppermute | solution.py:310
  78.8 6.4 %collective-permute-start.15 = (bf16[128,1024]{1,0:T(8,128)(2,1)S(1)}, bf16[128,1024]{1,0:T(8,128)(2,1)S(1)}, u32[]{:S(2)}, u32[]{:S(2)}) collective-permute-start(bf16[128,1024]{1,0:T(8,128)(2,1)S(1)} %add_convert_fusion.5), channel_id=1, source_target_pairs={{0,4},{1,3},{4,8},{5,1},{8,12},{9,5},{12,14},{13,9},{14,10},{15,13... | collective-permute-start | bytes 786440 | tf_op jit(solution)/shard_map/ppermute | solution.py:310
  80.3 7.8 %collective-permute-start.32 = (bf16[128,1024]{1,0:T(8,128)(2,1)S(1)}, bf16[128,1024]{1,0:T(8,128)(2,1)S(1)}, u32[]{:S(2)}, u32[]{:S(2)}) collective-permute-start(bf16[128,1024]{1,0:T(8,128)(2,1)S(1)} %add_convert_fusion.2), channel_id=1, source_target_pairs={{0,4},{1,3},{4,8},{5,1},{8,12},{9,5},{12,14},{13,9},{14,10},{15,13... | collective-permute-start | bytes 786440 | tf_op jit(solution)/shard_map/ppermute | solution.py:310
  85.3 6.4 %collective-permute-start.16 = (bf16[128,1024]{1,0:T(8,128)(2,1)S(1)}, bf16[128,1024]{1,0:T(8,128)(2,1)S(1)}, u32[]{:S(2)}, u32[]{:S(2)}) collective-permute-start(bf16[128,1024]{1,0:T(8,128)(2,1)S(1)} %add_convert_fusion.4), channel_id=1, source_target_pairs={{0,4},{1,3},{4,8},{5,1},{8,12},{9,5},{12,14},{13,9},{14,10},{15,13... | collective-permute-start | bytes 786440 | tf_op jit(solution)/shard_map/ppermute | solution.py:310
  88.2 6.4 %collective-permute-start.33 = (bf16[128,1024]{1,0:T(8,128)(2,1)S(1)}, bf16[128,1024]{1,0:T(8,128)(2,1)S(1)}, u32[]{:S(2)}, u32[]{:S(2)}) collective-permute-start(bf16[128,1024]{1,0:T(8,128)(2,1)S(1)} %add_convert_fusion.1), channel_id=1, source_target_pairs={{0,4},{1,3},{4,8},{5,1},{8,12},{9,5},{12,14},{13,9},{14,10},{15,13... | collective-permute-start | bytes 786440 | tf_op jit(solution)/shard_map/ppermute | solution.py:310
  91.8 6.4 %collective-permute-start.17 = (bf16[128,1024]{1,0:T(8,128)(2,1)S(1)}, bf16[128,1024]{1,0:T(8,128)(2,1)S(1)}, u32[]{:S(2)}, u32[]{:S(2)}) collective-permute-start(bf16[128,1024]{1,0:T(8,128)(2,1)S(1)} %add_convert_fusion.3), channel_id=1, source_target_pairs={{0,4},{1,3},{4,8},{5,1},{8,12},{9,5},{12,14},{13,9},{14,10},{15,13... | collective-permute-start | bytes 786440 | tf_op jit(solution)/shard_map/ppermute | solution.py:310
  94.6 6.4 %collective-permute-start.34 = (bf16[128,1024]{1,0:T(8,128)(2,1)S(1)}, bf16[128,1024]{1,0:T(8,128)(2,1)S(1)}, u32[]{:S(2)}, u32[]{:S(2)}) collective-permute-start(bf16[128,1024]{1,0:T(8,128)(2,1)S(1)} %add_convert_fusion), channel_id=1, source_target_pairs={{0,4},{1,3},{4,8},{5,1},{8,12},{9,5},{12,14},{13,9},{14,10},{15,13... | collective-permute-start | bytes 786440 | tf_op jit(solution)/shard_map/ppermute | solution.py:310
  98.3 2.9 %collective-permute-start.18 = (bf16[64,1024]{1,0:T(8,128)(2,1)S(1)}, bf16[64,1024]{1,0:T(8,128)(2,1)S(1)}, u32[]{:S(2)}, u32[]{:S(2)}) collective-permute-start(bf16[64,1024]{1,0:T(8,128)(2,1)S(1)} %fusion.4), channel_id=1, source_target_pairs={{0,1},{1,0},{2,3},{3,2},{4,5},{5,4},{6,7},{7,6},{8,9},{9,8},{10,11... | collective-permute-start | bytes 393224 | tf_op jit(solution)/shard_map/ppermute | solution.py:313
  101.1 1.4 %collective-permute-start.35 = (bf16[64,1024]{1,0:T(8,128)(2,1)S(1)}, bf16[64,1024]{1,0:T(8,128)(2,1)S(1)}, u32[]{:S(2)}, u32[]{:S(2)}) collective-permute-start(bf16[64,1024]{1,0:T(8,128)(2,1)S(1)} %fusion), channel_id=1, source_target_pairs={{0,1},{1,0},{2,3},{3,2},{4,5},{5,4},{6,7},{7,6},{8,9},{9,8},{10,11... | collective-permute-start | bytes 393224 | tf_op jit(solution)/shard_map/ppermute | solution.py:313

commit v3 on v2

v3 whole, which is shorter than its diff:
```python
import functools

import jax
import jax.numpy as jnp
from jax import lax
from jax.experimental import pallas as pl
from jax.experimental.pallas import tpu as pltpu
from jax.sharding import PartitionSpec as P

HEADS = 8
HEAD = 128
HALVES = 2
BOTH = ("seg", "ctx")
F32 = jnp.float32
BF16 = jnp.bfloat16
VMEM = pl.BlockSpec(memory_space=pltpu.VMEM)
HBM = pl.BlockSpec(memory_space=pltpu.HBM)
LIMIT = 16 * 1024 * 1024


def call(kernel, out_shape, in_specs, flops, *operands):
    many = isinstance(out_shape, list)
    return pl.pallas_call(
        kernel,
        out_shape=out_shape,
        in_specs=in_specs,
        out_specs=[VMEM] * len(out_shape) if many else VMEM,
        compiler_params=pltpu.CompilerParams(vmem_limit_bytes=LIMIT),
        cost_estimate=pl.CostEstimate(flops=flops, bytes_accessed=0, transcendentals=0),
    )(*operands)


def in_hbm(array):
    return pltpu.with_memory_space_constraint(array, pltpu.HBM)


def copies_of(sources, targets, sems):
    copies = [
        pltpu.make_async_copy(source, target, sems.at[i])
        for i, (source, target) in enumerate(zip(sources, targets))
    ]
    for copy in copies:
        copy.start()
    return copies


def chip_order(chips):
    return list(range(0, chips, 2)) + list(range(1, chips, 2))[::-1]


def ring_perm(chips, shift):
    order = chip_order(chips)
    pairs = []
    for place, chip in enumerate(order):
        pairs.append((chip * 2, order[(place + shift) % chips] * 2))
        pairs.append((chip * 2 + 1, order[(place - shift) % chips] * 2 + 1))
    return pairs


def core_perm(chips):
    return [(dev, dev ^ 1) for dev in range(2 * chips)]


def state_kernel(k_hbm, v_hbm, out_ref, k_ref, v_ref, sems):
    for copy in copies_of([k_hbm, v_hbm], [k_ref, v_ref], sems):
        copy.wait()
    for head in range(HEADS):
        cols = pl.ds(head * HEAD, HEAD)
        state = lax.dot_general(
            k_ref[:, cols], v_ref[:, cols], (((0,), (0,)), ((), ())), preferred_element_type=F32
        )
        out_ref[cols, :] = state.astype(BF16)


def inside_kernel(count, *refs):
    q_ref, k_ref, v_ref = refs[count + 1 : count + 4]
    out_hbm, out_ref, sems = refs[2 * count + 1 :]
    copies = copies_of(refs[:count], refs[count + 1 : 2 * count + 1], sems)
    for copy in copies[:3]:
        copy.wait()
    ntok = q_ref.shape[0]
    causal = lax.broadcasted_iota(jnp.int32, (ntok, ntok), 0) >= lax.broadcasted_iota(
        jnp.int32, (ntok, ntok), 1
    )
    for head in range(HEADS):
        cols = pl.ds(head * HEAD, HEAD)
        scores = lax.dot_general(
            q_ref[:, cols], k_ref[:, cols], (((1,), (1,)), ((), ())), preferred_element_type=F32
        )
        scores = jnp.where(causal, scores, 0.0).astype(BF16)
        out_ref[:, cols] = jnp.dot(scores, v_ref[:, cols], preferred_element_type=F32)
    copy = pltpu.make_async_copy(out_ref, out_hbm, sems.at[count])
    copy.start()
    for copy in copies[3:] + [copy]:
        copy.wait()


def attend_inside(arrays, after):
    count = len(arrays)
    outs = [pltpu.VMEM(a.shape, a.dtype) for a in arrays]
    outs.append(pltpu.HBM(arrays[0].shape, F32))
    return pl.pallas_call(
        functools.partial(inside_kernel, count),
        out_shape=outs,
        in_specs=[HBM] * count + [pl.BlockSpec(memory_space=pl.ANY)],
        out_specs=[VMEM] * count + [HBM],
        scratch_shapes=[pltpu.VMEM(arrays[0].shape, F32), pltpu.SemaphoreType.DMA((count + 1,))],
        compiler_params=pltpu.CompilerParams(vmem_limit_bytes=LIMIT),
    )(*[in_hbm(a) for a in arrays], after)


def prefix_kernel(pieces_ref, extra_ref, out_ref):
    devices, share, cols = pieces_ref.shape
    owners = extra_ref.shape[0]
    total = jnp.zeros((share, cols), F32)
    for dev in range(devices):
        rows = jnp.concatenate([total, extra_ref[dev % owners]])
        out_ref[dev] = rows.astype(BF16)
        total += pieces_ref[dev].astype(F32)


def scan_states(states, dense):
    rows, cols = states.shape
    ntok, owners = dense.shape
    devices = lax.axis_size(BOTH)
    share = rows // devices
    top = dense.astype(BF16).astype(F32)
    split = jnp.stack([top.T, (dense - top).T], axis=1)
    pairs = split.reshape(owners // 2, 2, 2, ntok)
    split = jnp.concatenate([split, pairs[:, ::-1].reshape(split.shape)], axis=1)
    extra = split.reshape(owners, 4 * ntok // cols, cols)
    used = extra.shape[1]
    extra = jnp.pad(extra, ((0, 0), (0, -used % 8), (0, 0)))
    pieces = states.reshape(devices, share, cols)
    pieces = lax.all_to_all(pieces, BOTH, split_axis=0, concat_axis=0, tiled=True)
    whole_tiles = share % 16 == 0
    if whole_tiles:
        out = jax.ShapeDtypeStruct((devices, share + extra.shape[1], cols), BF16)
        sums = call(prefix_kernel, out, [VMEM] * 2, 0, pieces, extra)
    else:
        earlier = jnp.arange(devices)[:, None] > jnp.arange(devices)[None, :]
        sums = jnp.dot(
            earlier.astype(BF16),
            pieces.reshape(devices, share * cols),
            preferred_element_type=F32,
        ).reshape(devices, share, cols)
        extra_all = jnp.concatenate([extra] * (devices // owners))
        sums = jnp.concatenate([sums, extra_all], axis=1).astype(BF16)
    sums = lax.all_to_all(sums, BOTH, split_axis=0, concat_axis=0, tiled=True)
    split = lax.dynamic_slice_in_dim(
        sums[:, share : share + used], lax.axis_index("seg") * owners, owners
    )
    split = split.reshape(owners, 4, ntok).astype(F32)
    mine = jnp.concatenate([split[:, 0] + split[:, 1], split[:, 2] + split[:, 3]]).T
    if not whole_tiles:
        sums = sums[:, :share].reshape(rows // HEAD, HEAD, cols)
        share = HEAD
    return sums, share, mine


def rms(rows, gain):
    mean_sq = jnp.mean(rows * rows, axis=1, keepdims=True)
    return rows * lax.rsqrt(mean_sq + 1e-06) * gain


def route_kernel(
    share, sums_ref, q_ref, proj_ref, gain_ref, moe_gain_ref, inside_hbm, hidden_hbm, *refs
):
    outs, (inside_ref, hidden_ref, sems) = refs[: 1 + HALVES], refs[1 + HALVES :]
    copies = copies_of([inside_hbm, hidden_hbm], [inside_ref, hidden_ref], sems)
    ntok, width = q_ref.shape
    slabs = HEAD // share
    attended = []
    for head in range(HEADS):
        cols = pl.ds(head * HEAD, HEAD)
        earlier = jnp.concatenate(
            [sums_ref[head * slabs + i, pl.ds(0, share), :] for i in range(slabs)]
        )
        attended.append(jnp.dot(q_ref[:, cols], earlier, preferred_element_type=F32))
    for copy in copies:
        copy.wait()
    attended = jnp.concatenate(attended, axis=1) + inside_ref[...]
    normed = rms(attended, gain_ref[...]).astype(BF16)
    mixed = hidden_ref[...].astype(F32) + jnp.dot(
        normed, proj_ref[...], preferred_element_type=F32
    )
    outs[0][...] = mixed
    routed = rms(mixed, moe_gain_ref[...]).astype(BF16)
    cut = ntok // HALVES
    for half in range(HALVES):
        outs[1 + half][...] = routed[half * cut : (half + 1) * cut]


def expert_kernel(chips, step, first, dense, rows_ref, *refs):
    weights, out_ref, refs = refs[:6], refs[6], refs[7:]
    copies = []
    if refs:
        copies = copies_of(weights, refs[:6], refs[6])
        weights = refs[:6]
    me = lax.axis_index("ctx")
    core, chip = me % 2, me // 2
    place = jnp.where(chip % 2 == 0, chip // 2, chips - 1 - chip // 2)
    spot = (place - (1 - 2 * core) * step + chips) % chips
    chip = jnp.where(2 * spot < chips, 2 * spot, 2 * (chips - spot) - 1)
    planes = [core] if step in (0, chips // 2) else [core, 1 - core]
    count = rows_ref.shape[0]
    cut = count // len(planes)
    table = dense[pl.ds(first, cut), :]
    lane = lax.broadcasted_iota(jnp.int32, table.shape, 1)
    rows = rows_ref[...]
    total = jnp.zeros(rows.shape, F32)
    for which in range(2):
        w_gate, w_up, w_down = weights[3 * which : 3 * which + 3]
        for copy in copies[3 * which : 3 * which + 3]:
            copy.wait()
        gate = jnp.dot(rows, w_gate[0], preferred_element_type=F32)
        upper = jnp.dot(rows, w_up[0], preferred_element_type=F32)
        inner = (gate / (1.0 + jnp.exp(-gate)) * upper).astype(BF16)
        result = jnp.dot(inner, w_down[0], preferred_element_type=F32)
        scales = []
        for plane in planes:
            column = which * 2 * chips + chip * 2 + plane
            picked = jnp.where(lane == column, table, 0.0)
            scales.append(jnp.sum(picked, axis=1, keepdims=True))
        total += result * jnp.concatenate(scales)
    out_ref[...] = total


def expert(rows, chips, step, first, dense, weights, staging):
    outs, specs, scratch = [jax.ShapeDtypeStruct(rows.shape, F32)], [VMEM] * 6, []
    if staging:
        outs += [pltpu.VMEM(w.shape, w.dtype) for w in weights]
        specs, scratch = [HBM] * 6, [pltpu.SemaphoreType.DMA((6,))]
        weights = [in_hbm(w) for w in weights]
    return pl.pallas_call(
        functools.partial(expert_kernel, chips, step, first),
        out_shape=outs,
        in_specs=[VMEM] * 2 + specs,
        out_specs=[VMEM] * len(outs),
        scratch_shapes=scratch,
        compiler_params=pltpu.CompilerParams(vmem_limit_bytes=LIMIT),
        cost_estimate=pl.CostEstimate(
            flops=0, bytes_accessed=0, transcendentals=0
        ),
    )(dense, rows, *weights)


def body(
    hidden_in,
    queries,
    key_rows,
    values,
    norm_gain,
    out_proj,
    moe_gain,
    w_gate,
    w_up,
    w_down,
    expert_ids,
    route_scale,
):
    ntok, width = queries.shape
    owners = lax.axis_size("ctx")
    chips = owners // 2
    out = jax.ShapeDtypeStruct((HEADS * HEAD, HEAD), BF16)
    states = pl.pallas_call(
        state_kernel,
        out_shape=out,
        in_specs=[pl.BlockSpec(memory_space=pltpu.HBM)] * 2,
        out_specs=VMEM,
        scratch_shapes=[pltpu.VMEM((ntok, width), BF16)] * 2 + [pltpu.SemaphoreType.DMA((2,))],
        compiler_params=pltpu.CompilerParams(vmem_limit_bytes=LIMIT),
    )(in_hbm(key_rows), in_hbm(values))
    scales = route_scale.astype(F32)
    weight = scales / jnp.sum(scales, axis=1, keepdims=True)
    grid = jnp.arange(owners, dtype=jnp.int32)
    dense = jnp.sum(
        jnp.where(expert_ids[:, :, None] == grid[None, None, :], weight[:, :, None], 0.0), axis=1
    )
    sums, share, dense = scan_states(states, dense)

    out = jax.ShapeDtypeStruct((ntok, width), F32)
    arrays = [queries, key_rows, values, out_proj, norm_gain[None, :], moe_gain[None, :]]
    queries, _, _, out_proj, norm_gain, moe_gain, inside = attend_inside(arrays, states)
    cut = ntok // HALVES
    held = [inside, hidden_in]
    mixed, *routed = pl.pallas_call(
        functools.partial(route_kernel, share),
        out_shape=[out] + [jax.ShapeDtypeStruct((cut, width), BF16)] * HALVES,
        in_specs=[VMEM] * 5 + [HBM] * len(held),
        out_specs=[VMEM] * (1 + HALVES),
        scratch_shapes=[pltpu.VMEM(a.shape, a.dtype) for a in held]
        + [pltpu.SemaphoreType.DMA((len(held),))],
        compiler_params=pltpu.CompilerParams(vmem_limit_bytes=LIMIT),
    )(sums, queries, out_proj, norm_gain, moe_gain, *[in_hbm(a) for a in held])

    far = chips // 2
    ring, back, swap = ring_perm(chips, 1), ring_perm(chips, -1), core_perm(chips)

    def hold(rows, *before):
        return lax.optimization_barrier((rows, before))[0]

    def send(rows, way):
        return lax.ppermute(rows, "ctx", way)

    def cross(rows):
        return lax.ppermute(rows, "ctx", swap)

    weights = [w_gate, w_up, w_down]
    weights += [cross(w) for w in weights]
    here, done = {}, {}
    first = []
    for half in range(HALVES):
        own, other = hold([routed[half], cross(routed[half])], *first)
        here[half, 0] = jnp.concatenate([own, other])
        first = [here[half, 0]]
        here[half, 1] = send(here[half, 0], ring)
    at_home, *weights = expert(jnp.concatenate(routed), chips, 0, 0, dense, weights, True)

    def work(half, step, *before):
        rows = hold(here[half, step], *before)
        done[half, step] = expert(rows, chips, step, half * cut, dense, weights, False)[0]

    for step in range(1, far):
        for half in range(HALVES):
            ready = at_home if step == 1 else done[half, step - 1]
            chunk = hold(here[half, step], ready)
            here[half, step + 1] = send(chunk if step + 1 < far else chunk[:cut], ring)
            if step + 1 < far:
                work(half, step)
    before = []
    for half in range(HALVES):
        for step in (far - 1, far):
            work(half, step, *before)
            before = [done[half, step]]

    moving = [send(done[half, far].astype(BF16), back).astype(F32) for half in range(HALVES)]
    if far > 1:
        moving = [jnp.concatenate([part, jnp.zeros_like(part)]) for part in moving]
    for step in range(far - 1, 0, -1):
        passed = []
        for half in range(HALVES):
            total = (done[half, step] + hold(moving[half], *passed)).astype(BF16)
            passed = [moving[half]]
            moving[half] = send(total, back).astype(F32)
    rows = []
    for half in range(HALVES):
        home = moving[half][:cut]
        if far > 1:
            home = home + cross(moving[half][cut:].astype(BF16)).astype(F32)
        here_rows = slice(half * cut, (half + 1) * cut)
        rows.append(mixed[here_rows] + (at_home[here_rows] + home))
    return jnp.concatenate(rows).astype(BF16)


def solution(mesh):
    rows = P(BOTH, None)
    expert_spec = P("ctx", None, None)
    return jax.shard_map(
        body,
        mesh=mesh,
        in_specs=(rows,) * 4 + (P(),) * 3 + (expert_spec,) * 3 + (rows,) * 2,
        out_specs=rows,
        check_vma=False,
    )
```

time: 104 us -> 99 us (0.952)
  waiting for transfers between devices: 42.7 us -> 36.5 us
  Pallas kernels: 24.6 us -> 29.6 us
  local copies, waits for them, and re-layouts: 3.68 us -> 0.18 us
    ppermute x16, waiting for transfers between devices: 25.6 us -> 19.6 us  [send(): return lax.ppermute(rows, 'ctx', way)]
    pallas_call x10, Pallas kernels: 17.6 us -> 22.7 us  [the longest x9 20.9 us: expert(): pl.pallas_call(functools.partial(expert_kernel, chips, step, first), out_...]
    unnamed x9 -> x1, local copies, waits for them, and re-layouts: 3.61 us -> 0.01 us
    ppermute x20 -> x7, starting transfers between devices: 4.59 us -> 1.54 us  [cross(): return lax.ppermute(rows, 'ctx', swap)]
    ppermute x16, starting transfers between devices: 14.1 us -> 16.7 us  [send(): return lax.ppermute(rows, 'ctx', way)]
    ppermute x20 -> x7, waiting for transfers between devices: 2.12 us -> 2.11 us  [cross(): return lax.ppermute(rows, 'ctx', swap)]
  transfers between devices with their start and end apart: 38 -> 25, of which waited for: 19 -> 14; matrix products, arithmetic and copies ran while one was open for 3% -> 3% of each run, Pallas kernels for 20% -> 28%
where the time goes in v3:
time: 99 us; the launch traced here: 98.6 us
  waiting for transfers between devices  36.5 us (37%)
  Pallas kernels  29.6 us (30%)
  starting transfers between devices  28.1 us (28%)
  other arithmetic  3.71 us (4%)
    pallas_call x9, Pallas kernels, expert(): pl.pallas_call(functools.partial(expert_kernel, chips, step, first), out_...  20.9 us
    ppermute x16, waiting for transfers between devices, send(): return lax.ppermute(rows, 'ctx', way)  19.6 us
    ppermute x16, starting transfers between devices, send(): return lax.ppermute(rows, 'ctx', way)  16.7 us
    all_to_all x1, waiting for transfers between devices, scan_states(): sums = lax.all_to_all(sums, BOTH, split_axis=0, concat_axis=0, tiled=True)  7.54 us
    all_to_all x1, starting transfers between devices, scan_states(): lax.all_to_all(pieces, BOTH, split_axis=0, concat_axis=0, tiled=True)  7.3 us
    all_to_all x1, waiting for transfers between devices, scan_states(): lax.all_to_all(pieces, BOTH, split_axis=0, concat_axis=0, tiled=True)  7.25 us
    pallas_call x1, Pallas kernels, attend_inside(): pl.pallas_call(functools.partial(inside_kernel, count), out_shape=outs, i...  4.13 us
    all_to_all x1, starting transfers between devices, scan_states(): sums = lax.all_to_all(sums, BOTH, split_axis=0, concat_axis=0, tiled=True)  2.59 us
  transfers between devices with their start and end apart: 25, of which 14 were waited for; matrix products, arithmetic and copies ran while one was open for 3% of the time, Pallas kernels for 28%

profile of v3, /device:TPU:0, one launch (start us, length us, event | category | flops | bytes accessed | tf_op | source)
XLA Modules:
  0.0 98.6 jit_solution(17322260860596448230)
XLA Ops:
  0.0 2.0 %shard_map.118.refs_6_ = bf16[1024,128]{1,0:T(8,128)(2,1)} custom-call(bf16[128,1024]{1,0:T(8,128)(2,1)} %refs_1_.2, bf16[128,1024]{1,0:T(8,128)(2,1)} %refs_2_.2), custom_call_target="tpu_custom_call" | custom-call | tf_op jit(solution)/shard_map/pallas_call | solution.py:266
  2.0 7.3 %all-to-all-start = ((bf16[32,32,128]{2,1,0:T(8,128)(2,1)}), bf16[32,32,128]{2,1,0:T(8,128)(2,1)S(1)}, u32[]{:S(2)}, u32[]{:S(2)}) async-start(bf16[32,32,128]{2,1,0:T(8,128)(2,1)} %bitcast), calls=%async_computation | async-start | bytes 524288 | tf_op jit(solution)/shard_map/all_to_all | solution.py:135
  9.3 0.3 collective-permute-start
  9.6 0.3 collective-permute-start.1
  9.9 0.3 collective-permute-start.2
  10.2 0.7 convert_reduce_fusion
  10.9 0.7 convert_divide_fusion
  11.6 0.7 select_reduce_fusion
  12.4 7.3 %all-to-all-done.pieces_ref = bf16[32,32,128]{2,1,0:T(8,128)(2,1)S(1)} async-done(((bf16[32,32,128]{2,1,0:T(8,128)(2,1)}), bf16[32,32,128]{2,1,0:T(8,128)(2,1)S(1)}, u32[]{:S(2)}, u32[]{:S(2)}) %all-to-all-start) | async-done | bytes 262176 | tf_op jit(solution)/shard_map/all_to_all | solution.py:135
  19.6 0.8 shard_map.119
  20.4 2.6 %all-to-all-start.1 = ((bf16[32,40,128]{2,1,0:T(8,128)(2,1)}), bf16[32,40,128]{2,1,0:T(8,128)(2,1)S(1)}, u32[]{:S(2)}, u32[]{:S(2)}) async-start(bf16[32,40,128]{2,1,0:T(8,128)(2,1)} %shard_map.119), calls=%async_computation.1 | async-start | bytes 655360 | tf_op jit(solution)/shard_map/all_to_all | solution.py:149
  23.0 4.1 %shard_map.120 = (bf16[128,1024]{1,0:T(8,128)(2,1)S(1)}, bf16[128,1024]{1,0:T(8,128)(2,1)}, bf16[128,1024]{1,0:T(8,128)(2,1)}, bf16[1024,1024]{1,0:T(8,128)(2,1)...) custom-call(bf16[128,1024]{1,0:T(8,128)(2,1)} %refs_0_.2, bf16[128,1024]{1,0:T(8,128)(2,1)} %refs_1_.2, ...), custom_call_target="tpu_custom_call" | custom-call | tf_op jit(solution)/shard_map/pallas_call | solution.py:102
  27.1 7.5 %all-to-all-done.1.sums_ref = bf16[32,40,128]{2,1,0:T(8,128)(2,1)S(1)} async-done(((bf16[32,40,128]{2,1,0:T(8,128)(2,1)}), bf16[32,40,128]{2,1,0:T(8,128)(2,1)S(1)}, u32[]{:S(2)}, u32[]{:S(2)}) %all-to-all-start.1) | async-done | bytes 327712 | tf_op jit(solution)/shard_map/all_to_all | solution.py:149
  34.7 1.8 %shard_map.121 = (f32[128,1024]{1,0:T(8,128)S(1)}, bf16[64,1024]{1,0:T(8,128)(2,1)S(1)}, bf16[64,1024]{1,0:T(8,128)(2,1)S(1)}) custom-call(bf16[32,40,128]{2,1,0:T(8,128)(2,1)S(1)} %all-to-all-done.1.sums_ref, bf16[128,1024]{1,0:T(8,128)(2,1)S(1)} %get-tuple-element.36.q_ref, bf16[1024,1024]{1,0:T(8,128)(2,1)S(1)} %get-tuple-element.37.proj_ref, ...), custom_call_target="tpu_custom_call" | custom-call | tf_op jit(solution)/shard_map/pallas_call | solution.py:287
  36.4 0.1 collective-permute-start.3
  36.5 0.5 collective-permute-start.13
  37.1 0.8 collective-permute-done.3
  37.9 1.1 %collective-permute-start.4 = (bf16[128,1024]{1,0:T(8,128)(2,1)S(1)}, bf16[128,1024]{1,0:T(8,128)(2,1)S(1)}, u32[]{:S(2)}, u32[]{:S(2)}) collective-permute-start(bf16[128,1024]{1,0:T(8,128)(2,1)S(1)} %constant_dynamic-update-slice_fusion), channel_id=1, source_target_pairs={{0,4},{1,3},{4,8},{5,1},{8,12},{9,5},{12,14},{13,9},{14,10},{15,13... | collective-permute-start | bytes 786440 | tf_op jit(solution)/shard_map/ppermute | solution.py:304
  39.0 0.5 collective-permute-start.14
  39.5 0.1 copy.29
  39.7 5.3 %shard_map.122 = (f32[128,1024]{1,0:T(8,128)S(1)}, bf16[1,1024,896]{2,1,0:T(8,128)(2,1)S(1)}, bf16[1,1024,896]{2,1,0:T(8,128)(2,1)S(1)}, bf16[1,896,1024]{2,1,0:...) custom-call(f32[128,32]{1,0:T(8,128)S(1)} %bitcast.24, ...), custom_call_target="tpu_custom_call" | custom-call | tf_op jit(solution)/shard_map/pallas_call | solution.py:235
  45.0 1.5 %collective-permute-start.5 = (bf16[128,1024]{1,0:T(8,128)(2,1)S(1)}, bf16[128,1024]{1,0:T(8,128)(2,1)S(1)}, u32[]{:S(2)}, u32[]{:S(2)}) collective-permute-start(bf16[128,1024]{1,0:T(8,128)(2,1)S(1)} %collective-permute-done.4.rows_ref), channel_id=1, source_target_pairs={{0,4},{1,3},{4,8},{5,1},{8,12},{9,5},{12,14},{13,9},{14,10},{15,13... | collective-permute-start | bytes 786440 | tf_op jit(solution)/shard_map/ppermute | solution.py:304
  46.6 0.6 collective-permute-done.14.rows_ref
  47.1 1.1 %collective-permute-start.15 = (bf16[128,1024]{1,0:T(8,128)(2,1)S(1)}, bf16[128,1024]{1,0:T(8,128)(2,1)S(1)}, u32[]{:S(2)}, u32[]{:S(2)}) collective-permute-start(bf16[128,1024]{1,0:T(8,128)(2,1)S(1)} %collective-permute-done.14.rows_ref), channel_id=1, source_target_pairs={{0,4},{1,3},{4,8},{5,1},{8,12},{9,5},{12,14},{13,9},{14,10},{15,13... | collective-permute-start | bytes 786440 | tf_op jit(solution)/shard_map/ppermute | solution.py:304
  48.2 1.9 %shard_map.123 = f32[128,1024]{1,0:T(8,128)S(1)} custom-call(f32[128,32]{1,0:T(8,128)S(1)} %bitcast.25, bf16[128,1024]{1,0:T(8,128)(2,1)S(1)} %collective-permute-done.4.rows_ref, bf16[1,1024,896]{2,1,0:T(8,128)(2,1)S(1)} %get-tuple-element.47.refs_0_, bf16[1,1024,896]{2,1,0:T(8,128)(2,1)S(1)} %get-tuple-element.48.refs_1_, ...), custom_call_target="tpu_custom_call" | custom-call | tf_op jit(solution)/shard_map/pallas_call | solution.py:235
  50.1 1.3 %collective-permute-done.5.rows_ref = bf16[128,1024]{1,0:T(8,128)(2,1)S(1)} collective-permute-done((bf16[128,1024]{1,0:T(8,128)(2,1)S(1)}, bf16[128,1024]{1,0:T(8,128)(2,1)S(1)}, u32[]{:S(2)}, u32[]{:S(2)}) %collective-permute-start.5) | collective-permute-done | bytes 262176 | tf_op jit(solution)/shard_map/ppermute | solution.py:304
  51.4 1.5 %collective-permute-start.6 = (bf16[128,1024]{1,0:T(8,128)(2,1)S(1)}, bf16[128,1024]{1,0:T(8,128)(2,1)S(1)}, u32[]{:S(2)}, u32[]{:S(2)}) collective-permute-start(bf16[128,1024]{1,0:T(8,128)(2,1)S(1)} %collective-permute-done.5.rows_ref), channel_id=1, source_target_pairs={{0,4},{1,3},{4,8},{5,1},{8,12},{9,5},{12,14},{13,9},{14,10},{15,13... | collective-permute-start | bytes 786440 | tf_op jit(solution)/shard_map/ppermute | solution.py:304
  52.9 1.9 %shard_map.127 = f32[128,1024]{1,0:T(8,128)S(1)} custom-call(f32[128,32]{1,0:T(8,128)S(1)} %bitcast.26, bf16[128,1024]{1,0:T(8,128)(2,1)S(1)} %collective-permute-done.14.rows_ref, bf16[1,1024,896]{2,1,0:T(8,128)(2,1)S(1)} %get-tuple-element.47.refs_0_, bf16[1,1024,896]{2,1,0:T(8,128)(2,1)S(1)} %get-tuple-element.48.refs_1_, ...), custom_call_target="tpu_custom_call" | custom-call | tf_op jit(solution)/shard_map/pallas_call | solution.py:235
  54.9 0.9 collective-permute-start.16
  55.7 1.9 %shard_map.124 = f32[128,1024]{1,0:T(8,128)S(1)} custom-call(f32[128,32]{1,0:T(8,128)S(1)} %bitcast.27, bf16[128,1024]{1,0:T(8,128)(2,1)S(1)} %collective-permute-done.5.rows_ref, bf16[1,1024,896]{2,1,0:T(8,128)(2,1)S(1)} %get-tuple-element.47.refs_0_, bf16[1,1024,896]{2,1,0:T(8,128)(2,1)S(1)} %get-tuple-element.48.refs_1_, ...), custom_call_target="tpu_custom_call" | custom-call | tf_op jit(solution)/shard_map/pallas_call | solution.py:235
  57.7 0.1 collective-permute-done.6.rows_ref
  57.8 1.7 %collective-permute-start.7 = (bf16[64,1024]{1,0:T(8,128)(2,1)S(1)}, bf16[64,1024]{1,0:T(8,128)(2,1)S(1)}, u32[]{:S(2)}, u32[]{:S(2)}) collective-permute-start(bf16[64,1024]{1,0:T(8,128)(2,1)S(1)} %slice.60), channel_id=1, source_target_pairs={{0,4},{1,3},{4,8},{5,1},{8,12},{9,5},{12,14},{13,9},{14,10},{15,13... | collective-permute-start | bytes 393224 | tf_op jit(solution)/shard_map/ppermute | solution.py:304
  59.6 1.9 %shard_map.128 = f32[128,1024]{1,0:T(8,128)S(1)} custom-call(f32[128,32]{1,0:T(8,128)S(1)} %bitcast.28, bf16[128,1024]{1,0:T(8,128)(2,1)S(1)} %collective-permute-done.15.rows_ref, bf16[1,1024,896]{2,1,0:T(8,128)(2,1)S(1)} %get-tuple-element.47.refs_0_, bf16[1,1024,896]{2,1,0:T(8,128)(2,1)S(1)} %get-tuple-element.48.refs_1_, ...), custom_call_target="tpu_custom_call" | custom-call | tf_op jit(solution)/shard_map/pallas_call | solution.py:235
  61.5 0.8 collective-permute-start.17
  62.3 1.9 %shard_map.125 = f32[128,1024]{1,0:T(8,128)S(1)} custom-call(f32[128,32]{1,0:T(8,128)S(1)} %bitcast.29, bf16[128,1024]{1,0:T(8,128)(2,1)S(1)} %collective-permute-done.6.rows_ref, bf16[1,1024,896]{2,1,0:T(8,128)(2,1)S(1)} %get-tuple-element.47.refs_0_, bf16[1,1024,896]{2,1,0:T(8,128)(2,1)S(1)} %get-tuple-element.48.refs_1_, ...), custom_call_target="tpu_custom_call" | custom-call | tf_op jit(solution)/shard_map/pallas_call | solution.py:235
  64.3 2.0 %shard_map.126 = f32[64,1024]{1,0:T(8,128)S(1)} custom-call(f32[128,32]{1,0:T(8,128)S(1)} %bitcast.30, bf16[64,1024]{1,0:T(8,128)(2,1)S(1)} %collective-permute-done.7.rows_ref, bf16[1,1024,896]{2,1,0:T(8,128)(2,1)S(1)} %get-tuple-element.47.refs_0_, bf16[1,1024,896]{2,1,0:T(8,128)(2,1)S(1)} %get-tuple-element.48.refs_1_, ...), custom_call_target="tpu_custom_call" | custom-call | tf_op jit(solution)/shard_map/pallas_call | solution.py:235
  66.3 1.3 %collective-permute-start.8 = (bf16[64,1024]{1,0:T(8,128)(2,1)S(1)}, bf16[64,1024]{1,0:T(8,128)(2,1)S(1)}, u32[]{:S(2)}, u32[]{:S(2)}) collective-permute-start(bf16[64,1024]{1,0:T(8,128)(2,1)S(1)} %convert_element_type.71), channel_id=1, source_target_pairs={{0,2},{1,5},{4,0},{5,9},{8,4},{9,13},{12,8},{13,15},{14,12},{15,11... | collective-permute-start | bytes 393224 | tf_op jit(solution)/shard_map/ppermute | solution.py:304
  67.6 1.9 %shard_map.129 = f32[128,1024]{1,0:T(8,128)S(1)} custom-call(f32[128,32]{1,0:T(8,128)S(1)} %bitcast.31, bf16[128,1024]{1,0:T(8,128)(2,1)S(1)} %collective-permute-done.16.rows_ref, bf16[1,1024,896]{2,1,0:T(8,128)(2,1)S(1)} %get-tuple-element.47.refs_0_, bf16[1,1024,896]{2,1,0:T(8,128)(2,1)S(1)} %get-tuple-element.48.refs_1_, ...), custom_call_target="tpu_custom_call" | custom-call | tf_op jit(solution)/shard_map/pallas_call | solution.py:235
  69.6 2.0 %shard_map.130 = f32[64,1024]{1,0:T(8,128)S(1)} custom-call(f32[128,32]{1,0:T(8,128)S(1)} %bitcast.32, bf16[64,1024]{1,0:T(8,128)(2,1)S(1)} %collective-permute-done.17.rows_ref, bf16[1,1024,896]{2,1,0:T(8,128)(2,1)S(1)} %get-tuple-element.47.refs_0_, bf16[1,1024,896]{2,1,0:T(8,128)(2,1)S(1)} %get-tuple-element.48.refs_1_, ...), custom_call_target="tpu_custom_call" | custom-call | tf_op jit(solution)/shard_map/pallas_call | solution.py:235
  71.6 0.7 collective-permute-start.18
  72.4 0.1 add_convert_fusion.5
  72.5 1.5 %collective-permute-start.9 = (bf16[128,1024]{1,0:T(8,128)(2,1)S(1)}, bf16[128,1024]{1,0:T(8,128)(2,1)S(1)}, u32[]{:S(2)}, u32[]{:S(2)}) collective-permute-start(bf16[128,1024]{1,0:T(8,128)(2,1)S(1)} %add_convert_fusion.5), channel_id=1, source_target_pairs={{0,2},{1,5},{4,0},{5,9},{8,4},{9,13},{12,8},{13,15},{14,12},{15,11... | collective-permute-start | bytes 786440 | tf_op jit(solution)/shard_map/ppermute | solution.py:304
  74.0 2.7 %collective-permute-done.18 = bf16[64,1024]{1,0:T(8,128)(2,1)S(1)} collective-permute-done((bf16[64,1024]{1,0:T(8,128)(2,1)S(1)}, bf16[64,1024]{1,0:T(8,128)(2,1)S(1)}, u32[]{:S(2)}, u32[]{:S(2)}) %collective-permute-start.18) | collective-permute-done | bytes 131104 | tf_op jit(solution)/shard_map/ppermute | solution.py:304
  76.7 0.1 add_convert_fusion.2
  76.8 0.7 collective-permute-start.19
  77.5 2.0 %collective-permute-done.9 = bf16[128,1024]{1,0:T(8,128)(2,1)S(1)} collective-permute-done((bf16[128,1024]{1,0:T(8,128)(2,1)S(1)}, bf16[128,1024]{1,0:T(8,128)(2,1)S(1)}, u32[]{:S(2)}, u32[]{:S(2)}) %collective-permute-start.9) | collective-permute-done | bytes 262176 | tf_op jit(solution)/shard_map/ppermute | solution.py:304
  79.5 0.1 add_convert_fusion.4
  79.6 0.9 collective-permute-start.10
  80.5 2.7 %collective-permute-done.19 = bf16[128,1024]{1,0:T(8,128)(2,1)S(1)} collective-permute-done((bf16[128,1024]{1,0:T(8,128)(2,1)S(1)}, bf16[128,1024]{1,0:T(8,128)(2,1)S(1)}, u32[]{:S(2)}, u32[]{:S(2)}) %collective-permute-start.19) | collective-permute-done | bytes 262176 | tf_op jit(solution)/shard_map/ppermute | solution.py:304
  83.2 0.1 add_convert_fusion.1
  83.3 0.7 collective-permute-start.20
  84.0 2.0 %collective-permute-done.10 = bf16[128,1024]{1,0:T(8,128)(2,1)S(1)} collective-permute-done((bf16[128,1024]{1,0:T(8,128)(2,1)S(1)}, bf16[128,1024]{1,0:T(8,128)(2,1)S(1)}, u32[]{:S(2)}, u32[]{:S(2)}) %collective-permute-start.10) | collective-permute-done | bytes 262176 | tf_op jit(solution)/shard_map/ppermute | solution.py:304
  86.1 0.1 add_convert_fusion.3
  86.1 0.9 collective-permute-start.11
  87.0 2.7 %collective-permute-done.20 = bf16[128,1024]{1,0:T(8,128)(2,1)S(1)} collective-permute-done((bf16[128,1024]{1,0:T(8,128)(2,1)S(1)}, bf16[128,1024]{1,0:T(8,128)(2,1)S(1)}, u32[]{:S(2)}, u32[]{:S(2)}) %collective-permute-start.20) | collective-permute-done | bytes 262176 | tf_op jit(solution)/shard_map/ppermute | solution.py:304
  89.8 0.1 add_convert_fusion
  89.8 0.7 collective-permute-start.21
  90.6 2.0 %collective-permute-done.11 = bf16[128,1024]{1,0:T(8,128)(2,1)S(1)} collective-permute-done((bf16[128,1024]{1,0:T(8,128)(2,1)S(1)}, bf16[128,1024]{1,0:T(8,128)(2,1)S(1)}, u32[]{:S(2)}, u32[]{:S(2)}) %collective-permute-start.11) | collective-permute-done | bytes 262176 | tf_op jit(solution)/shard_map/ppermute | solution.py:304
  92.6 0.1 collective-permute-start.12
  92.6 3.6 %collective-permute-done.21 = bf16[128,1024]{1,0:T(8,128)(2,1)S(1)} collective-permute-done((bf16[128,1024]{1,0:T(8,128)(2,1)S(1)}, bf16[128,1024]{1,0:T(8,128)(2,1)S(1)}, u32[]{:S(2)}, u32[]{:S(2)}) %collective-permute-start.21) | collective-permute-done | bytes 262176 | tf_op jit(solution)/shard_map/ppermute | solution.py:304
  96.3 0.1 collective-permute-start.22
  96.4 1.3 %collective-permute-done.22 = bf16[64,1024]{1,0:T(8,128)(2,1)S(1)} collective-permute-done((bf16[64,1024]{1,0:T(8,128)(2,1)S(1)}, bf16[64,1024]{1,0:T(8,128)(2,1)S(1)}, u32[]{:S(2)}, u32[]{:S(2)}) %collective-permute-start.22) | collective-permute-done | bytes 131104 | tf_op jit(solution)/shard_map/ppermute | solution.py:307
  97.7 0.1 add_convert_fusion.7
  97.8 0.7 pad_maximum_fusion.2
  (36 shorter events, 0.5 us)
Async XLA Ops:
  2.0 17.6 %all-to-all-start = ((bf16[32,32,128]{2,1,0:T(8,128)(2,1)}), bf16[32,32,128]{2,1,0:T(8,128)(2,1)S(1)}, u32[]{:S(2)}, u32[]{:S(2)}) async-start(bf16[32,32,128]{2,1,0:T(8,128)(2,1)} %bitcast), calls=%async_computation | async-start | bytes 524288 | tf_op jit(solution)/shard_map/all_to_all | solution.py:135
  9.3 30.3 %collective-permute-start = (bf16[1,1024,896]{2,1,0:T(8,128)(2,1)}, bf16[1,1024,896]{2,1,0:T(8,128)(2,1)}, u32[]{:S(2)}, u32[]{:S(2)}) collective-permute-start(bf16[1,1024,896]{2,1,0:T(8,128)(2,1)} %refs_0_.3), channel_id=1, source_target_pairs={{0,1},{1,0},{2,3},{3,2},{4,5},{5,4},{6,7},{7,6},{8,9},{9,8},{10,11... | collective-permute-start | bytes 5505032 | tf_op jit(solution)/shard_map/ppermute | solution.py:307
  9.6 30.0 %collective-permute-start.1 = (bf16[1,1024,896]{2,1,0:T(8,128)(2,1)}, bf16[1,1024,896]{2,1,0:T(8,128)(2,1)}, u32[]{:S(2)}, u32[]{:S(2)}) collective-permute-start(bf16[1,1024,896]{2,1,0:T(8,128)(2,1)} %refs_1_.3), channel_id=1, source_target_pairs={{0,1},{1,0},{2,3},{3,2},{4,5},{5,4},{6,7},{7,6},{8,9},{9,8},{10,11... | collective-permute-start | bytes 5505032 | tf_op jit(solution)/shard_map/ppermute | solution.py:307
  9.9 29.8 %collective-permute-start.2 = (bf16[1,896,1024]{2,1,0:T(8,128)(2,1)}, bf16[1,896,1024]{2,1,0:T(8,128)(2,1)}, u32[]{:S(2)}, u32[]{:S(2)}) collective-permute-start(bf16[1,896,1024]{2,1,0:T(8,128)(2,1)} %refs_2_.3), channel_id=1, source_target_pairs={{0,1},{1,0},{2,3},{3,2},{4,5},{5,4},{6,7},{7,6},{8,9},{9,8},{10,11... | collective-permute-start | bytes 5505032 | tf_op jit(solution)/shard_map/ppermute | solution.py:307
  20.4 14.3 %all-to-all-start.1 = ((bf16[32,40,128]{2,1,0:T(8,128)(2,1)}), bf16[32,40,128]{2,1,0:T(8,128)(2,1)S(1)}, u32[]{:S(2)}, u32[]{:S(2)}) async-start(bf16[32,40,128]{2,1,0:T(8,128)(2,1)} %shard_map.119), calls=%async_computation.1 | async-start | bytes 655360 | tf_op jit(solution)/shard_map/all_to_all | solution.py:149
  36.4 1.4 %collective-permute-start.3 = (bf16[64,1024]{1,0:T(8,128)(2,1)S(1)}, bf16[64,1024]{1,0:T(8,128)(2,1)S(1)}, u32[]{:S(2)}, u32[]{:S(2)}) collective-permute-start(bf16[64,1024]{1,0:T(8,128)(2,1)S(1)} %get-tuple-element.45), channel_id=1, source_target_pairs={{0,1},{1,0},{2,3},{3,2},{4,5},{5,4},{6,7},{7,6},{8,9},{9,8},{10,11... | collective-permute-start | bytes 393224 | tf_op jit(solution)/shard_map/ppermute | solution.py:307
  36.5 2.5 %collective-permute-start.13 = (bf16[64,1024]{1,0:T(8,128)(2,1)S(1)}, bf16[64,1024]{1,0:T(8,128)(2,1)S(1)}, u32[]{:S(2)}, u32[]{:S(2)}) collective-permute-start(bf16[64,1024]{1,0:T(8,128)(2,1)S(1)} %get-tuple-element.57), channel_id=1, source_target_pairs={{0,1},{1,0},{2,3},{3,2},{4,5},{5,4},{6,7},{7,6},{8,9},{9,8},{10,11... | collective-permute-start | bytes 393224 | tf_op jit(solution)/shard_map/ppermute | solution.py:307
  37.9 7.1 %collective-permute-start.4 = (bf16[128,1024]{1,0:T(8,128)(2,1)S(1)}, bf16[128,1024]{1,0:T(8,128)(2,1)S(1)}, u32[]{:S(2)}, u32[]{:S(2)}) collective-permute-start(bf16[128,1024]{1,0:T(8,128)(2,1)S(1)} %constant_dynamic-update-slice_fusion), channel_id=1, source_target_pairs={{0,4},{1,3},{4,8},{5,1},{8,12},{9,5},{12,14},{13,9},{14,10},{15,13... | collective-permute-start | bytes 786440 | tf_op jit(solution)/shard_map/ppermute | solution.py:304
  39.0 8.1 %collective-permute-start.14 = (bf16[128,1024]{1,0:T(8,128)(2,1)S(1)}, bf16[128,1024]{1,0:T(8,128)(2,1)S(1)}, u32[]{:S(2)}, u32[]{:S(2)}) collective-permute-start(bf16[128,1024]{1,0:T(8,128)(2,1)S(1)} %pad_maximum_fusion.1), channel_id=1, source_target_pairs={{0,4},{1,3},{4,8},{5,1},{8,12},{9,5},{12,14},{13,9},{14,10},{15,13... | collective-permute-start | bytes 786440 | tf_op jit(solution)/shard_map/ppermute | solution.py:304
  45.0 6.4 %collective-permute-start.5 = (bf16[128,1024]{1,0:T(8,128)(2,1)S(1)}, bf16[128,1024]{1,0:T(8,128)(2,1)S(1)}, u32[]{:S(2)}, u32[]{:S(2)}) collective-permute-start(bf16[128,1024]{1,0:T(8,128)(2,1)S(1)} %collective-permute-done.4.rows_ref), channel_id=1, source_target_pairs={{0,4},{1,3},{4,8},{5,1},{8,12},{9,5},{12,14},{13,9},{14,10},{15,13... | collective-permute-start | bytes 786440 | tf_op jit(solution)/shard_map/ppermute | solution.py:304
  47.1 7.8 %collective-permute-start.15 = (bf16[128,1024]{1,0:T(8,128)(2,1)S(1)}, bf16[128,1024]{1,0:T(8,128)(2,1)S(1)}, u32[]{:S(2)}, u32[]{:S(2)}) collective-permute-start(bf16[128,1024]{1,0:T(8,128)(2,1)S(1)} %collective-permute-done.14.rows_ref), channel_id=1, source_target_pairs={{0,4},{1,3},{4,8},{5,1},{8,12},{9,5},{12,14},{13,9},{14,10},{15,13... | collective-permute-start | bytes 786440 | tf_op jit(solution)/shard_map/ppermute | solution.py:304
  51.4 6.4 %collective-permute-start.6 = (bf16[128,1024]{1,0:T(8,128)(2,1)S(1)}, bf16[128,1024]{1,0:T(8,128)(2,1)S(1)}, u32[]{:S(2)}, u32[]{:S(2)}) collective-permute-start(bf16[128,1024]{1,0:T(8,128)(2,1)S(1)} %collective-permute-done.5.rows_ref), channel_id=1, source_target_pairs={{0,4},{1,3},{4,8},{5,1},{8,12},{9,5},{12,14},{13,9},{14,10},{15,13... | collective-permute-start | bytes 786440 | tf_op jit(solution)/shard_map/ppermute | solution.py:304
  54.9 6.6 %collective-permute-start.16 = (bf16[128,1024]{1,0:T(8,128)(2,1)S(1)}, bf16[128,1024]{1,0:T(8,128)(2,1)S(1)}, u32[]{:S(2)}, u32[]{:S(2)}) collective-permute-start(bf16[128,1024]{1,0:T(8,128)(2,1)S(1)} %collective-permute-done.15.rows_ref), channel_id=1, source_target_pairs={{0,4},{1,3},{4,8},{5,1},{8,12},{9,5},{12,14},{13,9},{14,10},{15,13... | collective-permute-start | bytes 786440 | tf_op jit(solution)/shard_map/ppermute | solution.py:304
  57.8 6.4 %collective-permute-start.7 = (bf16[64,1024]{1,0:T(8,128)(2,1)S(1)}, bf16[64,1024]{1,0:T(8,128)(2,1)S(1)}, u32[]{:S(2)}, u32[]{:S(2)}) collective-permute-start(bf16[64,1024]{1,0:T(8,128)(2,1)S(1)} %slice.60), channel_id=1, source_target_pairs={{0,4},{1,3},{4,8},{5,1},{8,12},{9,5},{12,14},{13,9},{14,10},{15,13... | collective-permute-start | bytes 393224 | tf_op jit(solution)/shard_map/ppermute | solution.py:304
  61.5 8.1 %collective-permute-start.17 = (bf16[64,1024]{1,0:T(8,128)(2,1)S(1)}, bf16[64,1024]{1,0:T(8,128)(2,1)S(1)}, u32[]{:S(2)}, u32[]{:S(2)}) collective-permute-start(bf16[64,1024]{1,0:T(8,128)(2,1)S(1)} %slice.66), channel_id=1, source_target_pairs={{0,4},{1,3},{4,8},{5,1},{8,12},{9,5},{12,14},{13,9},{14,10},{15,13... | collective-permute-start | bytes 393224 | tf_op jit(solution)/shard_map/ppermute | solution.py:304
  66.3 6.1 %collective-permute-start.8 = (bf16[64,1024]{1,0:T(8,128)(2,1)S(1)}, bf16[64,1024]{1,0:T(8,128)(2,1)S(1)}, u32[]{:S(2)}, u32[]{:S(2)}) collective-permute-start(bf16[64,1024]{1,0:T(8,128)(2,1)S(1)} %convert_element_type.71), channel_id=1, source_target_pairs={{0,2},{1,5},{4,0},{5,9},{8,4},{9,13},{12,8},{13,15},{14,12},{15,11... | collective-permute-start | bytes 393224 | tf_op jit(solution)/shard_map/ppermute | solution.py:304
  71.6 5.0 %collective-permute-start.18 = (bf16[64,1024]{1,0:T(8,128)(2,1)S(1)}, bf16[64,1024]{1,0:T(8,128)(2,1)S(1)}, u32[]{:S(2)}, u32[]{:S(2)}) collective-permute-start(bf16[64,1024]{1,0:T(8,128)(2,1)S(1)} %convert_element_type.78), channel_id=1, source_target_pairs={{0,2},{1,5},{4,0},{5,9},{8,4},{9,13},{12,8},{13,15},{14,12},{15,11... | collective-permute-start | bytes 393224 | tf_op jit(solution)/shard_map/ppermute | solution.py:304
  72.5 7.0 %collective-permute-start.9 = (bf16[128,1024]{1,0:T(8,128)(2,1)S(1)}, bf16[128,1024]{1,0:T(8,128)(2,1)S(1)}, u32[]{:S(2)}, u32[]{:S(2)}) collective-permute-start(bf16[128,1024]{1,0:T(8,128)(2,1)S(1)} %add_convert_fusion.5), channel_id=1, source_target_pairs={{0,2},{1,5},{4,0},{5,9},{8,4},{9,13},{12,8},{13,15},{14,12},{15,11... | collective-permute-start | bytes 786440 | tf_op jit(solution)/shard_map/ppermute | solution.py:304
  76.8 6.4 %collective-permute-start.19 = (bf16[128,1024]{1,0:T(8,128)(2,1)S(1)}, bf16[128,1024]{1,0:T(8,128)(2,1)S(1)}, u32[]{:S(2)}, u32[]{:S(2)}) collective-permute-start(bf16[128,1024]{1,0:T(8,128)(2,1)S(1)} %add_convert_fusion.2), channel_id=1, source_target_pairs={{0,2},{1,5},{4,0},{5,9},{8,4},{9,13},{12,8},{13,15},{14,12},{15,11... | collective-permute-start | bytes 786440 | tf_op jit(solution)/shard_map/ppermute | solution.py:304
  79.6 6.4 %collective-permute-start.10 = (bf16[128,1024]{1,0:T(8,128)(2,1)S(1)}, bf16[128,1024]{1,0:T(8,128)(2,1)S(1)}, u32[]{:S(2)}, u32[]{:S(2)}) collective-permute-start(bf16[128,1024]{1,0:T(8,128)(2,1)S(1)} %add_convert_fusion.4), channel_id=1, source_target_pairs={{0,2},{1,5},{4,0},{5,9},{8,4},{9,13},{12,8},{13,15},{14,12},{15,11... | collective-permute-start | bytes 786440 | tf_op jit(solution)/shard_map/ppermute | solution.py:304
  83.3 6.4 %collective-permute-start.20 = (bf16[128,1024]{1,0:T(8,128)(2,1)S(1)}, bf16[128,1024]{1,0:T(8,128)(2,1)S(1)}, u32[]{:S(2)}, u32[]{:S(2)}) collective-permute-start(bf16[128,1024]{1,0:T(8,128)(2,1)S(1)} %add_convert_fusion.1), channel_id=1, source_target_pairs={{0,2},{1,5},{4,0},{5,9},{8,4},{9,13},{12,8},{13,15},{14,12},{15,11... | collective-permute-start | bytes 786440 | tf_op jit(solution)/shard_map/ppermute | solution.py:304
  86.1 6.4 %collective-permute-start.11 = (bf16[128,1024]{1,0:T(8,128)(2,1)S(1)}, bf16[128,1024]{1,0:T(8,128)(2,1)S(1)}, u32[]{:S(2)}, u32[]{:S(2)}) collective-permute-start(bf16[128,1024]{1,0:T(8,128)(2,1)S(1)} %add_convert_fusion.3), channel_id=1, source_target_pairs={{0,2},{1,5},{4,0},{5,9},{8,4},{9,13},{12,8},{13,15},{14,12},{15,11... | collective-permute-start | bytes 786440 | tf_op jit(solution)/shard_map/ppermute | solution.py:304
  89.8 6.4 %collective-permute-start.21 = (bf16[128,1024]{1,0:T(8,128)(2,1)S(1)}, bf16[128,1024]{1,0:T(8,128)(2,1)S(1)}, u32[]{:S(2)}, u32[]{:S(2)}) collective-permute-start(bf16[128,1024]{1,0:T(8,128)(2,1)S(1)} %add_convert_fusion), channel_id=1, source_target_pairs={{0,2},{1,5},{4,0},{5,9},{8,4},{9,13},{12,8},{13,15},{14,12},{15,11... | collective-permute-start | bytes 786440 | tf_op jit(solution)/shard_map/ppermute | solution.py:304
  92.6 3.8 %collective-permute-start.12 = (bf16[64,1024]{1,0:T(8,128)(2,1)S(1)}, bf16[64,1024]{1,0:T(8,128)(2,1)S(1)}, u32[]{:S(2)}, u32[]{:S(2)}) collective-permute-start(bf16[64,1024]{1,0:T(8,128)(2,1)S(1)} %slice.76), channel_id=1, source_target_pairs={{0,1},{1,0},{2,3},{3,2},{4,5},{5,4},{6,7},{7,6},{8,9},{9,8},{10,11... | collective-permute-start | bytes 393224 | tf_op jit(solution)/shard_map/ppermute | solution.py:307
  96.3 1.4 %collective-permute-start.22 = (bf16[64,1024]{1,0:T(8,128)(2,1)S(1)}, bf16[64,1024]{1,0:T(8,128)(2,1)S(1)}, u32[]{:S(2)}, u32[]{:S(2)}) collective-permute-start(bf16[64,1024]{1,0:T(8,128)(2,1)S(1)} %slice.78), channel_id=1, source_target_pairs={{0,1},{1,0},{2,3},{3,2},{4,5},{5,4},{6,7},{7,6},{8,9},{9,8},{10,11... | collective-permute-start | bytes 393224 | tf_op jit(solution)/shard_map/ppermute | solution.py:307

commit v4 on v3

--- a/solution.py
+++ b/solution.py
@@ -9,7 +9,6 @@
 
 HEADS = 8
 HEAD = 128
-HALVES = 2
 BOTH = ("seg", "ctx")
 F32 = jnp.float32
 BF16 = jnp.bfloat16
@@ -166,7 +165,7 @@
 def route_kernel(
     share, sums_ref, q_ref, proj_ref, gain_ref, moe_gain_ref, inside_hbm, hidden_hbm, *refs
 ):
-    outs, (inside_ref, hidden_ref, sems) = refs[: 1 + HALVES], refs[1 + HALVES :]
+    mixed_ref, routed_ref, inside_ref, hidden_ref, sems = refs
     copies = copies_of([inside_hbm, hidden_hbm], [inside_ref, hidden_ref], sems)
     ntok, width = q_ref.shape
     slabs = HEAD // share
@@ -184,14 +183,11 @@
     mixed = hidden_ref[...].astype(F32) + jnp.dot(
         normed, proj_ref[...], preferred_element_type=F32
     )
-    outs[0][...] = mixed
-    routed = rms(mixed, moe_gain_ref[...]).astype(BF16)
-    cut = ntok // HALVES
-    for half in range(HALVES):
-        outs[1 + half][...] = routed[half * cut : (half + 1) * cut]
-
-
-def expert_kernel(chips, step, first, dense, rows_ref, *refs):
+    mixed_ref[...] = mixed
+    routed_ref[...] = rms(mixed, moe_gain_ref[...]).astype(BF16)
+
+
+def expert_kernel(chips, offset, flip, dense, rows_ref, *refs):
     weights, out_ref, refs = refs[:6], refs[6], refs[7:]
     copies = []
     if refs:
@@ -200,14 +196,12 @@
     me = lax.axis_index("ctx")
     core, chip = me % 2, me // 2
     place = jnp.where(chip % 2 == 0, chip // 2, chips - 1 - chip // 2)
-    spot = (place - (1 - 2 * core) * step + chips) % chips
+    spot = (place - (1 - 2 * core) * offset + chips) % chips
     chip = jnp.where(2 * spot < chips, 2 * spot, 2 * (chips - spot) - 1)
-    planes = [core] if step in (0, chips // 2) else [core, 1 - core]
-    count = rows_ref.shape[0]
-    cut = count // len(planes)
-    table = dense[pl.ds(first, cut), :]
+    source = chip * 2 + (1 - core if flip else core)
+    rows = rows_ref[...]
+    table = dense[...]
     lane = lax.broadcasted_iota(jnp.int32, table.shape, 1)
-    rows = rows_ref[...]
     total = jnp.zeros(rows.shape, F32)
     for which in range(2):
         w_gate, w_up, w_down = weights[3 * which : 3 * which + 3]
@@ -217,31 +211,25 @@
         upper = jnp.dot(rows, w_up[0], preferred_element_type=F32)
         inner = (gate / (1.0 + jnp.exp(-gate)) * upper).astype(BF16)
         result = jnp.dot(inner, w_down[0], preferred_element_type=F32)
-        scales = []
-        for plane in planes:
-            column = which * 2 * chips + chip * 2 + plane
-            picked = jnp.where(lane == column, table, 0.0)
-            scales.append(jnp.sum(picked, axis=1, keepdims=True))
-        total += result * jnp.concatenate(scales)
+        picked = jnp.where(lane == which * 2 * chips + source, table, 0.0)
+        total += result * jnp.sum(picked, axis=1, keepdims=True)
     out_ref[...] = total
 
 
-def expert(rows, chips, step, first, dense, weights, staging):
+def expert(rows, chips, offset, flip, dense, weights, staging=False):
     outs, specs, scratch = [jax.ShapeDtypeStruct(rows.shape, F32)], [VMEM] * 6, []
     if staging:
         outs += [pltpu.VMEM(w.shape, w.dtype) for w in weights]
         specs, scratch = [HBM] * 6, [pltpu.SemaphoreType.DMA((6,))]
         weights = [in_hbm(w) for w in weights]
     return pl.pallas_call(
-        functools.partial(expert_kernel, chips, step, first),
+        functools.partial(expert_kernel, chips, offset, flip),
         out_shape=outs,
         in_specs=[VMEM] * 2 + specs,
         out_specs=[VMEM] * len(outs),
         scratch_shapes=scratch,
         compiler_params=pltpu.CompilerParams(vmem_limit_bytes=LIMIT),
-        cost_estimate=pl.CostEstimate(
-            flops=0, bytes_accessed=0, transcendentals=0
-        ),
+        cost_estimate=pl.CostEstimate(flops=0, bytes_accessed=0, transcendentals=0),
     )(dense, rows, *weights)
 
 
@@ -282,13 +270,12 @@
     out = jax.ShapeDtypeStruct((ntok, width), F32)
     arrays = [queries, key_rows, values, out_proj, norm_gain[None, :], moe_gain[None, :]]
     queries, _, _, out_proj, norm_gain, moe_gain, inside = attend_inside(arrays, states)
-    cut = ntok // HALVES
     held = [inside, hidden_in]
-    mixed, *routed = pl.pallas_call(
+    mixed, routed = pl.pallas_call(
         functools.partial(route_kernel, share),
-        out_shape=[out] + [jax.ShapeDtypeStruct((cut, width), BF16)] * HALVES,
+        out_shape=[out, jax.ShapeDtypeStruct((ntok, width), BF16)],
         in_specs=[VMEM] * 5 + [HBM] * len(held),
-        out_specs=[VMEM] * (1 + HALVES),
+        out_specs=[VMEM] * 2,
         scratch_shapes=[pltpu.VMEM(a.shape, a.dtype) for a in held]
         + [pltpu.SemaphoreType.DMA((len(held),))],
         compiler_params=pltpu.CompilerParams(vmem_limit_bytes=LIMIT),
@@ -303,54 +290,40 @@
     def send(rows, way):
         return lax.ppermute(rows, "ctx", way)
 
-    def cross(rows):
-        return lax.ppermute(rows, "ctx", swap)
-
     weights = [w_gate, w_up, w_down]
-    weights += [cross(w) for w in weights]
-    here, done = {}, {}
-    first = []
-    for half in range(HALVES):
-        own, other = hold([routed[half], cross(routed[half])], *first)
-        here[half, 0] = jnp.concatenate([own, other])
-        first = [here[half, 0]]
-        here[half, 1] = send(here[half, 0], ring)
-    at_home, *weights = expert(jnp.concatenate(routed), chips, 0, 0, dense, weights, True)
-
-    def work(half, step, *before):
-        rows = hold(here[half, step], *before)
-        done[half, step] = expert(rows, chips, step, half * cut, dense, weights, False)[0]
-
+    weights += [send(w, swap) for w in weights]
+    here = [send(routed, ring), send(send(routed, swap), ring)]
+    at_home, *weights = expert(routed, chips, 0, 0, dense, weights, True)
+    done, ready = {}, [at_home, at_home]
     for step in range(1, far):
-        for half in range(HALVES):
-            ready = at_home if step == 1 else done[half, step - 1]
-            chunk = hold(here[half, step], ready)
-            here[half, step + 1] = send(chunk if step + 1 < far else chunk[:cut], ring)
-            if step + 1 < far:
-                work(half, step)
-    before = []
-    for half in range(HALVES):
-        for step in (far - 1, far):
-            work(half, step, *before)
-            before = [done[half, step]]
-
-    moving = [send(done[half, far].astype(BF16), back).astype(F32) for half in range(HALVES)]
+        passed = []
+        for chain in range(2):
+            rows = hold(here[chain], ready[chain], *passed)
+            passed = [rows]
+            if step + 1 < far or chain == 0:
+                here[chain] = send(rows, ring)
+            if step + 1 < far or chain:
+                (done[chain, step],) = expert(rows, chips, step, chain, dense, weights)
+                ready[chain] = done[chain, step]
+            else:
+                late = rows
+    (done[0, far],) = expert(hold(here[0], *ready), chips, far, 0, dense, weights)
     if far > 1:
-        moving = [jnp.concatenate([part, jnp.zeros_like(part)]) for part in moving]
-    for step in range(far - 1, 0, -1):
-        passed = []
-        for half in range(HALVES):
-            total = (done[half, step] + hold(moving[half], *passed)).astype(BF16)
-            passed = [moving[half]]
-            moving[half] = send(total, back).astype(F32)
-    rows = []
-    for half in range(HALVES):
-        home = moving[half][:cut]
-        if far > 1:
-            home = home + cross(moving[half][cut:].astype(BF16)).astype(F32)
-        here_rows = slice(half * cut, (half + 1) * cut)
-        rows.append(mixed[here_rows] + (at_home[here_rows] + home))
-    return jnp.concatenate(rows).astype(BF16)
+        late = hold(late, done[0, far])
+        (done[0, far - 1],) = expert(late, chips, far - 1, 0, dense, weights)
+
+    moving = [None, None]
+    for step in range(far, 0, -1):
+        for chain in range(2):
+            if (chain, step) in done:
+                total = done[chain, step]
+                if moving[chain] is not None:
+                    total = total + moving[chain]
+                moving[chain] = send(total.astype(BF16), back).astype(F32)
+    home = mixed + at_home
+    if far > 1:
+        home = home + send(moving[1].astype(BF16), swap).astype(F32)
+    return (home + moving[0]).astype(BF16)
 
 
 def solution(mesh):

time: 99 us -> 93 us (0.939)
  waiting for transfers between devices: 36.5 us -> 33.9 us
  Pallas kernels: 29.6 us -> 27.4 us
    pallas_call x10 -> x9, Pallas kernels: 22.7 us -> 20.5 us  [the longest x8 18.7 us: expert(): pl.pallas_call(functools.partial(expert_kernel, chips, offset, flip), out...]
    ppermute x7 -> x0, waiting for transfers between devices: 2.11 us -> none  [cross(): return lax.ppermute(rows, 'ctx', swap)]
    ppermute x7 -> x0, starting transfers between devices: 1.54 us -> none  [cross(): return lax.ppermute(rows, 'ctx', swap)]
    ppermute x16 -> x19, starting transfers between devices: 16.7 us -> 17.7 us  [send(): return lax.ppermute(rows, 'ctx', way)]
    ppermute x16 -> x19, waiting for transfers between devices: 19.6 us -> 19.1 us  [send(): return lax.ppermute(rows, 'ctx', way)]
  transfers between devices with their start and end apart: 25 -> 21, of which waited for: 14 -> 16; matrix products, arithmetic and copies ran while one was open for 3% -> 3% of each run, Pallas kernels for 28% -> 27%
where the time goes in v4:
time: 93 us; the launch traced here: 92.6 us
  waiting for transfers between devices  33.9 us (36%)
  starting transfers between devices  27.6 us (30%)
  Pallas kernels  27.4 us (29%)
  other arithmetic  3.36 us (4%)
    ppermute x19, waiting for transfers between devices, send(): return lax.ppermute(rows, 'ctx', way)  19.1 us
    pallas_call x8, Pallas kernels, expert(): pl.pallas_call(functools.partial(expert_kernel, chips, offset, flip), out...  18.7 us
    ppermute x19, starting transfers between devices, send(): return lax.ppermute(rows, 'ctx', way)  17.7 us
    all_to_all x1, waiting for transfers between devices, scan_states(): sums = lax.all_to_all(sums, BOTH, split_axis=0, concat_axis=0, tiled=True)  7.56 us
    all_to_all x1, starting transfers between devices, scan_states(): lax.all_to_all(pieces, BOTH, split_axis=0, concat_axis=0, tiled=True)  7.3 us
    all_to_all x1, waiting for transfers between devices, scan_states(): lax.all_to_all(pieces, BOTH, split_axis=0, concat_axis=0, tiled=True)  7.25 us
    pallas_call x1, Pallas kernels, attend_inside(): pl.pallas_call(functools.partial(inside_kernel, count), out_shape=outs, i...  4.11 us
    all_to_all x1, starting transfers between devices, scan_states(): sums = lax.all_to_all(sums, BOTH, split_axis=0, concat_axis=0, tiled=True)  2.59 us
  transfers between devices with their start and end apart: 21, of which 16 were waited for; matrix products, arithmetic and copies ran while one was open for 3% of the time, Pallas kernels for 27%

profile of v4, /device:TPU:0, one launch (start us, length us, event | category | flops | bytes accessed | tf_op | source)
XLA Modules:
  0.0 92.6 jit_solution(8007058609389786001)
XLA Ops:
  0.0 2.0 %shard_map.118.refs_6_ = bf16[1024,128]{1,0:T(8,128)(2,1)} custom-call(bf16[128,1024]{1,0:T(8,128)(2,1)} %refs_1_.2, bf16[128,1024]{1,0:T(8,128)(2,1)} %refs_2_.2), custom_call_target="tpu_custom_call" | custom-call | tf_op jit(solution)/shard_map/pallas_call | solution.py:254
  2.0 7.3 %all-to-all-start = ((bf16[32,32,128]{2,1,0:T(8,128)(2,1)}), bf16[32,32,128]{2,1,0:T(8,128)(2,1)S(1)}, u32[]{:S(2)}, u32[]{:S(2)}) async-start(bf16[32,32,128]{2,1,0:T(8,128)(2,1)} %bitcast), calls=%async_computation | async-start | bytes 524288 | tf_op jit(solution)/shard_map/all_to_all | solution.py:134
  9.3 0.3 collective-permute-start
  9.6 0.3 collective-permute-start.1
  9.9 0.3 collective-permute-start.2
  10.2 0.7 convert_reduce_fusion
  10.9 0.7 convert_divide_fusion
  11.6 0.7 select_reduce_fusion
  12.4 7.3 %all-to-all-done.pieces_ref = bf16[32,32,128]{2,1,0:T(8,128)(2,1)S(1)} async-done(((bf16[32,32,128]{2,1,0:T(8,128)(2,1)}), bf16[32,32,128]{2,1,0:T(8,128)(2,1)S(1)}, u32[]{:S(2)}, u32[]{:S(2)}) %all-to-all-start) | async-done | bytes 262176 | tf_op jit(solution)/shard_map/all_to_all | solution.py:134
  19.6 0.8 shard_map.119
  20.4 2.6 %all-to-all-start.1 = ((bf16[32,40,128]{2,1,0:T(8,128)(2,1)}), bf16[32,40,128]{2,1,0:T(8,128)(2,1)S(1)}, u32[]{:S(2)}, u32[]{:S(2)}) async-start(bf16[32,40,128]{2,1,0:T(8,128)(2,1)} %shard_map.119), calls=%async_computation.1 | async-start | bytes 655360 | tf_op jit(solution)/shard_map/all_to_all | solution.py:148
  23.0 4.1 %shard_map.120 = (bf16[128,1024]{1,0:T(8,128)(2,1)S(1)}, bf16[128,1024]{1,0:T(8,128)(2,1)}, bf16[128,1024]{1,0:T(8,128)(2,1)}, bf16[1024,1024]{1,0:T(8,128)(2,1)...) custom-call(bf16[128,1024]{1,0:T(8,128)(2,1)} %refs_0_.2, bf16[128,1024]{1,0:T(8,128)(2,1)} %refs_1_.2, ...), custom_call_target="tpu_custom_call" | custom-call | tf_op jit(solution)/shard_map/pallas_call | solution.py:101
  27.1 7.6 %all-to-all-done.1.sums_ref = bf16[32,40,128]{2,1,0:T(8,128)(2,1)S(1)} async-done(((bf16[32,40,128]{2,1,0:T(8,128)(2,1)}), bf16[32,40,128]{2,1,0:T(8,128)(2,1)S(1)}, u32[]{:S(2)}, u32[]{:S(2)}) %all-to-all-start.1) | async-done | bytes 327712 | tf_op jit(solution)/shard_map/all_to_all | solution.py:148
  34.7 1.8 %shard_map.121 = (f32[128,1024]{1,0:T(8,128)S(1)}, bf16[128,1024]{1,0:T(8,128)(2,1)S(1)}) custom-call(bf16[32,40,128]{2,1,0:T(8,128)(2,1)S(1)} %all-to-all-done.1.sums_ref, bf16[128,1024]{1,0:T(8,128)(2,1)S(1)} %get-tuple-element.27.q_ref, bf16[1024,1024]{1,0:T(8,128)(2,1)S(1)} %get-tuple-element.28.proj_ref, f32[1,1024]{1,0:T(1,128)S(1)} %get-tuple-element.29.gain_ref, ...), custom_call_target="tpu_custom_call" | custom-call | tf_op jit(solution)/shard_map/pallas_call | solution.py:274
  36.4 0.1 collective-permute-start.3
  36.5 1.1 %collective-permute-start.5 = (bf16[128,1024]{1,0:T(8,128)(2,1)S(1)}, bf16[128,1024]{1,0:T(8,128)(2,1)S(1)}, u32[]{:S(2)}, u32[]{:S(2)}) collective-permute-start(bf16[128,1024]{1,0:T(8,128)(2,1)S(1)} %get-tuple-element.33.rows_ref), channel_id=1, source_target_pairs={{0,4},{1,3},{4,8},{5,1},{8,12},{9,5},{12,14},{13,9},{14,10},{15,13... | collective-permute-start | bytes 786440 | tf_op jit(solution)/shard_map/ppermute | solution.py:291
  37.7 0.4 collective-permute-done.3
  38.0 1.1 %collective-permute-start.4 = (bf16[128,1024]{1,0:T(8,128)(2,1)S(1)}, bf16[128,1024]{1,0:T(8,128)(2,1)S(1)}, u32[]{:S(2)}, u32[]{:S(2)}) collective-permute-start(bf16[128,1024]{1,0:T(8,128)(2,1)S(1)} %collective-permute-done.3), channel_id=1, source_target_pairs={{0,4},{1,3},{4,8},{5,1},{8,12},{9,5},{12,14},{13,9},{14,10},{15,13... | collective-permute-start | bytes 786440 | tf_op jit(solution)/shard_map/ppermute | solution.py:291
  39.1 0.1 copy.29
  39.2 0.0 collective-permute-done.refs_3_
  39.2 0.0 collective-permute-done.1.refs_4_
  39.3 0.0 collective-permute-done.2.refs_5_
  39.3 5.3 %shard_map.122 = (f32[128,1024]{1,0:T(8,128)S(1)}, bf16[1,1024,896]{2,1,0:T(8,128)(2,1)S(1)}, bf16[1,1024,896]{2,1,0:T(8,128)(2,1)S(1)}, bf16[1,896,1024]{2,1,0:...) custom-call(f32[128,32]{1,0:T(8,128)S(1)} %bitcast.24, ...), custom_call_target="tpu_custom_call" | custom-call | tf_op jit(solution)/shard_map/pallas_call | solution.py:225
  44.6 0.0 collective-permute-done.5.rows_ref
  44.6 0.6 collective-permute-start.7
  45.2 0.5 collective-permute-done.4.rows_ref
  45.8 1.1 %collective-permute-start.6 = (bf16[128,1024]{1,0:T(8,128)(2,1)S(1)}, bf16[128,1024]{1,0:T(8,128)(2,1)S(1)}, u32[]{:S(2)}, u32[]{:S(2)}) collective-permute-start(bf16[128,1024]{1,0:T(8,128)(2,1)S(1)} %collective-permute-done.4.rows_ref), channel_id=1, source_target_pairs={{0,4},{1,3},{4,8},{5,1},{8,12},{9,5},{12,14},{13,9},{14,10},{15,13... | collective-permute-start | bytes 786440 | tf_op jit(solution)/shard_map/ppermute | solution.py:291
  46.8 1.9 %shard_map.124 = f32[128,1024]{1,0:T(8,128)S(1)} custom-call(f32[128,32]{1,0:T(8,128)S(1)} %bitcast.25, bf16[128,1024]{1,0:T(8,128)(2,1)S(1)} %collective-permute-done.5.rows_ref, bf16[1,1024,896]{2,1,0:T(8,128)(2,1)S(1)} %get-tuple-element.37.refs_0_, bf16[1,1024,896]{2,1,0:T(8,128)(2,1)S(1)} %get-tuple-element.38.refs_1_, ...), custom_call_target="tpu_custom_call" | custom-call | tf_op jit(solution)/shard_map/pallas_call | solution.py:225
  48.7 2.3 %collective-permute-done.7.rows_ref = bf16[128,1024]{1,0:T(8,128)(2,1)S(1)} collective-permute-done((bf16[128,1024]{1,0:T(8,128)(2,1)S(1)}, bf16[128,1024]{1,0:T(8,128)(2,1)S(1)}, u32[]{:S(2)}, u32[]{:S(2)}) %collective-permute-start.7) | collective-permute-done | bytes 262176 | tf_op jit(solution)/shard_map/ppermute | solution.py:291
  51.0 0.6 collective-permute-start.9
  51.6 1.9 %shard_map.123 = f32[128,1024]{1,0:T(8,128)S(1)} custom-call(f32[128,32]{1,0:T(8,128)S(1)} %bitcast.26, bf16[128,1024]{1,0:T(8,128)(2,1)S(1)} %collective-permute-done.4.rows_ref, bf16[1,1024,896]{2,1,0:T(8,128)(2,1)S(1)} %get-tuple-element.37.refs_0_, bf16[1,1024,896]{2,1,0:T(8,128)(2,1)S(1)} %get-tuple-element.38.refs_1_, ...), custom_call_target="tpu_custom_call" | custom-call | tf_op jit(solution)/shard_map/pallas_call | solution.py:225
  53.5 0.3 collective-permute-done.6.rows_ref
  53.8 1.1 %collective-permute-start.8 = (bf16[128,1024]{1,0:T(8,128)(2,1)S(1)}, bf16[128,1024]{1,0:T(8,128)(2,1)S(1)}, u32[]{:S(2)}, u32[]{:S(2)}) collective-permute-start(bf16[128,1024]{1,0:T(8,128)(2,1)S(1)} %collective-permute-done.6.rows_ref), channel_id=1, source_target_pairs={{0,4},{1,3},{4,8},{5,1},{8,12},{9,5},{12,14},{13,9},{14,10},{15,13... | collective-permute-start | bytes 786440 | tf_op jit(solution)/shard_map/ppermute | solution.py:291
  54.9 1.9 %shard_map.126 = f32[128,1024]{1,0:T(8,128)S(1)} custom-call(f32[128,32]{1,0:T(8,128)S(1)} %bitcast.27, bf16[128,1024]{1,0:T(8,128)(2,1)S(1)} %collective-permute-done.7.rows_ref, bf16[1,1024,896]{2,1,0:T(8,128)(2,1)S(1)} %get-tuple-element.37.refs_0_, bf16[1,1024,896]{2,1,0:T(8,128)(2,1)S(1)} %get-tuple-element.38.refs_1_, ...), custom_call_target="tpu_custom_call" | custom-call | tf_op jit(solution)/shard_map/pallas_call | solution.py:225
  56.9 0.5 collective-permute-done.9.rows_ref
  57.4 0.6 collective-permute-start.14
  58.0 1.9 %shard_map.125 = f32[128,1024]{1,0:T(8,128)S(1)} custom-call(f32[128,32]{1,0:T(8,128)S(1)} %bitcast.28, bf16[128,1024]{1,0:T(8,128)(2,1)S(1)} %collective-permute-done.6.rows_ref, bf16[1,1024,896]{2,1,0:T(8,128)(2,1)S(1)} %get-tuple-element.37.refs_0_, bf16[1,1024,896]{2,1,0:T(8,128)(2,1)S(1)} %get-tuple-element.38.refs_1_, ...), custom_call_target="tpu_custom_call" | custom-call | tf_op jit(solution)/shard_map/pallas_call | solution.py:225
  59.9 0.3 collective-permute-done.8.rows_ref
  60.2 1.9 %shard_map.127 = f32[128,1024]{1,0:T(8,128)S(1)} custom-call(f32[128,32]{1,0:T(8,128)S(1)} %bitcast.29, bf16[128,1024]{1,0:T(8,128)(2,1)S(1)} %collective-permute-done.8.rows_ref, bf16[1,1024,896]{2,1,0:T(8,128)(2,1)S(1)} %get-tuple-element.37.refs_0_, bf16[1,1024,896]{2,1,0:T(8,128)(2,1)S(1)} %get-tuple-element.38.refs_1_, ...), custom_call_target="tpu_custom_call" | custom-call | tf_op jit(solution)/shard_map/pallas_call | solution.py:225
  62.1 1.3 %collective-permute-start.10 = (bf16[128,1024]{1,0:T(8,128)(2,1)S(1)}, bf16[128,1024]{1,0:T(8,128)(2,1)S(1)}, u32[]{:S(2)}, u32[]{:S(2)}) collective-permute-start(bf16[128,1024]{1,0:T(8,128)(2,1)S(1)} %convert_element_type.69), channel_id=1, source_target_pairs={{0,2},{1,5},{4,0},{5,9},{8,4},{9,13},{12,8},{13,15},{14,12},{15,11... | collective-permute-start | bytes 786440 | tf_op jit(solution)/shard_map/ppermute | solution.py:291
  63.4 0.5 collective-permute-done.14.rows_ref
  63.9 1.9 %shard_map.128 = f32[128,1024]{1,0:T(8,128)S(1)} custom-call(f32[128,32]{1,0:T(8,128)S(1)} %bitcast.30, bf16[128,1024]{1,0:T(8,128)(2,1)S(1)} %collective-permute-done.14.rows_ref, bf16[1,1024,896]{2,1,0:T(8,128)(2,1)S(1)} %get-tuple-element.37.refs_0_, bf16[1,1024,896]{2,1,0:T(8,128)(2,1)S(1)} %get-tuple-element.38.refs_1_, ...), custom_call_target="tpu_custom_call" | custom-call | tf_op jit(solution)/shard_map/pallas_call | solution.py:225
  65.9 1.6 %collective-permute-start.15 = (bf16[128,1024]{1,0:T(8,128)(2,1)S(1)}, bf16[128,1024]{1,0:T(8,128)(2,1)S(1)}, u32[]{:S(2)}, u32[]{:S(2)}) collective-permute-start(bf16[128,1024]{1,0:T(8,128)(2,1)S(1)} %convert_element_type.75), channel_id=1, source_target_pairs={{0,2},{1,5},{4,0},{5,9},{8,4},{9,13},{12,8},{13,15},{14,12},{15,11... | collective-permute-start | bytes 786440 | tf_op jit(solution)/shard_map/ppermute | solution.py:291
  67.5 1.0 %collective-permute-done.10 = bf16[128,1024]{1,0:T(8,128)(2,1)S(1)} collective-permute-done((bf16[128,1024]{1,0:T(8,128)(2,1)S(1)}, bf16[128,1024]{1,0:T(8,128)(2,1)S(1)}, u32[]{:S(2)}, u32[]{:S(2)}) %collective-permute-start.10) | collective-permute-done | bytes 262176 | tf_op jit(solution)/shard_map/ppermute | solution.py:291
  68.6 0.1 add_convert_fusion.5
  68.6 1.3 %collective-permute-start.11 = (bf16[128,1024]{1,0:T(8,128)(2,1)S(1)}, bf16[128,1024]{1,0:T(8,128)(2,1)S(1)}, u32[]{:S(2)}, u32[]{:S(2)}) collective-permute-start(bf16[128,1024]{1,0:T(8,128)(2,1)S(1)} %add_convert_fusion.5), channel_id=1, source_target_pairs={{0,2},{1,5},{4,0},{5,9},{8,4},{9,13},{12,8},{13,15},{14,12},{15,11... | collective-permute-start | bytes 786440 | tf_op jit(solution)/shard_map/ppermute | solution.py:291
  69.9 1.9 %shard_map.129 = f32[128,1024]{1,0:T(8,128)S(1)} custom-call(f32[128,32]{1,0:T(8,128)S(1)} %bitcast.31, bf16[128,1024]{1,0:T(8,128)(2,1)S(1)} %collective-permute-done.9.rows_ref, bf16[1,1024,896]{2,1,0:T(8,128)(2,1)S(1)} %get-tuple-element.37.refs_0_, bf16[1,1024,896]{2,1,0:T(8,128)(2,1)S(1)} %get-tuple-element.38.refs_1_, ...), custom_call_target="tpu_custom_call" | custom-call | tf_op jit(solution)/shard_map/pallas_call | solution.py:225
  71.8 0.5 collective-permute-done.15
  72.3 0.1 add_convert_fusion.3
  72.4 1.6 %collective-permute-start.16 = (bf16[128,1024]{1,0:T(8,128)(2,1)S(1)}, bf16[128,1024]{1,0:T(8,128)(2,1)S(1)}, u32[]{:S(2)}, u32[]{:S(2)}) collective-permute-start(bf16[128,1024]{1,0:T(8,128)(2,1)S(1)} %add_convert_fusion.3), channel_id=1, source_target_pairs={{0,2},{1,5},{4,0},{5,9},{8,4},{9,13},{12,8},{13,15},{14,12},{15,11... | collective-permute-start | bytes 786440 | tf_op jit(solution)/shard_map/ppermute | solution.py:291
  74.0 1.1 %collective-permute-done.11 = bf16[128,1024]{1,0:T(8,128)(2,1)S(1)} collective-permute-done((bf16[128,1024]{1,0:T(8,128)(2,1)S(1)}, bf16[128,1024]{1,0:T(8,128)(2,1)S(1)}, u32[]{:S(2)}, u32[]{:S(2)}) %collective-permute-start.11) | collective-permute-done | bytes 262176 | tf_op jit(solution)/shard_map/ppermute | solution.py:291
  75.1 0.1 add_convert_fusion.4
  75.2 1.6 %collective-permute-start.12 = (bf16[128,1024]{1,0:T(8,128)(2,1)S(1)}, bf16[128,1024]{1,0:T(8,128)(2,1)S(1)}, u32[]{:S(2)}, u32[]{:S(2)}) collective-permute-start(bf16[128,1024]{1,0:T(8,128)(2,1)S(1)} %add_convert_fusion.4), channel_id=1, source_target_pairs={{0,2},{1,5},{4,0},{5,9},{8,4},{9,13},{12,8},{13,15},{14,12},{15,11... | collective-permute-start | bytes 786440 | tf_op jit(solution)/shard_map/ppermute | solution.py:291
  76.8 2.0 %collective-permute-done.16 = bf16[128,1024]{1,0:T(8,128)(2,1)S(1)} collective-permute-done((bf16[128,1024]{1,0:T(8,128)(2,1)S(1)}, bf16[128,1024]{1,0:T(8,128)(2,1)S(1)}, u32[]{:S(2)}, u32[]{:S(2)}) %collective-permute-start.16) | collective-permute-done | bytes 262176 | tf_op jit(solution)/shard_map/ppermute | solution.py:291
  78.8 0.1 add_convert_fusion.2
  78.9 1.6 %collective-permute-start.17 = (bf16[128,1024]{1,0:T(8,128)(2,1)S(1)}, bf16[128,1024]{1,0:T(8,128)(2,1)S(1)}, u32[]{:S(2)}, u32[]{:S(2)}) collective-permute-start(bf16[128,1024]{1,0:T(8,128)(2,1)S(1)} %add_convert_fusion.2), channel_id=1, source_target_pairs={{0,2},{1,5},{4,0},{5,9},{8,4},{9,13},{12,8},{13,15},{14,12},{15,11... | collective-permute-start | bytes 786440 | tf_op jit(solution)/shard_map/ppermute | solution.py:291
  80.5 1.1 %collective-permute-done.12 = bf16[128,1024]{1,0:T(8,128)(2,1)S(1)} collective-permute-done((bf16[128,1024]{1,0:T(8,128)(2,1)S(1)}, bf16[128,1024]{1,0:T(8,128)(2,1)S(1)}, u32[]{:S(2)}, u32[]{:S(2)}) %collective-permute-start.12) | collective-permute-done | bytes 262176 | tf_op jit(solution)/shard_map/ppermute | solution.py:291
  81.6 0.0 collective-permute-start.13
  81.6 3.7 %collective-permute-done.17 = bf16[128,1024]{1,0:T(8,128)(2,1)S(1)} collective-permute-done((bf16[128,1024]{1,0:T(8,128)(2,1)S(1)}, bf16[128,1024]{1,0:T(8,128)(2,1)S(1)}, u32[]{:S(2)}, u32[]{:S(2)}) %collective-permute-start.17) | collective-permute-done | bytes 262176 | tf_op jit(solution)/shard_map/ppermute | solution.py:291
  85.3 0.1 add_convert_fusion.1
  85.4 1.6 %collective-permute-start.18 = (bf16[128,1024]{1,0:T(8,128)(2,1)S(1)}, bf16[128,1024]{1,0:T(8,128)(2,1)S(1)}, u32[]{:S(2)}, u32[]{:S(2)}) collective-permute-start(bf16[128,1024]{1,0:T(8,128)(2,1)S(1)} %add_convert_fusion.1), channel_id=1, source_target_pairs={{0,2},{1,5},{4,0},{5,9},{8,4},{9,13},{12,8},{13,15},{14,12},{15,11... | collective-permute-start | bytes 786440 | tf_op jit(solution)/shard_map/ppermute | solution.py:291
  87.0 0.0 collective-permute-done.13
  87.0 4.8 %collective-permute-done.18 = bf16[128,1024]{1,0:T(8,128)(2,1)S(1)} collective-permute-done((bf16[128,1024]{1,0:T(8,128)(2,1)S(1)}, bf16[128,1024]{1,0:T(8,128)(2,1)S(1)}, u32[]{:S(2)}, u32[]{:S(2)}) %collective-permute-start.18) | collective-permute-done | bytes 262176 | tf_op jit(solution)/shard_map/ppermute | solution.py:291
  91.8 0.8 add_convert_fusion
  (11 shorter events, 0.2 us)
Async XLA Ops:
  2.0 17.6 %all-to-all-start = ((bf16[32,32,128]{2,1,0:T(8,128)(2,1)}), bf16[32,32,128]{2,1,0:T(8,128)(2,1)S(1)}, u32[]{:S(2)}, u32[]{:S(2)}) async-start(bf16[32,32,128]{2,1,0:T(8,128)(2,1)} %bitcast), calls=%async_computation | async-start | bytes 524288 | tf_op jit(solution)/shard_map/all_to_all | solution.py:134
  9.3 29.9 %collective-permute-start = (bf16[1,1024,896]{2,1,0:T(8,128)(2,1)}, bf16[1,1024,896]{2,1,0:T(8,128)(2,1)}, u32[]{:S(2)}, u32[]{:S(2)}) collective-permute-start(bf16[1,1024,896]{2,1,0:T(8,128)(2,1)} %refs_0_.3), channel_id=1, source_target_pairs={{0,1},{1,0},{2,3},{3,2},{4,5},{5,4},{6,7},{7,6},{8,9},{9,8},{10,11... | collective-permute-start | bytes 5505032 | tf_op jit(solution)/shard_map/ppermute | solution.py:291
  9.6 29.6 %collective-permute-start.1 = (bf16[1,1024,896]{2,1,0:T(8,128)(2,1)}, bf16[1,1024,896]{2,1,0:T(8,128)(2,1)}, u32[]{:S(2)}, u32[]{:S(2)}) collective-permute-start(bf16[1,1024,896]{2,1,0:T(8,128)(2,1)} %refs_1_.3), channel_id=1, source_target_pairs={{0,1},{1,0},{2,3},{3,2},{4,5},{5,4},{6,7},{7,6},{8,9},{9,8},{10,11... | collective-permute-start | bytes 5505032 | tf_op jit(solution)/shard_map/ppermute | solution.py:291
  9.9 29.4 %collective-permute-start.2 = (bf16[1,896,1024]{2,1,0:T(8,128)(2,1)}, bf16[1,896,1024]{2,1,0:T(8,128)(2,1)}, u32[]{:S(2)}, u32[]{:S(2)}) collective-permute-start(bf16[1,896,1024]{2,1,0:T(8,128)(2,1)} %refs_2_.3), channel_id=1, source_target_pairs={{0,1},{1,0},{2,3},{3,2},{4,5},{5,4},{6,7},{7,6},{8,9},{9,8},{10,11... | collective-permute-start | bytes 5505032 | tf_op jit(solution)/shard_map/ppermute | solution.py:291
  20.4 14.3 %all-to-all-start.1 = ((bf16[32,40,128]{2,1,0:T(8,128)(2,1)}), bf16[32,40,128]{2,1,0:T(8,128)(2,1)S(1)}, u32[]{:S(2)}, u32[]{:S(2)}) async-start(bf16[32,40,128]{2,1,0:T(8,128)(2,1)} %shard_map.119), calls=%async_computation.1 | async-start | bytes 655360 | tf_op jit(solution)/shard_map/all_to_all | solution.py:148
  36.4 1.6 %collective-permute-start.3 = (bf16[128,1024]{1,0:T(8,128)(2,1)S(1)}, bf16[128,1024]{1,0:T(8,128)(2,1)S(1)}, u32[]{:S(2)}, u32[]{:S(2)}) collective-permute-start(bf16[128,1024]{1,0:T(8,128)(2,1)S(1)} %get-tuple-element.33.rows_ref), channel_id=1, source_target_pairs={{0,1},{1,0},{2,3},{3,2},{4,5},{5,4},{6,7},{7,6},{8,9},{9,8},{10,11... | collective-permute-start | bytes 786440 | tf_op jit(solution)/shard_map/ppermute | solution.py:291
  36.5 8.1 %collective-permute-start.5 = (bf16[128,1024]{1,0:T(8,128)(2,1)S(1)}, bf16[128,1024]{1,0:T(8,128)(2,1)S(1)}, u32[]{:S(2)}, u32[]{:S(2)}) collective-permute-start(bf16[128,1024]{1,0:T(8,128)(2,1)S(1)} %get-tuple-element.33.rows_ref), channel_id=1, source_target_pairs={{0,4},{1,3},{4,8},{5,1},{8,12},{9,5},{12,14},{13,9},{14,10},{15,13... | collective-permute-start | bytes 786440 | tf_op jit(solution)/shard_map/ppermute | solution.py:291
  38.0 7.7 %collective-permute-start.4 = (bf16[128,1024]{1,0:T(8,128)(2,1)S(1)}, bf16[128,1024]{1,0:T(8,128)(2,1)S(1)}, u32[]{:S(2)}, u32[]{:S(2)}) collective-permute-start(bf16[128,1024]{1,0:T(8,128)(2,1)S(1)} %collective-permute-done.3), channel_id=1, source_target_pairs={{0,4},{1,3},{4,8},{5,1},{8,12},{9,5},{12,14},{13,9},{14,10},{15,13... | collective-permute-start | bytes 786440 | tf_op jit(solution)/shard_map/ppermute | solution.py:291
  44.6 6.4 %collective-permute-start.7 = (bf16[128,1024]{1,0:T(8,128)(2,1)S(1)}, bf16[128,1024]{1,0:T(8,128)(2,1)S(1)}, u32[]{:S(2)}, u32[]{:S(2)}) collective-permute-start(bf16[128,1024]{1,0:T(8,128)(2,1)S(1)} %collective-permute-done.5.rows_ref), channel_id=1, source_target_pairs={{0,4},{1,3},{4,8},{5,1},{8,12},{9,5},{12,14},{13,9},{14,10},{15,13... | collective-permute-start | bytes 786440 | tf_op jit(solution)/shard_map/ppermute | solution.py:291
  45.8 8.1 %collective-permute-start.6 = (bf16[128,1024]{1,0:T(8,128)(2,1)S(1)}, bf16[128,1024]{1,0:T(8,128)(2,1)S(1)}, u32[]{:S(2)}, u32[]{:S(2)}) collective-permute-start(bf16[128,1024]{1,0:T(8,128)(2,1)S(1)} %collective-permute-done.4.rows_ref), channel_id=1, source_target_pairs={{0,4},{1,3},{4,8},{5,1},{8,12},{9,5},{12,14},{13,9},{14,10},{15,13... | collective-permute-start | bytes 786440 | tf_op jit(solution)/shard_map/ppermute | solution.py:291
  51.0 6.4 %collective-permute-start.9 = (bf16[128,1024]{1,0:T(8,128)(2,1)S(1)}, bf16[128,1024]{1,0:T(8,128)(2,1)S(1)}, u32[]{:S(2)}, u32[]{:S(2)}) collective-permute-start(bf16[128,1024]{1,0:T(8,128)(2,1)S(1)} %collective-permute-done.7.rows_ref), channel_id=1, source_target_pairs={{0,4},{1,3},{4,8},{5,1},{8,12},{9,5},{12,14},{13,9},{14,10},{15,13... | collective-permute-start | bytes 786440 | tf_op jit(solution)/shard_map/ppermute | solution.py:291
  53.8 6.4 %collective-permute-start.8 = (bf16[128,1024]{1,0:T(8,128)(2,1)S(1)}, bf16[128,1024]{1,0:T(8,128)(2,1)S(1)}, u32[]{:S(2)}, u32[]{:S(2)}) collective-permute-start(bf16[128,1024]{1,0:T(8,128)(2,1)S(1)} %collective-permute-done.6.rows_ref), channel_id=1, source_target_pairs={{0,4},{1,3},{4,8},{5,1},{8,12},{9,5},{12,14},{13,9},{14,10},{15,13... | collective-permute-start | bytes 786440 | tf_op jit(solution)/shard_map/ppermute | solution.py:291
  57.4 6.6 %collective-permute-start.14 = (bf16[128,1024]{1,0:T(8,128)(2,1)S(1)}, bf16[128,1024]{1,0:T(8,128)(2,1)S(1)}, u32[]{:S(2)}, u32[]{:S(2)}) collective-permute-start(bf16[128,1024]{1,0:T(8,128)(2,1)S(1)} %collective-permute-done.9.rows_ref), channel_id=1, source_target_pairs={{0,4},{1,3},{4,8},{5,1},{8,12},{9,5},{12,14},{13,9},{14,10},{15,13... | collective-permute-start | bytes 786440 | tf_op jit(solution)/shard_map/ppermute | solution.py:291
  62.1 6.4 %collective-permute-start.10 = (bf16[128,1024]{1,0:T(8,128)(2,1)S(1)}, bf16[128,1024]{1,0:T(8,128)(2,1)S(1)}, u32[]{:S(2)}, u32[]{:S(2)}) collective-permute-start(bf16[128,1024]{1,0:T(8,128)(2,1)S(1)} %convert_element_type.69), channel_id=1, source_target_pairs={{0,2},{1,5},{4,0},{5,9},{8,4},{9,13},{12,8},{13,15},{14,12},{15,11... | collective-permute-start | bytes 786440 | tf_op jit(solution)/shard_map/ppermute | solution.py:291
  65.9 6.4 %collective-permute-start.15 = (bf16[128,1024]{1,0:T(8,128)(2,1)S(1)}, bf16[128,1024]{1,0:T(8,128)(2,1)S(1)}, u32[]{:S(2)}, u32[]{:S(2)}) collective-permute-start(bf16[128,1024]{1,0:T(8,128)(2,1)S(1)} %convert_element_type.75), channel_id=1, source_target_pairs={{0,2},{1,5},{4,0},{5,9},{8,4},{9,13},{12,8},{13,15},{14,12},{15,11... | collective-permute-start | bytes 786440 | tf_op jit(solution)/shard_map/ppermute | solution.py:291
  68.6 6.5 %collective-permute-start.11 = (bf16[128,1024]{1,0:T(8,128)(2,1)S(1)}, bf16[128,1024]{1,0:T(8,128)(2,1)S(1)}, u32[]{:S(2)}, u32[]{:S(2)}) collective-permute-start(bf16[128,1024]{1,0:T(8,128)(2,1)S(1)} %add_convert_fusion.5), channel_id=1, source_target_pairs={{0,2},{1,5},{4,0},{5,9},{8,4},{9,13},{12,8},{13,15},{14,12},{15,11... | collective-permute-start | bytes 786440 | tf_op jit(solution)/shard_map/ppermute | solution.py:291
  72.4 6.4 %collective-permute-start.16 = (bf16[128,1024]{1,0:T(8,128)(2,1)S(1)}, bf16[128,1024]{1,0:T(8,128)(2,1)S(1)}, u32[]{:S(2)}, u32[]{:S(2)}) collective-permute-start(bf16[128,1024]{1,0:T(8,128)(2,1)S(1)} %add_convert_fusion.3), channel_id=1, source_target_pairs={{0,2},{1,5},{4,0},{5,9},{8,4},{9,13},{12,8},{13,15},{14,12},{15,11... | collective-permute-start | bytes 786440 | tf_op jit(solution)/shard_map/ppermute | solution.py:291
  75.2 6.4 %collective-permute-start.12 = (bf16[128,1024]{1,0:T(8,128)(2,1)S(1)}, bf16[128,1024]{1,0:T(8,128)(2,1)S(1)}, u32[]{:S(2)}, u32[]{:S(2)}) collective-permute-start(bf16[128,1024]{1,0:T(8,128)(2,1)S(1)} %add_convert_fusion.4), channel_id=1, source_target_pairs={{0,2},{1,5},{4,0},{5,9},{8,4},{9,13},{12,8},{13,15},{14,12},{15,11... | collective-permute-start | bytes 786440 | tf_op jit(solution)/shard_map/ppermute | solution.py:291
  78.9 6.4 %collective-permute-start.17 = (bf16[128,1024]{1,0:T(8,128)(2,1)S(1)}, bf16[128,1024]{1,0:T(8,128)(2,1)S(1)}, u32[]{:S(2)}, u32[]{:S(2)}) collective-permute-start(bf16[128,1024]{1,0:T(8,128)(2,1)S(1)} %add_convert_fusion.2), channel_id=1, source_target_pairs={{0,2},{1,5},{4,0},{5,9},{8,4},{9,13},{12,8},{13,15},{14,12},{15,11... | collective-permute-start | bytes 786440 | tf_op jit(solution)/shard_map/ppermute | solution.py:291
  81.6 5.4 %collective-permute-start.13 = (bf16[128,1024]{1,0:T(8,128)(2,1)S(1)}, bf16[128,1024]{1,0:T(8,128)(2,1)S(1)}, u32[]{:S(2)}, u32[]{:S(2)}) collective-permute-start(bf16[128,1024]{1,0:T(8,128)(2,1)S(1)} %collective-permute-done.12), channel_id=1, source_target_pairs={{0,1},{1,0},{2,3},{3,2},{4,5},{5,4},{6,7},{7,6},{8,9},{9,8},{10,11... | collective-permute-start | bytes 786440 | tf_op jit(solution)/shard_map/ppermute | solution.py:291
  85.4 6.4 %collective-permute-start.18 = (bf16[128,1024]{1,0:T(8,128)(2,1)S(1)}, bf16[128,1024]{1,0:T(8,128)(2,1)S(1)}, u32[]{:S(2)}, u32[]{:S(2)}) collective-permute-start(bf16[128,1024]{1,0:T(8,128)(2,1)S(1)} %add_convert_fusion.1), channel_id=1, source_target_pairs={{0,2},{1,5},{4,0},{5,9},{8,4},{9,13},{12,8},{13,15},{14,12},{15,11... | collective-permute-start | bytes 786440 | tf_op jit(solution)/shard_map/ppermute | solution.py:291

commit v5 on v4

--- a/solution.py
+++ b/solution.py
@@ -187,8 +187,9 @@
     routed_ref[...] = rms(mixed, moe_gain_ref[...]).astype(BF16)
 
 
-def expert_kernel(chips, offset, flip, dense, rows_ref, *refs):
-    weights, out_ref, refs = refs[:6], refs[6], refs[7:]
+def expert_kernel(chips, offset, flip, experts, dense, rows_ref, *refs):
+    count = 3 * len(experts) if len(refs) < 13 else 6
+    weights, out_ref, refs = refs[:count], refs[count], refs[count + 1 :]
     copies = []
     if refs:
         copies = copies_of(weights, refs[:6], refs[6])
@@ -203,9 +204,9 @@
     table = dense[...]
     lane = lax.broadcasted_iota(jnp.int32, table.shape, 1)
     total = jnp.zeros(rows.shape, F32)
-    for which in range(2):
-        w_gate, w_up, w_down = weights[3 * which : 3 * which + 3]
-        for copy in copies[3 * which : 3 * which + 3]:
+    for i, which in enumerate(experts):
+        w_gate, w_up, w_down = weights[3 * i : 3 * i + 3]
+        for copy in copies[3 * i : 3 * i + 3]:
             copy.wait()
         gate = jnp.dot(rows, w_gate[0], preferred_element_type=F32)
         upper = jnp.dot(rows, w_up[0], preferred_element_type=F32)
@@ -214,16 +215,19 @@
         picked = jnp.where(lane == which * 2 * chips + source, table, 0.0)
         total += result * jnp.sum(picked, axis=1, keepdims=True)
     out_ref[...] = total
-
-
-def expert(rows, chips, offset, flip, dense, weights, staging=False):
-    outs, specs, scratch = [jax.ShapeDtypeStruct(rows.shape, F32)], [VMEM] * 6, []
+    for copy in copies[3 * len(experts) :]:
+        copy.wait()
+
+
+def expert(rows, chips, offset, flip, dense, weights, experts=(0, 1), staging=False):
+    outs = [jax.ShapeDtypeStruct(rows.shape, F32)]
+    specs, scratch = [VMEM] * len(weights), []
     if staging:
         outs += [pltpu.VMEM(w.shape, w.dtype) for w in weights]
         specs, scratch = [HBM] * 6, [pltpu.SemaphoreType.DMA((6,))]
         weights = [in_hbm(w) for w in weights]
     return pl.pallas_call(
-        functools.partial(expert_kernel, chips, offset, flip),
+        functools.partial(expert_kernel, chips, offset, flip, experts),
         out_shape=outs,
         in_specs=[VMEM] * 2 + specs,
         out_specs=[VMEM] * len(outs),
@@ -293,8 +297,8 @@
     weights = [w_gate, w_up, w_down]
     weights += [send(w, swap) for w in weights]
     here = [send(routed, ring), send(send(routed, swap), ring)]
-    at_home, *weights = expert(routed, chips, 0, 0, dense, weights, True)
-    done, ready = {}, [at_home, at_home]
+    home_own, *weights = expert(routed, chips, 0, 0, dense, weights, (0,), True)
+    done, ready = {}, [home_own, home_own]
     for step in range(1, far):
         passed = []
         for chain in range(2):
@@ -312,6 +316,8 @@
         late = hold(late, done[0, far])
         (done[0, far - 1],) = expert(late, chips, far - 1, 0, dense, weights)
 
+    start = hold(routed, done[0, max(far - 1, 1)])
+    (home_other,) = expert(start, chips, 0, 0, dense, weights[3:], (1,))
     moving = [None, None]
     for step in range(far, 0, -1):
         for chain in range(2):
@@ -320,7 +326,7 @@
                 if moving[chain] is not None:
                     total = total + moving[chain]
                 moving[chain] = send(total.astype(BF16), back).astype(F32)
-    home = mixed + at_home
+    home = mixed + home_own + home_other
     if far > 1:
         home = home + send(moving[1].astype(BF16), swap).astype(F32)
     return (home + moving[0]).astype(BF16)

time: 93 us -> 92 us (0.989)
  waiting for transfers between devices: 33.9 us -> 31.2 us
  starting transfers between devices: 27.6 us -> 29.2 us
    ppermute x19, waiting for transfers between devices: 19.1 us -> 16.4 us  [send(): return lax.ppermute(rows, 'ctx', way)]
    ppermute x19, starting transfers between devices: 17.7 us -> 19.3 us  [send(): return lax.ppermute(rows, 'ctx', way)]
    pallas_call x8 -> x9, Pallas kernels: 18.7 us -> 18.7 us  [expert(): pl.pallas_call(functools.partial(expert_kernel, chips, offset, flip, expe...]
  transfers between devices with their start and end apart: 21 -> 21, of which waited for: 16 -> 15; matrix products, arithmetic and copies ran while one was open for 3% -> 3% of each run, Pallas kernels for 27% -> 28%
where the time goes in v5:
time: 92 us; the launch traced here: 91.6 us
  waiting for transfers between devices  31.2 us (34%)
  starting transfers between devices  29.2 us (32%)
  Pallas kernels  27.4 us (30%)
  other arithmetic  3.41 us (4%)
    ppermute x19, starting transfers between devices, send(): return lax.ppermute(rows, 'ctx', way)  19.3 us
    pallas_call x9, Pallas kernels, expert(): pl.pallas_call(functools.partial(expert_kernel, chips, offset, flip, expe...  18.7 us
    ppermute x19, waiting for transfers between devices, send(): return lax.ppermute(rows, 'ctx', way)  16.4 us
    all_to_all x1, waiting for transfers between devices, scan_states(): sums = lax.all_to_all(sums, BOTH, split_axis=0, concat_axis=0, tiled=True)  7.56 us
    all_to_all x1, starting transfers between devices, scan_states(): lax.all_to_all(pieces, BOTH, split_axis=0, concat_axis=0, tiled=True)  7.3 us
    all_to_all x1, waiting for transfers between devices, scan_states(): lax.all_to_all(pieces, BOTH, split_axis=0, concat_axis=0, tiled=True)  7.25 us
    pallas_call x1, Pallas kernels, attend_inside(): pl.pallas_call(functools.partial(inside_kernel, count), out_shape=outs, i...  4.11 us
    all_to_all x1, starting transfers between devices, scan_states(): sums = lax.all_to_all(sums, BOTH, split_axis=0, concat_axis=0, tiled=True)  2.59 us
  transfers between devices with their start and end apart: 21, of which 15 were waited for; matrix products, arithmetic and copies ran while one was open for 3% of the time, Pallas kernels for 28%

profile of v5, /device:TPU:0, one launch (start us, length us, event | category | flops | bytes accessed | tf_op | source)
XLA Modules:
  0.0 91.6 jit_solution(6596499264212317932)
XLA Ops:
  0.0 2.0 %shard_map.118.refs_6_ = bf16[1024,128]{1,0:T(8,128)(2,1)} custom-call(bf16[128,1024]{1,0:T(8,128)(2,1)} %refs_1_.2, bf16[128,1024]{1,0:T(8,128)(2,1)} %refs_2_.2), custom_call_target="tpu_custom_call" | custom-call | tf_op jit(solution)/shard_map/pallas_call | solution.py:258
  2.0 7.3 %all-to-all-start = ((bf16[32,32,128]{2,1,0:T(8,128)(2,1)}), bf16[32,32,128]{2,1,0:T(8,128)(2,1)S(1)}, u32[]{:S(2)}, u32[]{:S(2)}) async-start(bf16[32,32,128]{2,1,0:T(8,128)(2,1)} %bitcast), calls=%async_computation | async-start | bytes 524288 | tf_op jit(solution)/shard_map/all_to_all | solution.py:134
  9.3 0.3 collective-permute-start
  9.6 0.3 collective-permute-start.1
  9.9 0.3 collective-permute-start.2
  10.2 0.7 convert_reduce_fusion
  10.9 0.7 convert_divide_fusion
  11.6 0.7 select_reduce_fusion
  12.4 7.3 %all-to-all-done.pieces_ref = bf16[32,32,128]{2,1,0:T(8,128)(2,1)S(1)} async-done(((bf16[32,32,128]{2,1,0:T(8,128)(2,1)}), bf16[32,32,128]{2,1,0:T(8,128)(2,1)S(1)}, u32[]{:S(2)}, u32[]{:S(2)}) %all-to-all-start) | async-done | bytes 262176 | tf_op jit(solution)/shard_map/all_to_all | solution.py:134
  19.6 0.8 shard_map.119
  20.4 2.6 %all-to-all-start.1 = ((bf16[32,40,128]{2,1,0:T(8,128)(2,1)}), bf16[32,40,128]{2,1,0:T(8,128)(2,1)S(1)}, u32[]{:S(2)}, u32[]{:S(2)}) async-start(bf16[32,40,128]{2,1,0:T(8,128)(2,1)} %shard_map.119), calls=%async_computation.1 | async-start | bytes 655360 | tf_op jit(solution)/shard_map/all_to_all | solution.py:148
  23.0 4.1 %shard_map.120 = (bf16[128,1024]{1,0:T(8,128)(2,1)S(1)}, bf16[128,1024]{1,0:T(8,128)(2,1)}, bf16[128,1024]{1,0:T(8,128)(2,1)}, bf16[1024,1024]{1,0:T(8,128)(2,1)...) custom-call(bf16[128,1024]{1,0:T(8,128)(2,1)} %refs_0_.2, bf16[128,1024]{1,0:T(8,128)(2,1)} %refs_1_.2, ...), custom_call_target="tpu_custom_call" | custom-call | tf_op jit(solution)/shard_map/pallas_call | solution.py:101
  27.1 7.6 %all-to-all-done.1.sums_ref = bf16[32,40,128]{2,1,0:T(8,128)(2,1)S(1)} async-done(((bf16[32,40,128]{2,1,0:T(8,128)(2,1)}), bf16[32,40,128]{2,1,0:T(8,128)(2,1)S(1)}, u32[]{:S(2)}, u32[]{:S(2)}) %all-to-all-start.1) | async-done | bytes 327712 | tf_op jit(solution)/shard_map/all_to_all | solution.py:148
  34.7 1.8 %shard_map.121 = (f32[128,1024]{1,0:T(8,128)S(1)}, bf16[128,1024]{1,0:T(8,128)(2,1)S(1)}) custom-call(bf16[32,40,128]{2,1,0:T(8,128)(2,1)S(1)} %all-to-all-done.1.sums_ref, bf16[128,1024]{1,0:T(8,128)(2,1)S(1)} %get-tuple-element.28.q_ref, bf16[1024,1024]{1,0:T(8,128)(2,1)S(1)} %get-tuple-element.29.proj_ref, f32[1,1024]{1,0:T(1,128)S(1)} %get-tuple-element.30.gain_ref, ...), custom_call_target="tpu_custom_call" | custom-call | tf_op jit(solution)/shard_map/pallas_call | solution.py:278
  36.4 0.1 collective-permute-start.7
  36.5 1.1 %collective-permute-start.3 = (bf16[128,1024]{1,0:T(8,128)(2,1)S(1)}, bf16[128,1024]{1,0:T(8,128)(2,1)S(1)}, u32[]{:S(2)}, u32[]{:S(2)}) collective-permute-start(bf16[128,1024]{1,0:T(8,128)(2,1)S(1)} %get-tuple-element.50.rows_ref), channel_id=1, source_target_pairs={{0,4},{1,3},{4,8},{5,1},{8,12},{9,5},{12,14},{13,9},{14,10},{15,13... | collective-permute-start | bytes 786440 | tf_op jit(solution)/shard_map/ppermute | solution.py:295
  37.7 0.4 collective-permute-done.7
  38.0 1.1 %collective-permute-start.8 = (bf16[128,1024]{1,0:T(8,128)(2,1)S(1)}, bf16[128,1024]{1,0:T(8,128)(2,1)S(1)}, u32[]{:S(2)}, u32[]{:S(2)}) collective-permute-start(bf16[128,1024]{1,0:T(8,128)(2,1)S(1)} %collective-permute-done.7), channel_id=1, source_target_pairs={{0,4},{1,3},{4,8},{5,1},{8,12},{9,5},{12,14},{13,9},{14,10},{15,13... | collective-permute-start | bytes 786440 | tf_op jit(solution)/shard_map/ppermute | solution.py:295
  39.1 0.1 copy.29
  39.2 0.0 collective-permute-done.refs_3_
  39.2 0.0 collective-permute-done.1.refs_4_
  39.3 0.0 collective-permute-done.2.refs_5_
  39.3 4.3 %shard_map.122 = (f32[128,1024]{1,0:T(8,128)S(1)}, bf16[1,1024,896]{2,1,0:T(8,128)(2,1)S(1)}, bf16[1,1024,896]{2,1,0:T(8,128)(2,1)S(1)}, bf16[1,896,1024]{2,1,0:...) custom-call(f32[128,32]{1,0:T(8,128)S(1)} %bitcast.24, ...), custom_call_target="tpu_custom_call" | custom-call | tf_op jit(solution)/shard_map/pallas_call | solution.py:229
  43.5 0.0 collective-permute-done.3.rows_ref
  43.5 0.6 collective-permute-start.4
  44.2 1.6 %collective-permute-done.8.rows_ref = bf16[128,1024]{1,0:T(8,128)(2,1)S(1)} collective-permute-done((bf16[128,1024]{1,0:T(8,128)(2,1)S(1)}, bf16[128,1024]{1,0:T(8,128)(2,1)S(1)}, u32[]{:S(2)}, u32[]{:S(2)}) %collective-permute-start.8) | collective-permute-done | bytes 262176 | tf_op jit(solution)/shard_map/ppermute | solution.py:295
  45.8 1.1 %collective-permute-start.9 = (bf16[128,1024]{1,0:T(8,128)(2,1)S(1)}, bf16[128,1024]{1,0:T(8,128)(2,1)S(1)}, u32[]{:S(2)}, u32[]{:S(2)}) collective-permute-start(bf16[128,1024]{1,0:T(8,128)(2,1)S(1)} %collective-permute-done.8.rows_ref), channel_id=1, source_target_pairs={{0,4},{1,3},{4,8},{5,1},{8,12},{9,5},{12,14},{13,9},{14,10},{15,13... | collective-permute-start | bytes 786440 | tf_op jit(solution)/shard_map/ppermute | solution.py:295
  46.8 1.9 %shard_map.123 = f32[128,1024]{1,0:T(8,128)S(1)} custom-call(f32[128,32]{1,0:T(8,128)S(1)} %bitcast.25, bf16[128,1024]{1,0:T(8,128)(2,1)S(1)} %collective-permute-done.3.rows_ref, bf16[1,1024,896]{2,1,0:T(8,128)(2,1)S(1)} %get-tuple-element.37.refs_0_, bf16[1,1024,896]{2,1,0:T(8,128)(2,1)S(1)} %get-tuple-element.38.refs_1_, ...), custom_call_target="tpu_custom_call" | custom-call | tf_op jit(solution)/shard_map/pallas_call | solution.py:229
  48.7 1.2 %collective-permute-done.4.rows_ref = bf16[128,1024]{1,0:T(8,128)(2,1)S(1)} collective-permute-done((bf16[128,1024]{1,0:T(8,128)(2,1)S(1)}, bf16[128,1024]{1,0:T(8,128)(2,1)S(1)}, u32[]{:S(2)}, u32[]{:S(2)}) %collective-permute-start.4) | collective-permute-done | bytes 262176 | tf_op jit(solution)/shard_map/ppermute | solution.py:295
  50.0 0.6 collective-permute-start.5
  50.6 1.9 %shard_map.125 = f32[128,1024]{1,0:T(8,128)S(1)} custom-call(f32[128,32]{1,0:T(8,128)S(1)} %bitcast.26, bf16[128,1024]{1,0:T(8,128)(2,1)S(1)} %collective-permute-done.8.rows_ref, bf16[1,1024,896]{2,1,0:T(8,128)(2,1)S(1)} %get-tuple-element.37.refs_0_, bf16[1,1024,896]{2,1,0:T(8,128)(2,1)S(1)} %get-tuple-element.38.refs_1_, ...), custom_call_target="tpu_custom_call" | custom-call | tf_op jit(solution)/shard_map/pallas_call | solution.py:229
  52.5 0.3 collective-permute-done.9.rows_ref
  52.8 1.1 %collective-permute-start.10 = (bf16[128,1024]{1,0:T(8,128)(2,1)S(1)}, bf16[128,1024]{1,0:T(8,128)(2,1)S(1)}, u32[]{:S(2)}, u32[]{:S(2)}) collective-permute-start(bf16[128,1024]{1,0:T(8,128)(2,1)S(1)} %collective-permute-done.9.rows_ref), channel_id=1, source_target_pairs={{0,4},{1,3},{4,8},{5,1},{8,12},{9,5},{12,14},{13,9},{14,10},{15,13... | collective-permute-start | bytes 786440 | tf_op jit(solution)/shard_map/ppermute | solution.py:295
  53.9 1.9 %shard_map.124 = f32[128,1024]{1,0:T(8,128)S(1)} custom-call(f32[128,32]{1,0:T(8,128)S(1)} %bitcast.27, bf16[128,1024]{1,0:T(8,128)(2,1)S(1)} %collective-permute-done.4.rows_ref, bf16[1,1024,896]{2,1,0:T(8,128)(2,1)S(1)} %get-tuple-element.37.refs_0_, bf16[1,1024,896]{2,1,0:T(8,128)(2,1)S(1)} %get-tuple-element.38.refs_1_, ...), custom_call_target="tpu_custom_call" | custom-call | tf_op jit(solution)/shard_map/pallas_call | solution.py:229
  55.8 0.5 collective-permute-done.5.rows_ref
  56.3 0.6 collective-permute-start.6
  56.9 1.9 %shard_map.126 = f32[128,1024]{1,0:T(8,128)S(1)} custom-call(f32[128,32]{1,0:T(8,128)S(1)} %bitcast.28, bf16[128,1024]{1,0:T(8,128)(2,1)S(1)} %collective-permute-done.9.rows_ref, bf16[1,1024,896]{2,1,0:T(8,128)(2,1)S(1)} %get-tuple-element.37.refs_0_, bf16[1,1024,896]{2,1,0:T(8,128)(2,1)S(1)} %get-tuple-element.38.refs_1_, ...), custom_call_target="tpu_custom_call" | custom-call | tf_op jit(solution)/shard_map/pallas_call | solution.py:229
  58.8 0.3 collective-permute-done.10.rows_ref
  59.1 1.9 %shard_map.127 = f32[128,1024]{1,0:T(8,128)S(1)} custom-call(f32[128,32]{1,0:T(8,128)S(1)} %bitcast.29, bf16[128,1024]{1,0:T(8,128)(2,1)S(1)} %collective-permute-done.10.rows_ref, bf16[1,1024,896]{2,1,0:T(8,128)(2,1)S(1)} %get-tuple-element.37.refs_0_, bf16[1,1024,896]{2,1,0:T(8,128)(2,1)S(1)} %get-tuple-element.38.refs_1_, ...), custom_call_target="tpu_custom_call" | custom-call | tf_op jit(solution)/shard_map/pallas_call | solution.py:229
  61.1 1.3 %collective-permute-start.11 = (bf16[128,1024]{1,0:T(8,128)(2,1)S(1)}, bf16[128,1024]{1,0:T(8,128)(2,1)S(1)}, u32[]{:S(2)}, u32[]{:S(2)}) collective-permute-start(bf16[128,1024]{1,0:T(8,128)(2,1)S(1)} %convert_element_type.69), channel_id=1, source_target_pairs={{0,2},{1,5},{4,0},{5,9},{8,4},{9,13},{12,8},{13,15},{14,12},{15,11... | collective-permute-start | bytes 786440 | tf_op jit(solution)/shard_map/ppermute | solution.py:295
  62.4 0.6 collective-permute-done.6.rows_ref
  62.9 1.9 %shard_map.128 = f32[128,1024]{1,0:T(8,128)S(1)} custom-call(f32[128,32]{1,0:T(8,128)S(1)} %bitcast.30, bf16[128,1024]{1,0:T(8,128)(2,1)S(1)} %collective-permute-done.6.rows_ref, bf16[1,1024,896]{2,1,0:T(8,128)(2,1)S(1)} %get-tuple-element.37.refs_0_, bf16[1,1024,896]{2,1,0:T(8,128)(2,1)S(1)} %get-tuple-element.38.refs_1_, ...), custom_call_target="tpu_custom_call" | custom-call | tf_op jit(solution)/shard_map/pallas_call | solution.py:229
  64.9 1.6 %collective-permute-start.15 = (bf16[128,1024]{1,0:T(8,128)(2,1)S(1)}, bf16[128,1024]{1,0:T(8,128)(2,1)S(1)}, u32[]{:S(2)}, u32[]{:S(2)}) collective-permute-start(bf16[128,1024]{1,0:T(8,128)(2,1)S(1)} %convert_element_type.75), channel_id=1, source_target_pairs={{0,2},{1,5},{4,0},{5,9},{8,4},{9,13},{12,8},{13,15},{14,12},{15,11... | collective-permute-start | bytes 786440 | tf_op jit(solution)/shard_map/ppermute | solution.py:295
  66.5 1.9 %shard_map.129 = f32[128,1024]{1,0:T(8,128)S(1)} custom-call(f32[128,32]{1,0:T(8,128)S(1)} %bitcast.31, bf16[128,1024]{1,0:T(8,128)(2,1)S(1)} %collective-permute-done.5.rows_ref, bf16[1,1024,896]{2,1,0:T(8,128)(2,1)S(1)} %get-tuple-element.37.refs_0_, bf16[1,1024,896]{2,1,0:T(8,128)(2,1)S(1)} %get-tuple-element.38.refs_1_, ...), custom_call_target="tpu_custom_call" | custom-call | tf_op jit(solution)/shard_map/pallas_call | solution.py:229
  68.4 0.0 collective-permute-done.11
  68.4 0.1 add_convert_fusion.5
  68.5 2.0 %collective-permute-start.12 = (bf16[128,1024]{1,0:T(8,128)(2,1)S(1)}, bf16[128,1024]{1,0:T(8,128)(2,1)S(1)}, u32[]{:S(2)}, u32[]{:S(2)}) collective-permute-start(bf16[128,1024]{1,0:T(8,128)(2,1)S(1)} %add_convert_fusion.5), channel_id=1, source_target_pairs={{0,2},{1,5},{4,0},{5,9},{8,4},{9,13},{12,8},{13,15},{14,12},{15,11... | collective-permute-start | bytes 786440 | tf_op jit(solution)/shard_map/ppermute | solution.py:295
  70.4 0.8 collective-permute-done.15
  71.3 0.1 add_convert_fusion.3
  71.4 1.6 %collective-permute-start.16 = (bf16[128,1024]{1,0:T(8,128)(2,1)S(1)}, bf16[128,1024]{1,0:T(8,128)(2,1)S(1)}, u32[]{:S(2)}, u32[]{:S(2)}) collective-permute-start(bf16[128,1024]{1,0:T(8,128)(2,1)S(1)} %add_convert_fusion.3), channel_id=1, source_target_pairs={{0,2},{1,5},{4,0},{5,9},{8,4},{9,13},{12,8},{13,15},{14,12},{15,11... | collective-permute-start | bytes 786440 | tf_op jit(solution)/shard_map/ppermute | solution.py:295
  73.0 1.9 %collective-permute-done.12 = bf16[128,1024]{1,0:T(8,128)(2,1)S(1)} collective-permute-done((bf16[128,1024]{1,0:T(8,128)(2,1)S(1)}, bf16[128,1024]{1,0:T(8,128)(2,1)S(1)}, u32[]{:S(2)}, u32[]{:S(2)}) %collective-permute-start.12) | collective-permute-done | bytes 262176 | tf_op jit(solution)/shard_map/ppermute | solution.py:295
  74.9 0.1 add_convert_fusion.4
  75.0 2.0 %collective-permute-start.13 = (bf16[128,1024]{1,0:T(8,128)(2,1)S(1)}, bf16[128,1024]{1,0:T(8,128)(2,1)S(1)}, u32[]{:S(2)}, u32[]{:S(2)}) collective-permute-start(bf16[128,1024]{1,0:T(8,128)(2,1)S(1)} %add_convert_fusion.4), channel_id=1, source_target_pairs={{0,2},{1,5},{4,0},{5,9},{8,4},{9,13},{12,8},{13,15},{14,12},{15,11... | collective-permute-start | bytes 786440 | tf_op jit(solution)/shard_map/ppermute | solution.py:295
  76.9 0.8 collective-permute-done.16
  77.8 0.1 add_convert_fusion.2
  77.8 1.9 %collective-permute-start.17 = (bf16[128,1024]{1,0:T(8,128)(2,1)S(1)}, bf16[128,1024]{1,0:T(8,128)(2,1)S(1)}, u32[]{:S(2)}, u32[]{:S(2)}) collective-permute-start(bf16[128,1024]{1,0:T(8,128)(2,1)S(1)} %add_convert_fusion.2), channel_id=1, source_target_pairs={{0,2},{1,5},{4,0},{5,9},{8,4},{9,13},{12,8},{13,15},{14,12},{15,11... | collective-permute-start | bytes 786440 | tf_op jit(solution)/shard_map/ppermute | solution.py:295
  79.7 1.7 %collective-permute-done.13 = bf16[128,1024]{1,0:T(8,128)(2,1)S(1)} collective-permute-done((bf16[128,1024]{1,0:T(8,128)(2,1)S(1)}, bf16[128,1024]{1,0:T(8,128)(2,1)S(1)}, u32[]{:S(2)}, u32[]{:S(2)}) %collective-permute-start.13) | collective-permute-done | bytes 262176 | tf_op jit(solution)/shard_map/ppermute | solution.py:295
  81.4 2.9 %collective-permute-done.17 = bf16[128,1024]{1,0:T(8,128)(2,1)S(1)} collective-permute-done((bf16[128,1024]{1,0:T(8,128)(2,1)S(1)}, bf16[128,1024]{1,0:T(8,128)(2,1)S(1)}, u32[]{:S(2)}, u32[]{:S(2)}) %collective-permute-start.17) | collective-permute-done | bytes 262176 | tf_op jit(solution)/shard_map/ppermute | solution.py:295
  84.3 0.1 add_convert_fusion.1
  84.3 1.9 %collective-permute-start.18 = (bf16[128,1024]{1,0:T(8,128)(2,1)S(1)}, bf16[128,1024]{1,0:T(8,128)(2,1)S(1)}, u32[]{:S(2)}, u32[]{:S(2)}) collective-permute-start(bf16[128,1024]{1,0:T(8,128)(2,1)S(1)} %add_convert_fusion.1), channel_id=1, source_target_pairs={{0,2},{1,5},{4,0},{5,9},{8,4},{9,13},{12,8},{13,15},{14,12},{15,11... | collective-permute-start | bytes 786440 | tf_op jit(solution)/shard_map/ppermute | solution.py:295
  86.2 1.0 %shard_map.130 = f32[128,1024]{1,0:T(8,128)S(1)} custom-call(f32[128,32]{1,0:T(8,128)S(1)} %bitcast.32, bf16[128,1024]{1,0:T(8,128)(2,1)S(1)} %get-tuple-element.50.rows_ref, bf16[1,1024,896]{2,1,0:T(8,128)(2,1)S(1)} %get-tuple-element.40.refs_3_.refs_0_, bf16[1,1024,896]{2,1,0:T(8,128)(2,1)S(1)} %get-tuple-element.41.refs_4_.refs_1_, ...), custom_call_target="tpu_custom_call" | custom-call | tf_op jit(solution)/shard_map/pallas_call | solution.py:229
  87.3 0.0 collective-permute-done.14
  87.3 3.5 %collective-permute-done.18 = bf16[128,1024]{1,0:T(8,128)(2,1)S(1)} collective-permute-done((bf16[128,1024]{1,0:T(8,128)(2,1)S(1)}, bf16[128,1024]{1,0:T(8,128)(2,1)S(1)}, u32[]{:S(2)}, u32[]{:S(2)}) %collective-permute-start.18) | collective-permute-done | bytes 262176 | tf_op jit(solution)/shard_map/ppermute | solution.py:295
  90.7 0.9 add_convert_fusion
  (12 shorter events, 0.2 us)
Async XLA Ops:
  2.0 17.6 %all-to-all-start = ((bf16[32,32,128]{2,1,0:T(8,128)(2,1)}), bf16[32,32,128]{2,1,0:T(8,128)(2,1)S(1)}, u32[]{:S(2)}, u32[]{:S(2)}) async-start(bf16[32,32,128]{2,1,0:T(8,128)(2,1)} %bitcast), calls=%async_computation | async-start | bytes 524288 | tf_op jit(solution)/shard_map/all_to_all | solution.py:134
  9.3 29.9 %collective-permute-start = (bf16[1,1024,896]{2,1,0:T(8,128)(2,1)}, bf16[1,1024,896]{2,1,0:T(8,128)(2,1)}, u32[]{:S(2)}, u32[]{:S(2)}) collective-permute-start(bf16[1,1024,896]{2,1,0:T(8,128)(2,1)} %refs_0_.3), channel_id=1, source_target_pairs={{0,1},{1,0},{2,3},{3,2},{4,5},{5,4},{6,7},{7,6},{8,9},{9,8},{10,11... | collective-permute-start | bytes 5505032 | tf_op jit(solution)/shard_map/ppermute | solution.py:295
  9.6 29.6 %collective-permute-start.1 = (bf16[1,1024,896]{2,1,0:T(8,128)(2,1)}, bf16[1,1024,896]{2,1,0:T(8,128)(2,1)}, u32[]{:S(2)}, u32[]{:S(2)}) collective-permute-start(bf16[1,1024,896]{2,1,0:T(8,128)(2,1)} %refs_1_.3), channel_id=1, source_target_pairs={{0,1},{1,0},{2,3},{3,2},{4,5},{5,4},{6,7},{7,6},{8,9},{9,8},{10,11... | collective-permute-start | bytes 5505032 | tf_op jit(solution)/shard_map/ppermute | solution.py:295
  9.9 29.4 %collective-permute-start.2 = (bf16[1,896,1024]{2,1,0:T(8,128)(2,1)}, bf16[1,896,1024]{2,1,0:T(8,128)(2,1)}, u32[]{:S(2)}, u32[]{:S(2)}) collective-permute-start(bf16[1,896,1024]{2,1,0:T(8,128)(2,1)} %refs_2_.3), channel_id=1, source_target_pairs={{0,1},{1,0},{2,3},{3,2},{4,5},{5,4},{6,7},{7,6},{8,9},{9,8},{10,11... | collective-permute-start | bytes 5505032 | tf_op jit(solution)/shard_map/ppermute | solution.py:295
  20.4 14.3 %all-to-all-start.1 = ((bf16[32,40,128]{2,1,0:T(8,128)(2,1)}), bf16[32,40,128]{2,1,0:T(8,128)(2,1)S(1)}, u32[]{:S(2)}, u32[]{:S(2)}) async-start(bf16[32,40,128]{2,1,0:T(8,128)(2,1)} %shard_map.119), calls=%async_computation.1 | async-start | bytes 655360 | tf_op jit(solution)/shard_map/all_to_all | solution.py:148
  36.4 1.6 %collective-permute-start.7 = (bf16[128,1024]{1,0:T(8,128)(2,1)S(1)}, bf16[128,1024]{1,0:T(8,128)(2,1)S(1)}, u32[]{:S(2)}, u32[]{:S(2)}) collective-permute-start(bf16[128,1024]{1,0:T(8,128)(2,1)S(1)} %get-tuple-element.50.rows_ref), channel_id=1, source_target_pairs={{0,1},{1,0},{2,3},{3,2},{4,5},{5,4},{6,7},{7,6},{8,9},{9,8},{10,11... | collective-permute-start | bytes 786440 | tf_op jit(solution)/shard_map/ppermute | solution.py:295
  36.5 7.0 %collective-permute-start.3 = (bf16[128,1024]{1,0:T(8,128)(2,1)S(1)}, bf16[128,1024]{1,0:T(8,128)(2,1)S(1)}, u32[]{:S(2)}, u32[]{:S(2)}) collective-permute-start(bf16[128,1024]{1,0:T(8,128)(2,1)S(1)} %get-tuple-element.50.rows_ref), channel_id=1, source_target_pairs={{0,4},{1,3},{4,8},{5,1},{8,12},{9,5},{12,14},{13,9},{14,10},{15,13... | collective-permute-start | bytes 786440 | tf_op jit(solution)/shard_map/ppermute | solution.py:295
  38.0 7.7 %collective-permute-start.8 = (bf16[128,1024]{1,0:T(8,128)(2,1)S(1)}, bf16[128,1024]{1,0:T(8,128)(2,1)S(1)}, u32[]{:S(2)}, u32[]{:S(2)}) collective-permute-start(bf16[128,1024]{1,0:T(8,128)(2,1)S(1)} %collective-permute-done.7), channel_id=1, source_target_pairs={{0,4},{1,3},{4,8},{5,1},{8,12},{9,5},{12,14},{13,9},{14,10},{15,13... | collective-permute-start | bytes 786440 | tf_op jit(solution)/shard_map/ppermute | solution.py:295
  43.5 6.4 %collective-permute-start.4 = (bf16[128,1024]{1,0:T(8,128)(2,1)S(1)}, bf16[128,1024]{1,0:T(8,128)(2,1)S(1)}, u32[]{:S(2)}, u32[]{:S(2)}) collective-permute-start(bf16[128,1024]{1,0:T(8,128)(2,1)S(1)} %collective-permute-done.3.rows_ref), channel_id=1, source_target_pairs={{0,4},{1,3},{4,8},{5,1},{8,12},{9,5},{12,14},{13,9},{14,10},{15,13... | collective-permute-start | bytes 786440 | tf_op jit(solution)/shard_map/ppermute | solution.py:295
  45.8 7.0 %collective-permute-start.9 = (bf16[128,1024]{1,0:T(8,128)(2,1)S(1)}, bf16[128,1024]{1,0:T(8,128)(2,1)S(1)}, u32[]{:S(2)}, u32[]{:S(2)}) collective-permute-start(bf16[128,1024]{1,0:T(8,128)(2,1)S(1)} %collective-permute-done.8.rows_ref), channel_id=1, source_target_pairs={{0,4},{1,3},{4,8},{5,1},{8,12},{9,5},{12,14},{13,9},{14,10},{15,13... | collective-permute-start | bytes 786440 | tf_op jit(solution)/shard_map/ppermute | solution.py:295
  50.0 6.4 %collective-permute-start.5 = (bf16[128,1024]{1,0:T(8,128)(2,1)S(1)}, bf16[128,1024]{1,0:T(8,128)(2,1)S(1)}, u32[]{:S(2)}, u32[]{:S(2)}) collective-permute-start(bf16[128,1024]{1,0:T(8,128)(2,1)S(1)} %collective-permute-done.4.rows_ref), channel_id=1, source_target_pairs={{0,4},{1,3},{4,8},{5,1},{8,12},{9,5},{12,14},{13,9},{14,10},{15,13... | collective-permute-start | bytes 786440 | tf_op jit(solution)/shard_map/ppermute | solution.py:295
  52.8 6.4 %collective-permute-start.10 = (bf16[128,1024]{1,0:T(8,128)(2,1)S(1)}, bf16[128,1024]{1,0:T(8,128)(2,1)S(1)}, u32[]{:S(2)}, u32[]{:S(2)}) collective-permute-start(bf16[128,1024]{1,0:T(8,128)(2,1)S(1)} %collective-permute-done.9.rows_ref), channel_id=1, source_target_pairs={{0,4},{1,3},{4,8},{5,1},{8,12},{9,5},{12,14},{13,9},{14,10},{15,13... | collective-permute-start | bytes 786440 | tf_op jit(solution)/shard_map/ppermute | solution.py:295
  56.3 6.6 %collective-permute-start.6 = (bf16[128,1024]{1,0:T(8,128)(2,1)S(1)}, bf16[128,1024]{1,0:T(8,128)(2,1)S(1)}, u32[]{:S(2)}, u32[]{:S(2)}) collective-permute-start(bf16[128,1024]{1,0:T(8,128)(2,1)S(1)} %collective-permute-done.5.rows_ref), channel_id=1, source_target_pairs={{0,4},{1,3},{4,8},{5,1},{8,12},{9,5},{12,14},{13,9},{14,10},{15,13... | collective-permute-start | bytes 786440 | tf_op jit(solution)/shard_map/ppermute | solution.py:295
  61.1 7.3 %collective-permute-start.11 = (bf16[128,1024]{1,0:T(8,128)(2,1)S(1)}, bf16[128,1024]{1,0:T(8,128)(2,1)S(1)}, u32[]{:S(2)}, u32[]{:S(2)}) collective-permute-start(bf16[128,1024]{1,0:T(8,128)(2,1)S(1)} %convert_element_type.69), channel_id=1, source_target_pairs={{0,2},{1,5},{4,0},{5,9},{8,4},{9,13},{12,8},{13,15},{14,12},{15,11... | collective-permute-start | bytes 786440 | tf_op jit(solution)/shard_map/ppermute | solution.py:295
  64.9 6.4 %collective-permute-start.15 = (bf16[128,1024]{1,0:T(8,128)(2,1)S(1)}, bf16[128,1024]{1,0:T(8,128)(2,1)S(1)}, u32[]{:S(2)}, u32[]{:S(2)}) collective-permute-start(bf16[128,1024]{1,0:T(8,128)(2,1)S(1)} %convert_element_type.75), channel_id=1, source_target_pairs={{0,2},{1,5},{4,0},{5,9},{8,4},{9,13},{12,8},{13,15},{14,12},{15,11... | collective-permute-start | bytes 786440 | tf_op jit(solution)/shard_map/ppermute | solution.py:295
  68.5 6.4 %collective-permute-start.12 = (bf16[128,1024]{1,0:T(8,128)(2,1)S(1)}, bf16[128,1024]{1,0:T(8,128)(2,1)S(1)}, u32[]{:S(2)}, u32[]{:S(2)}) collective-permute-start(bf16[128,1024]{1,0:T(8,128)(2,1)S(1)} %add_convert_fusion.5), channel_id=1, source_target_pairs={{0,2},{1,5},{4,0},{5,9},{8,4},{9,13},{12,8},{13,15},{14,12},{15,11... | collective-permute-start | bytes 786440 | tf_op jit(solution)/shard_map/ppermute | solution.py:295
  71.4 6.4 %collective-permute-start.16 = (bf16[128,1024]{1,0:T(8,128)(2,1)S(1)}, bf16[128,1024]{1,0:T(8,128)(2,1)S(1)}, u32[]{:S(2)}, u32[]{:S(2)}) collective-permute-start(bf16[128,1024]{1,0:T(8,128)(2,1)S(1)} %add_convert_fusion.3), channel_id=1, source_target_pairs={{0,2},{1,5},{4,0},{5,9},{8,4},{9,13},{12,8},{13,15},{14,12},{15,11... | collective-permute-start | bytes 786440 | tf_op jit(solution)/shard_map/ppermute | solution.py:295
  75.0 6.4 %collective-permute-start.13 = (bf16[128,1024]{1,0:T(8,128)(2,1)S(1)}, bf16[128,1024]{1,0:T(8,128)(2,1)S(1)}, u32[]{:S(2)}, u32[]{:S(2)}) collective-permute-start(bf16[128,1024]{1,0:T(8,128)(2,1)S(1)} %add_convert_fusion.4), channel_id=1, source_target_pairs={{0,2},{1,5},{4,0},{5,9},{8,4},{9,13},{12,8},{13,15},{14,12},{15,11... | collective-permute-start | bytes 786440 | tf_op jit(solution)/shard_map/ppermute | solution.py:295
  77.8 6.4 %collective-permute-start.17 = (bf16[128,1024]{1,0:T(8,128)(2,1)S(1)}, bf16[128,1024]{1,0:T(8,128)(2,1)S(1)}, u32[]{:S(2)}, u32[]{:S(2)}) collective-permute-start(bf16[128,1024]{1,0:T(8,128)(2,1)S(1)} %add_convert_fusion.2), channel_id=1, source_target_pairs={{0,2},{1,5},{4,0},{5,9},{8,4},{9,13},{12,8},{13,15},{14,12},{15,11... | collective-permute-start | bytes 786440 | tf_op jit(solution)/shard_map/ppermute | solution.py:295
  81.4 5.9 %collective-permute-start.14 = (bf16[128,1024]{1,0:T(8,128)(2,1)S(1)}, bf16[128,1024]{1,0:T(8,128)(2,1)S(1)}, u32[]{:S(2)}, u32[]{:S(2)}) collective-permute-start(bf16[128,1024]{1,0:T(8,128)(2,1)S(1)} %collective-permute-done.13), channel_id=1, source_target_pairs={{0,1},{1,0},{2,3},{3,2},{4,5},{5,4},{6,7},{7,6},{8,9},{9,8},{10,11... | collective-permute-start | bytes 786440 | tf_op jit(solution)/shard_map/ppermute | solution.py:295
  84.3 6.4 %collective-permute-start.18 = (bf16[128,1024]{1,0:T(8,128)(2,1)S(1)}, bf16[128,1024]{1,0:T(8,128)(2,1)S(1)}, u32[]{:S(2)}, u32[]{:S(2)}) collective-permute-start(bf16[128,1024]{1,0:T(8,128)(2,1)S(1)} %add_convert_fusion.1), channel_id=1, source_target_pairs={{0,2},{1,5},{4,0},{5,9},{8,4},{9,13},{12,8},{13,15},{14,12},{15,11... | collective-permute-start | bytes 786440 | tf_op jit(solution)/shard_map/ppermute | solution.py:295

commit v6 on v5

--- a/solution.py
+++ b/solution.py
@@ -14,6 +14,7 @@
 BF16 = jnp.bfloat16
 VMEM = pl.BlockSpec(memory_space=pltpu.VMEM)
 HBM = pl.BlockSpec(memory_space=pltpu.HBM)
+EARLY = 5
 LIMIT = 16 * 1024 * 1024
 
 
@@ -187,13 +188,15 @@
     routed_ref[...] = rms(mixed, moe_gain_ref[...]).astype(BF16)
 
 
-def expert_kernel(chips, offset, flip, experts, dense, rows_ref, *refs):
-    count = 3 * len(experts) if len(refs) < 13 else 6
-    weights, out_ref, refs = refs[:count], refs[count], refs[count + 1 :]
-    copies = []
-    if refs:
-        copies = copies_of(weights, refs[:6], refs[6])
-        weights = refs[:6]
+def expert_kernel(chips, offset, flip, experts, staged, dense, rows_ref, *refs):
+    count = len(refs) - 1 - (len(staged) + 1 if staged else 0)
+    weights, out_ref, refs = list(refs[:count]), refs[count], refs[count + 1 :]
+    waiting = {}
+    if staged:
+        copies = copies_of([weights[i] for i in staged], refs[:-1], refs[-1])
+        waiting = dict(zip(staged, copies))
+        for i, ref in zip(staged, refs):
+            weights[i] = ref
     me = lax.axis_index("ctx")
     core, chip = me % 2, me // 2
     place = jnp.where(chip % 2 == 0, chip // 2, chips - 1 - chip // 2)
@@ -206,8 +209,9 @@
     total = jnp.zeros(rows.shape, F32)
     for i, which in enumerate(experts):
         w_gate, w_up, w_down = weights[3 * i : 3 * i + 3]
-        for copy in copies[3 * i : 3 * i + 3]:
-            copy.wait()
+        for j in range(3 * i, 3 * i + 3):
+            if j in waiting:
+                waiting.pop(j).wait()
         gate = jnp.dot(rows, w_gate[0], preferred_element_type=F32)
         upper = jnp.dot(rows, w_up[0], preferred_element_type=F32)
         inner = (gate / (1.0 + jnp.exp(-gate)) * upper).astype(BF16)
@@ -215,19 +219,20 @@
         picked = jnp.where(lane == which * 2 * chips + source, table, 0.0)
         total += result * jnp.sum(picked, axis=1, keepdims=True)
     out_ref[...] = total
-    for copy in copies[3 * len(experts) :]:
-        copy.wait()
-
-
-def expert(rows, chips, offset, flip, dense, weights, experts=(0, 1), staging=False):
+    for copy in waiting.values():
+        copy.wait()
+
+
+def expert(rows, chips, offset, flip, dense, weights, experts=(0, 1), staged=()):
     outs = [jax.ShapeDtypeStruct(rows.shape, F32)]
     specs, scratch = [VMEM] * len(weights), []
-    if staging:
-        outs += [pltpu.VMEM(w.shape, w.dtype) for w in weights]
-        specs, scratch = [HBM] * 6, [pltpu.SemaphoreType.DMA((6,))]
-        weights = [in_hbm(w) for w in weights]
+    if staged:
+        outs += [pltpu.VMEM(weights[i].shape, weights[i].dtype) for i in staged]
+        specs = [HBM if i in staged else VMEM for i in range(len(weights))]
+        weights = [in_hbm(w) if i in staged else w for i, w in enumerate(weights)]
+        scratch = [pltpu.SemaphoreType.DMA((len(staged),))]
     return pl.pallas_call(
-        functools.partial(expert_kernel, chips, offset, flip, experts),
+        functools.partial(expert_kernel, chips, offset, flip, experts, staged),
         out_shape=outs,
         in_specs=[VMEM] * 2 + specs,
         out_specs=[VMEM] * len(outs),
@@ -297,7 +302,9 @@
     weights = [w_gate, w_up, w_down]
     weights += [send(w, swap) for w in weights]
     here = [send(routed, ring), send(send(routed, swap), ring)]
-    home_own, *weights = expert(routed, chips, 0, 0, dense, weights, (0,), True)
+    early = tuple(range(EARLY))
+    home_own, *held = expert(routed, chips, 0, 0, dense, weights[:EARLY], (0,), early)
+    weights = held + weights[EARLY:]
     done, ready = {}, [home_own, home_own]
     for step in range(1, far):
         passed = []
@@ -307,7 +314,11 @@
             if step + 1 < far or chain == 0:
                 here[chain] = send(rows, ring)
             if step + 1 < far or chain:
-                (done[chain, step],) = expert(rows, chips, step, chain, dense, weights)
+                late_ones = () if done else tuple(range(EARLY, 6))
+                done[chain, step], *held = expert(
+                    rows, chips, step, chain, dense, weights, (0, 1), late_ones
+                )
+                weights = weights[: len(weights) - len(held)] + held
                 ready[chain] = done[chain, step]
             else:
                 late = rows
@@ -324,12 +335,14 @@
             if (chain, step) in done:
                 total = done[chain, step]
                 if moving[chain] is not None:
-                    total = total + moving[chain]
-                moving[chain] = send(total.astype(BF16), back).astype(F32)
-    home = mixed + home_own + home_other
+                    total = total + moving[chain].astype(F32)
+                total = total.astype(BF16)
+                moving[chain] = send(total, back)
+    home = mixed + home_own + home_other + moving[0].astype(F32)
     if far > 1:
-        home = home + send(moving[1].astype(BF16), swap).astype(F32)
-    return (home + moving[0]).astype(BF16)
+        other = send(moving[1], swap)
+        home = home + hold(other, moving[0]).astype(F32)
+    return home.astype(BF16)
 
 
 def solution(mesh):

time: 92 us -> 91.3 us (level)
  waiting for transfers between devices: 31.2 us -> 28.1 us
  starting transfers between devices: 29.2 us -> 31.5 us
    ppermute x19, waiting for transfers between devices: 16.4 us -> 13.3 us  [send(): return lax.ppermute(rows, 'ctx', way)]
    ppermute x19, starting transfers between devices: 19.3 us -> 21.6 us  [send(): return lax.ppermute(rows, 'ctx', way)]
  transfers between devices with their start and end apart: 21 -> 21, of which waited for: 15 -> 14; matrix products, arithmetic and copies ran while one was open for 3% -> 3% of each run, Pallas kernels for 28% -> 28%
where the time goes in v6:
time: 91.3 us; the launch traced here: 90.9 us
  starting transfers between devices  31.5 us (35%)
  waiting for transfers between devices  28.1 us (31%)
  Pallas kernels  27.5 us (30%)
  other arithmetic  3.41 us (4%)
    ppermute x19, starting transfers between devices, send(): return lax.ppermute(rows, 'ctx', way)  21.6 us
    pallas_call x9, Pallas kernels, expert(): pl.pallas_call(functools.partial(expert_kernel, chips, offset, flip, expe...  18.8 us
    ppermute x19, waiting for transfers between devices, send(): return lax.ppermute(rows, 'ctx', way)  13.3 us
    all_to_all x1, waiting for transfers between devices, scan_states(): sums = lax.all_to_all(sums, BOTH, split_axis=0, concat_axis=0, tiled=True)  7.56 us
    all_to_all x1, starting transfers between devices, scan_states(): lax.all_to_all(pieces, BOTH, split_axis=0, concat_axis=0, tiled=True)  7.3 us
    all_to_all x1, waiting for transfers between devices, scan_states(): lax.all_to_all(pieces, BOTH, split_axis=0, concat_axis=0, tiled=True)  7.25 us
    pallas_call x1, Pallas kernels, attend_inside(): pl.pallas_call(functools.partial(inside_kernel, count), out_shape=outs, i...  4.12 us
    all_to_all x1, starting transfers between devices, scan_states(): sums = lax.all_to_all(sums, BOTH, split_axis=0, concat_axis=0, tiled=True)  2.59 us
  transfers between devices with their start and end apart: 21, of which 14 were waited for; matrix products, arithmetic and copies ran while one was open for 3% of the time, Pallas kernels for 28%

profile of v6, /device:TPU:0, one launch (start us, length us, event | category | flops | bytes accessed | tf_op | source)
XLA Modules:
  0.0 90.9 jit_solution(12719616657443093539)
XLA Ops:
  0.0 2.0 %shard_map.118.refs_6_ = bf16[1024,128]{1,0:T(8,128)(2,1)} custom-call(bf16[128,1024]{1,0:T(8,128)(2,1)} %refs_1_.2, bf16[128,1024]{1,0:T(8,128)(2,1)} %refs_2_.2), custom_call_target="tpu_custom_call" | custom-call | tf_op jit(solution)/shard_map/pallas_call | solution.py:263
  2.0 7.3 %all-to-all-start = ((bf16[32,32,128]{2,1,0:T(8,128)(2,1)}), bf16[32,32,128]{2,1,0:T(8,128)(2,1)S(1)}, u32[]{:S(2)}, u32[]{:S(2)}) async-start(bf16[32,32,128]{2,1,0:T(8,128)(2,1)} %bitcast), calls=%async_computation | async-start | bytes 524288 | tf_op jit(solution)/shard_map/all_to_all | solution.py:135
  9.3 0.3 collective-permute-start
  9.6 0.3 collective-permute-start.1
  9.9 0.3 collective-permute-start.4
  10.2 0.7 convert_reduce_fusion
  10.9 0.7 convert_divide_fusion
  11.6 0.7 select_reduce_fusion
  12.4 7.3 %all-to-all-done.pieces_ref = bf16[32,32,128]{2,1,0:T(8,128)(2,1)S(1)} async-done(((bf16[32,32,128]{2,1,0:T(8,128)(2,1)}), bf16[32,32,128]{2,1,0:T(8,128)(2,1)S(1)}, u32[]{:S(2)}, u32[]{:S(2)}) %all-to-all-start) | async-done | bytes 262176 | tf_op jit(solution)/shard_map/all_to_all | solution.py:135
  19.6 0.8 shard_map.119
  20.4 2.6 %all-to-all-start.1 = ((bf16[32,40,128]{2,1,0:T(8,128)(2,1)}), bf16[32,40,128]{2,1,0:T(8,128)(2,1)S(1)}, u32[]{:S(2)}, u32[]{:S(2)}) async-start(bf16[32,40,128]{2,1,0:T(8,128)(2,1)} %shard_map.119), calls=%async_computation.1 | async-start | bytes 655360 | tf_op jit(solution)/shard_map/all_to_all | solution.py:149
  23.0 4.1 %shard_map.120 = (bf16[128,1024]{1,0:T(8,128)(2,1)S(1)}, bf16[128,1024]{1,0:T(8,128)(2,1)}, bf16[128,1024]{1,0:T(8,128)(2,1)}, bf16[1024,1024]{1,0:T(8,128)(2,1)...) custom-call(bf16[128,1024]{1,0:T(8,128)(2,1)} %refs_0_.2, bf16[128,1024]{1,0:T(8,128)(2,1)} %refs_1_.2, ...), custom_call_target="tpu_custom_call" | custom-call | tf_op jit(solution)/shard_map/pallas_call | solution.py:102
  27.1 7.6 %all-to-all-done.1.sums_ref = bf16[32,40,128]{2,1,0:T(8,128)(2,1)S(1)} async-done(((bf16[32,40,128]{2,1,0:T(8,128)(2,1)}), bf16[32,40,128]{2,1,0:T(8,128)(2,1)S(1)}, u32[]{:S(2)}, u32[]{:S(2)}) %all-to-all-start.1) | async-done | bytes 327712 | tf_op jit(solution)/shard_map/all_to_all | solution.py:149
  34.7 1.8 %shard_map.121 = (f32[128,1024]{1,0:T(8,128)S(1)}, bf16[128,1024]{1,0:T(8,128)(2,1)S(1)}) custom-call(bf16[32,40,128]{2,1,0:T(8,128)(2,1)S(1)} %all-to-all-done.1.sums_ref, bf16[128,1024]{1,0:T(8,128)(2,1)S(1)} %get-tuple-element.30.q_ref, bf16[1024,1024]{1,0:T(8,128)(2,1)S(1)} %get-tuple-element.31.proj_ref, f32[1,1024]{1,0:T(1,128)S(1)} %get-tuple-element.32.gain_ref, ...), custom_call_target="tpu_custom_call" | custom-call | tf_op jit(solution)/shard_map/pallas_call | solution.py:283
  36.4 0.1 collective-permute-start.7
  36.5 1.1 %collective-permute-start.2 = (bf16[128,1024]{1,0:T(8,128)(2,1)S(1)}, bf16[128,1024]{1,0:T(8,128)(2,1)S(1)}, u32[]{:S(2)}, u32[]{:S(2)}) collective-permute-start(bf16[128,1024]{1,0:T(8,128)(2,1)S(1)} %get-tuple-element.53.rows_ref), channel_id=1, source_target_pairs={{0,4},{1,3},{4,8},{5,1},{8,12},{9,5},{12,14},{13,9},{14,10},{15,13... | collective-permute-start | bytes 786440 | tf_op jit(solution)/shard_map/ppermute | solution.py:300
  37.7 0.4 collective-permute-done.7
  38.1 1.0 %collective-permute-start.8 = (bf16[128,1024]{1,0:T(8,128)(2,1)S(1)}, bf16[128,1024]{1,0:T(8,128)(2,1)S(1)}, u32[]{:S(2)}, u32[]{:S(2)}) collective-permute-start(bf16[128,1024]{1,0:T(8,128)(2,1)S(1)} %collective-permute-done.7), channel_id=1, source_target_pairs={{0,4},{1,3},{4,8},{5,1},{8,12},{9,5},{12,14},{13,9},{14,10},{15,13... | collective-permute-start | bytes 786440 | tf_op jit(solution)/shard_map/ppermute | solution.py:300
  39.1 0.1 copy.29
  39.2 0.0 collective-permute-done.refs_3_
  39.2 0.0 collective-permute-done.1.refs_4_
  39.2 3.7 %shard_map.122 = (f32[128,1024]{1,0:T(8,128)S(1)}, bf16[1,1024,896]{2,1,0:T(8,128)(2,1)S(1)}, bf16[1,1024,896]{2,1,0:T(8,128)(2,1)S(1)}, bf16[1,896,1024]{2,1,0:...) custom-call(f32[128,32]{1,0:T(8,128)S(1)} %bitcast.24, ...), custom_call_target="tpu_custom_call" | custom-call | tf_op jit(solution)/shard_map/pallas_call | solution.py:234
  43.0 0.0 collective-permute-done.2.rows_ref
  43.0 1.0 %collective-permute-start.3 = (bf16[128,1024]{1,0:T(8,128)(2,1)S(1)}, bf16[128,1024]{1,0:T(8,128)(2,1)S(1)}, u32[]{:S(2)}, u32[]{:S(2)}) collective-permute-start(bf16[128,1024]{1,0:T(8,128)(2,1)S(1)} %collective-permute-done.2.rows_ref), channel_id=1, source_target_pairs={{0,4},{1,3},{4,8},{5,1},{8,12},{9,5},{12,14},{13,9},{14,10},{15,13... | collective-permute-start | bytes 786440 | tf_op jit(solution)/shard_map/ppermute | solution.py:300
  44.0 1.8 %collective-permute-done.8.rows_ref = bf16[128,1024]{1,0:T(8,128)(2,1)S(1)} collective-permute-done((bf16[128,1024]{1,0:T(8,128)(2,1)S(1)}, bf16[128,1024]{1,0:T(8,128)(2,1)S(1)}, u32[]{:S(2)}, u32[]{:S(2)}) %collective-permute-start.8) | collective-permute-done | bytes 262176 | tf_op jit(solution)/shard_map/ppermute | solution.py:300
  45.8 1.0 %collective-permute-start.9 = (bf16[128,1024]{1,0:T(8,128)(2,1)S(1)}, bf16[128,1024]{1,0:T(8,128)(2,1)S(1)}, u32[]{:S(2)}, u32[]{:S(2)}) collective-permute-start(bf16[128,1024]{1,0:T(8,128)(2,1)S(1)} %collective-permute-done.8.rows_ref), channel_id=1, source_target_pairs={{0,4},{1,3},{4,8},{5,1},{8,12},{9,5},{12,14},{13,9},{14,10},{15,13... | collective-permute-start | bytes 786440 | tf_op jit(solution)/shard_map/ppermute | solution.py:300
  46.8 0.0 collective-permute-done.4.refs_5_
  46.8 2.6 %shard_map.123 = (f32[128,1024]{1,0:T(8,128)S(1)}, bf16[1,896,1024]{2,1,0:T(8,128)(2,1)S(1)}) custom-call(f32[128,32]{1,0:T(8,128)S(1)} %bitcast.25, bf16[128,1024]{1,0:T(8,128)(2,1)S(1)} %collective-permute-done.2.rows_ref, bf16[1,1024,896]{2,1,0:T(8,128)(2,1)S(1)} %get-tuple-element.39.refs_0_, bf16[1,1024,896]{2,1,0:T(8,128)(2,1)S(1)} %get-tuple-element.40.refs_1_, ...), custom_call_target="tpu_custom_call" | custom-call | tf_op jit(solution)/shard_map/pallas_call | solution.py:234
  49.4 0.0 collective-permute-done.3.rows_ref
  49.4 1.0 %collective-permute-start.5 = (bf16[128,1024]{1,0:T(8,128)(2,1)S(1)}, bf16[128,1024]{1,0:T(8,128)(2,1)S(1)}, u32[]{:S(2)}, u32[]{:S(2)}) collective-permute-start(bf16[128,1024]{1,0:T(8,128)(2,1)S(1)} %collective-permute-done.3.rows_ref), channel_id=1, source_target_pairs={{0,4},{1,3},{4,8},{5,1},{8,12},{9,5},{12,14},{13,9},{14,10},{15,13... | collective-permute-start | bytes 786440 | tf_op jit(solution)/shard_map/ppermute | solution.py:300
  50.4 1.9 %shard_map.125 = f32[128,1024]{1,0:T(8,128)S(1)} custom-call(f32[128,32]{1,0:T(8,128)S(1)} %bitcast.26, bf16[128,1024]{1,0:T(8,128)(2,1)S(1)} %collective-permute-done.8.rows_ref, bf16[1,1024,896]{2,1,0:T(8,128)(2,1)S(1)} %get-tuple-element.39.refs_0_, bf16[1,1024,896]{2,1,0:T(8,128)(2,1)S(1)} %get-tuple-element.40.refs_1_, ...), custom_call_target="tpu_custom_call" | custom-call | tf_op jit(solution)/shard_map/pallas_call | solution.py:234
  52.3 0.0 collective-permute-done.9.rows_ref
  52.3 1.1 %collective-permute-start.10 = (bf16[128,1024]{1,0:T(8,128)(2,1)S(1)}, bf16[128,1024]{1,0:T(8,128)(2,1)S(1)}, u32[]{:S(2)}, u32[]{:S(2)}) collective-permute-start(bf16[128,1024]{1,0:T(8,128)(2,1)S(1)} %collective-permute-done.9.rows_ref), channel_id=1, source_target_pairs={{0,4},{1,3},{4,8},{5,1},{8,12},{9,5},{12,14},{13,9},{14,10},{15,13... | collective-permute-start | bytes 786440 | tf_op jit(solution)/shard_map/ppermute | solution.py:300
  53.4 1.9 %shard_map.124 = f32[128,1024]{1,0:T(8,128)S(1)} custom-call(f32[128,32]{1,0:T(8,128)S(1)} %bitcast.27, bf16[128,1024]{1,0:T(8,128)(2,1)S(1)} %collective-permute-done.3.rows_ref, bf16[1,1024,896]{2,1,0:T(8,128)(2,1)S(1)} %get-tuple-element.39.refs_0_, bf16[1,1024,896]{2,1,0:T(8,128)(2,1)S(1)} %get-tuple-element.40.refs_1_, ...), custom_call_target="tpu_custom_call" | custom-call | tf_op jit(solution)/shard_map/pallas_call | solution.py:234
  55.3 0.5 collective-permute-done.5.rows_ref
  55.8 0.9 %collective-permute-start.6 = (bf16[128,1024]{1,0:T(8,128)(2,1)S(1)}, bf16[128,1024]{1,0:T(8,128)(2,1)S(1)}, u32[]{:S(2)}, u32[]{:S(2)}) collective-permute-start(bf16[128,1024]{1,0:T(8,128)(2,1)S(1)} %collective-permute-done.5.rows_ref), channel_id=1, source_target_pairs={{0,4},{1,3},{4,8},{5,1},{8,12},{9,5},{12,14},{13,9},{14,10},{15,13... | collective-permute-start | bytes 786440 | tf_op jit(solution)/shard_map/ppermute | solution.py:300
  56.7 1.9 %shard_map.126 = f32[128,1024]{1,0:T(8,128)S(1)} custom-call(f32[128,32]{1,0:T(8,128)S(1)} %bitcast.28, bf16[128,1024]{1,0:T(8,128)(2,1)S(1)} %collective-permute-done.9.rows_ref, bf16[1,1024,896]{2,1,0:T(8,128)(2,1)S(1)} %get-tuple-element.39.refs_0_, bf16[1,1024,896]{2,1,0:T(8,128)(2,1)S(1)} %get-tuple-element.40.refs_1_, ...), custom_call_target="tpu_custom_call" | custom-call | tf_op jit(solution)/shard_map/pallas_call | solution.py:234
  58.7 0.1 collective-permute-done.10.rows_ref
  58.7 1.9 %shard_map.127 = f32[128,1024]{1,0:T(8,128)S(1)} custom-call(f32[128,32]{1,0:T(8,128)S(1)} %bitcast.29, bf16[128,1024]{1,0:T(8,128)(2,1)S(1)} %collective-permute-done.10.rows_ref, bf16[1,1024,896]{2,1,0:T(8,128)(2,1)S(1)} %get-tuple-element.39.refs_0_, bf16[1,1024,896]{2,1,0:T(8,128)(2,1)S(1)} %get-tuple-element.40.refs_1_, ...), custom_call_target="tpu_custom_call" | custom-call | tf_op jit(solution)/shard_map/pallas_call | solution.py:234
  60.7 1.3 %collective-permute-start.15 = (bf16[128,1024]{1,0:T(8,128)(2,1)S(1)}, bf16[128,1024]{1,0:T(8,128)(2,1)S(1)}, u32[]{:S(2)}, u32[]{:S(2)}) collective-permute-start(bf16[128,1024]{1,0:T(8,128)(2,1)S(1)} %convert_element_type.75), channel_id=1, source_target_pairs={{0,2},{1,5},{4,0},{5,9},{8,4},{9,13},{12,8},{13,15},{14,12},{15,11... | collective-permute-start | bytes 786440 | tf_op jit(solution)/shard_map/ppermute | solution.py:300
  62.0 0.2 collective-permute-done.6.rows_ref
  62.2 1.9 %shard_map.128 = f32[128,1024]{1,0:T(8,128)S(1)} custom-call(f32[128,32]{1,0:T(8,128)S(1)} %bitcast.30, bf16[128,1024]{1,0:T(8,128)(2,1)S(1)} %collective-permute-done.6.rows_ref, bf16[1,1024,896]{2,1,0:T(8,128)(2,1)S(1)} %get-tuple-element.39.refs_0_, bf16[1,1024,896]{2,1,0:T(8,128)(2,1)S(1)} %get-tuple-element.40.refs_1_, ...), custom_call_target="tpu_custom_call" | custom-call | tf_op jit(solution)/shard_map/pallas_call | solution.py:234
  64.2 2.2 %collective-permute-start.11 = (bf16[128,1024]{1,0:T(8,128)(2,1)S(1)}, bf16[128,1024]{1,0:T(8,128)(2,1)S(1)}, u32[]{:S(2)}, u32[]{:S(2)}) collective-permute-start(bf16[128,1024]{1,0:T(8,128)(2,1)S(1)} %convert_element_type.67), channel_id=1, source_target_pairs={{0,2},{1,5},{4,0},{5,9},{8,4},{9,13},{12,8},{13,15},{14,12},{15,11... | collective-permute-start | bytes 786440 | tf_op jit(solution)/shard_map/ppermute | solution.py:300
  66.4 0.7 collective-permute-done.15
  67.1 0.1 add_convert_fusion.2
  67.2 1.3 %collective-permute-start.16 = (bf16[128,1024]{1,0:T(8,128)(2,1)S(1)}, bf16[128,1024]{1,0:T(8,128)(2,1)S(1)}, u32[]{:S(2)}, u32[]{:S(2)}) collective-permute-start(bf16[128,1024]{1,0:T(8,128)(2,1)S(1)} %add_convert_fusion.2), channel_id=1, source_target_pairs={{0,2},{1,5},{4,0},{5,9},{8,4},{9,13},{12,8},{13,15},{14,12},{15,11... | collective-permute-start | bytes 786440 | tf_op jit(solution)/shard_map/ppermute | solution.py:300
  68.5 1.9 %shard_map.129 = f32[128,1024]{1,0:T(8,128)S(1)} custom-call(f32[128,32]{1,0:T(8,128)S(1)} %bitcast.31, bf16[128,1024]{1,0:T(8,128)(2,1)S(1)} %collective-permute-done.5.rows_ref, bf16[1,1024,896]{2,1,0:T(8,128)(2,1)S(1)} %get-tuple-element.39.refs_0_, bf16[1,1024,896]{2,1,0:T(8,128)(2,1)S(1)} %get-tuple-element.40.refs_1_, ...), custom_call_target="tpu_custom_call" | custom-call | tf_op jit(solution)/shard_map/pallas_call | solution.py:234
  70.4 0.2 collective-permute-done.11
  70.6 0.1 add_convert_fusion.5
  70.6 2.2 %collective-permute-start.12 = (bf16[128,1024]{1,0:T(8,128)(2,1)S(1)}, bf16[128,1024]{1,0:T(8,128)(2,1)S(1)}, u32[]{:S(2)}, u32[]{:S(2)}) collective-permute-start(bf16[128,1024]{1,0:T(8,128)(2,1)S(1)} %add_convert_fusion.5), channel_id=1, source_target_pairs={{0,2},{1,5},{4,0},{5,9},{8,4},{9,13},{12,8},{13,15},{14,12},{15,11... | collective-permute-start | bytes 786440 | tf_op jit(solution)/shard_map/ppermute | solution.py:300
  72.9 0.7 collective-permute-done.16
  73.6 0.1 add_convert_fusion.1
  73.7 2.0 %collective-permute-start.17 = (bf16[128,1024]{1,0:T(8,128)(2,1)S(1)}, bf16[128,1024]{1,0:T(8,128)(2,1)S(1)}, u32[]{:S(2)}, u32[]{:S(2)}) collective-permute-start(bf16[128,1024]{1,0:T(8,128)(2,1)S(1)} %add_convert_fusion.1), channel_id=1, source_target_pairs={{0,2},{1,5},{4,0},{5,9},{8,4},{9,13},{12,8},{13,15},{14,12},{15,11... | collective-permute-start | bytes 786440 | tf_op jit(solution)/shard_map/ppermute | solution.py:300
  75.7 1.4 %collective-permute-done.12 = bf16[128,1024]{1,0:T(8,128)(2,1)S(1)} collective-permute-done((bf16[128,1024]{1,0:T(8,128)(2,1)S(1)}, bf16[128,1024]{1,0:T(8,128)(2,1)S(1)}, u32[]{:S(2)}, u32[]{:S(2)}) %collective-permute-start.12) | collective-permute-done | bytes 262176 | tf_op jit(solution)/shard_map/ppermute | solution.py:300
  77.1 0.1 add_convert_fusion.4
  77.1 2.2 %collective-permute-start.13 = (bf16[128,1024]{1,0:T(8,128)(2,1)S(1)}, bf16[128,1024]{1,0:T(8,128)(2,1)S(1)}, u32[]{:S(2)}, u32[]{:S(2)}) collective-permute-start(bf16[128,1024]{1,0:T(8,128)(2,1)S(1)} %add_convert_fusion.4), channel_id=1, source_target_pairs={{0,2},{1,5},{4,0},{5,9},{8,4},{9,13},{12,8},{13,15},{14,12},{15,11... | collective-permute-start | bytes 786440 | tf_op jit(solution)/shard_map/ppermute | solution.py:300
  79.4 0.7 collective-permute-done.17
  80.1 3.5 %collective-permute-done.13 = bf16[128,1024]{1,0:T(8,128)(2,1)S(1)} collective-permute-done((bf16[128,1024]{1,0:T(8,128)(2,1)S(1)}, bf16[128,1024]{1,0:T(8,128)(2,1)S(1)}, u32[]{:S(2)}, u32[]{:S(2)}) %collective-permute-start.13) | collective-permute-done | bytes 262176 | tf_op jit(solution)/shard_map/ppermute | solution.py:300
  83.6 0.1 add_convert_fusion.3
  83.6 2.2 %collective-permute-start.14 = (bf16[128,1024]{1,0:T(8,128)(2,1)S(1)}, bf16[128,1024]{1,0:T(8,128)(2,1)S(1)}, u32[]{:S(2)}, u32[]{:S(2)}) collective-permute-start(bf16[128,1024]{1,0:T(8,128)(2,1)S(1)} %add_convert_fusion.3), channel_id=1, source_target_pairs={{0,2},{1,5},{4,0},{5,9},{8,4},{9,13},{12,8},{13,15},{14,12},{15,11... | collective-permute-start | bytes 786440 | tf_op jit(solution)/shard_map/ppermute | solution.py:300
  85.8 1.0 %shard_map.130 = f32[128,1024]{1,0:T(8,128)S(1)} custom-call(f32[128,32]{1,0:T(8,128)S(1)} %bitcast.32, bf16[128,1024]{1,0:T(8,128)(2,1)S(1)} %get-tuple-element.53.rows_ref, bf16[1,1024,896]{2,1,0:T(8,128)(2,1)S(1)} %get-tuple-element.42.refs_3_.refs_0_, bf16[1,1024,896]{2,1,0:T(8,128)(2,1)S(1)} %get-tuple-element.43.refs_4_.refs_1_, ...), custom_call_target="tpu_custom_call" | custom-call | tf_op jit(solution)/shard_map/pallas_call | solution.py:234
  86.9 0.0 collective-permute-done.18
  86.9 3.1 %collective-permute-done.14 = bf16[128,1024]{1,0:T(8,128)(2,1)S(1)} collective-permute-done((bf16[128,1024]{1,0:T(8,128)(2,1)S(1)}, bf16[128,1024]{1,0:T(8,128)(2,1)S(1)}, u32[]{:S(2)}, u32[]{:S(2)}) %collective-permute-start.14) | collective-permute-done | bytes 262176 | tf_op jit(solution)/shard_map/ppermute | solution.py:300
  90.0 0.9 add_convert_fusion
  (12 shorter events, 0.2 us)
Async XLA Ops:
  2.0 17.6 %all-to-all-start = ((bf16[32,32,128]{2,1,0:T(8,128)(2,1)}), bf16[32,32,128]{2,1,0:T(8,128)(2,1)S(1)}, u32[]{:S(2)}, u32[]{:S(2)}) async-start(bf16[32,32,128]{2,1,0:T(8,128)(2,1)} %bitcast), calls=%async_computation | async-start | bytes 524288 | tf_op jit(solution)/shard_map/all_to_all | solution.py:135
  9.3 29.9 %collective-permute-start = (bf16[1,1024,896]{2,1,0:T(8,128)(2,1)}, bf16[1,1024,896]{2,1,0:T(8,128)(2,1)}, u32[]{:S(2)}, u32[]{:S(2)}) collective-permute-start(bf16[1,1024,896]{2,1,0:T(8,128)(2,1)} %refs_0_.3), channel_id=1, source_target_pairs={{0,1},{1,0},{2,3},{3,2},{4,5},{5,4},{6,7},{7,6},{8,9},{9,8},{10,11... | collective-permute-start | bytes 5505032 | tf_op jit(solution)/shard_map/ppermute | solution.py:300
  9.6 29.6 %collective-permute-start.1 = (bf16[1,1024,896]{2,1,0:T(8,128)(2,1)}, bf16[1,1024,896]{2,1,0:T(8,128)(2,1)}, u32[]{:S(2)}, u32[]{:S(2)}) collective-permute-start(bf16[1,1024,896]{2,1,0:T(8,128)(2,1)} %refs_1_.3), channel_id=1, source_target_pairs={{0,1},{1,0},{2,3},{3,2},{4,5},{5,4},{6,7},{7,6},{8,9},{9,8},{10,11... | collective-permute-start | bytes 5505032 | tf_op jit(solution)/shard_map/ppermute | solution.py:300
  9.9 36.9 %collective-permute-start.4 = (bf16[1,896,1024]{2,1,0:T(8,128)(2,1)}, bf16[1,896,1024]{2,1,0:T(8,128)(2,1)}, u32[]{:S(2)}, u32[]{:S(2)}) collective-permute-start(bf16[1,896,1024]{2,1,0:T(8,128)(2,1)} %refs_2_.3), channel_id=1, source_target_pairs={{0,1},{1,0},{2,3},{3,2},{4,5},{5,4},{6,7},{7,6},{8,9},{9,8},{10,11... | collective-permute-start | bytes 5505032 | tf_op jit(solution)/shard_map/ppermute | solution.py:300
  20.4 14.3 %all-to-all-start.1 = ((bf16[32,40,128]{2,1,0:T(8,128)(2,1)}), bf16[32,40,128]{2,1,0:T(8,128)(2,1)S(1)}, u32[]{:S(2)}, u32[]{:S(2)}) async-start(bf16[32,40,128]{2,1,0:T(8,128)(2,1)} %shard_map.119), calls=%async_computation.1 | async-start | bytes 655360 | tf_op jit(solution)/shard_map/all_to_all | solution.py:149
  36.4 1.6 %collective-permute-start.7 = (bf16[128,1024]{1,0:T(8,128)(2,1)S(1)}, bf16[128,1024]{1,0:T(8,128)(2,1)S(1)}, u32[]{:S(2)}, u32[]{:S(2)}) collective-permute-start(bf16[128,1024]{1,0:T(8,128)(2,1)S(1)} %get-tuple-element.53.rows_ref), channel_id=1, source_target_pairs={{0,1},{1,0},{2,3},{3,2},{4,5},{5,4},{6,7},{7,6},{8,9},{9,8},{10,11... | collective-permute-start | bytes 786440 | tf_op jit(solution)/shard_map/ppermute | solution.py:300
  36.5 6.5 %collective-permute-start.2 = (bf16[128,1024]{1,0:T(8,128)(2,1)S(1)}, bf16[128,1024]{1,0:T(8,128)(2,1)S(1)}, u32[]{:S(2)}, u32[]{:S(2)}) collective-permute-start(bf16[128,1024]{1,0:T(8,128)(2,1)S(1)} %get-tuple-element.53.rows_ref), channel_id=1, source_target_pairs={{0,4},{1,3},{4,8},{5,1},{8,12},{9,5},{12,14},{13,9},{14,10},{15,13... | collective-permute-start | bytes 786440 | tf_op jit(solution)/shard_map/ppermute | solution.py:300
  38.1 7.7 %collective-permute-start.8 = (bf16[128,1024]{1,0:T(8,128)(2,1)S(1)}, bf16[128,1024]{1,0:T(8,128)(2,1)S(1)}, u32[]{:S(2)}, u32[]{:S(2)}) collective-permute-start(bf16[128,1024]{1,0:T(8,128)(2,1)S(1)} %collective-permute-done.7), channel_id=1, source_target_pairs={{0,4},{1,3},{4,8},{5,1},{8,12},{9,5},{12,14},{13,9},{14,10},{15,13... | collective-permute-start | bytes 786440 | tf_op jit(solution)/shard_map/ppermute | solution.py:300
  43.0 6.4 %collective-permute-start.3 = (bf16[128,1024]{1,0:T(8,128)(2,1)S(1)}, bf16[128,1024]{1,0:T(8,128)(2,1)S(1)}, u32[]{:S(2)}, u32[]{:S(2)}) collective-permute-start(bf16[128,1024]{1,0:T(8,128)(2,1)S(1)} %collective-permute-done.2.rows_ref), channel_id=1, source_target_pairs={{0,4},{1,3},{4,8},{5,1},{8,12},{9,5},{12,14},{13,9},{14,10},{15,13... | collective-permute-start | bytes 786440 | tf_op jit(solution)/shard_map/ppermute | solution.py:300
  45.8 6.5 %collective-permute-start.9 = (bf16[128,1024]{1,0:T(8,128)(2,1)S(1)}, bf16[128,1024]{1,0:T(8,128)(2,1)S(1)}, u32[]{:S(2)}, u32[]{:S(2)}) collective-permute-start(bf16[128,1024]{1,0:T(8,128)(2,1)S(1)} %collective-permute-done.8.rows_ref), channel_id=1, source_target_pairs={{0,4},{1,3},{4,8},{5,1},{8,12},{9,5},{12,14},{13,9},{14,10},{15,13... | collective-permute-start | bytes 786440 | tf_op jit(solution)/shard_map/ppermute | solution.py:300
  49.4 6.4 %collective-permute-start.5 = (bf16[128,1024]{1,0:T(8,128)(2,1)S(1)}, bf16[128,1024]{1,0:T(8,128)(2,1)S(1)}, u32[]{:S(2)}, u32[]{:S(2)}) collective-permute-start(bf16[128,1024]{1,0:T(8,128)(2,1)S(1)} %collective-permute-done.3.rows_ref), channel_id=1, source_target_pairs={{0,4},{1,3},{4,8},{5,1},{8,12},{9,5},{12,14},{13,9},{14,10},{15,13... | collective-permute-start | bytes 786440 | tf_op jit(solution)/shard_map/ppermute | solution.py:300
  52.3 6.4 %collective-permute-start.10 = (bf16[128,1024]{1,0:T(8,128)(2,1)S(1)}, bf16[128,1024]{1,0:T(8,128)(2,1)S(1)}, u32[]{:S(2)}, u32[]{:S(2)}) collective-permute-start(bf16[128,1024]{1,0:T(8,128)(2,1)S(1)} %collective-permute-done.9.rows_ref), channel_id=1, source_target_pairs={{0,4},{1,3},{4,8},{5,1},{8,12},{9,5},{12,14},{13,9},{14,10},{15,13... | collective-permute-start | bytes 786440 | tf_op jit(solution)/shard_map/ppermute | solution.py:300
  55.8 6.4 %collective-permute-start.6 = (bf16[128,1024]{1,0:T(8,128)(2,1)S(1)}, bf16[128,1024]{1,0:T(8,128)(2,1)S(1)}, u32[]{:S(2)}, u32[]{:S(2)}) collective-permute-start(bf16[128,1024]{1,0:T(8,128)(2,1)S(1)} %collective-permute-done.5.rows_ref), channel_id=1, source_target_pairs={{0,4},{1,3},{4,8},{5,1},{8,12},{9,5},{12,14},{13,9},{14,10},{15,13... | collective-permute-start | bytes 786440 | tf_op jit(solution)/shard_map/ppermute | solution.py:300
  60.7 6.4 %collective-permute-start.15 = (bf16[128,1024]{1,0:T(8,128)(2,1)S(1)}, bf16[128,1024]{1,0:T(8,128)(2,1)S(1)}, u32[]{:S(2)}, u32[]{:S(2)}) collective-permute-start(bf16[128,1024]{1,0:T(8,128)(2,1)S(1)} %convert_element_type.75), channel_id=1, source_target_pairs={{0,2},{1,5},{4,0},{5,9},{8,4},{9,13},{12,8},{13,15},{14,12},{15,11... | collective-permute-start | bytes 786440 | tf_op jit(solution)/shard_map/ppermute | solution.py:300
  64.2 6.4 %collective-permute-start.11 = (bf16[128,1024]{1,0:T(8,128)(2,1)S(1)}, bf16[128,1024]{1,0:T(8,128)(2,1)S(1)}, u32[]{:S(2)}, u32[]{:S(2)}) collective-permute-start(bf16[128,1024]{1,0:T(8,128)(2,1)S(1)} %convert_element_type.67), channel_id=1, source_target_pairs={{0,2},{1,5},{4,0},{5,9},{8,4},{9,13},{12,8},{13,15},{14,12},{15,11... | collective-permute-start | bytes 786440 | tf_op jit(solution)/shard_map/ppermute | solution.py:300
  67.2 6.4 %collective-permute-start.16 = (bf16[128,1024]{1,0:T(8,128)(2,1)S(1)}, bf16[128,1024]{1,0:T(8,128)(2,1)S(1)}, u32[]{:S(2)}, u32[]{:S(2)}) collective-permute-start(bf16[128,1024]{1,0:T(8,128)(2,1)S(1)} %add_convert_fusion.2), channel_id=1, source_target_pairs={{0,2},{1,5},{4,0},{5,9},{8,4},{9,13},{12,8},{13,15},{14,12},{15,11... | collective-permute-start | bytes 786440 | tf_op jit(solution)/shard_map/ppermute | solution.py:300
  70.6 6.4 %collective-permute-start.12 = (bf16[128,1024]{1,0:T(8,128)(2,1)S(1)}, bf16[128,1024]{1,0:T(8,128)(2,1)S(1)}, u32[]{:S(2)}, u32[]{:S(2)}) collective-permute-start(bf16[128,1024]{1,0:T(8,128)(2,1)S(1)} %add_convert_fusion.5), channel_id=1, source_target_pairs={{0,2},{1,5},{4,0},{5,9},{8,4},{9,13},{12,8},{13,15},{14,12},{15,11... | collective-permute-start | bytes 786440 | tf_op jit(solution)/shard_map/ppermute | solution.py:300
  73.7 6.4 %collective-permute-start.17 = (bf16[128,1024]{1,0:T(8,128)(2,1)S(1)}, bf16[128,1024]{1,0:T(8,128)(2,1)S(1)}, u32[]{:S(2)}, u32[]{:S(2)}) collective-permute-start(bf16[128,1024]{1,0:T(8,128)(2,1)S(1)} %add_convert_fusion.1), channel_id=1, source_target_pairs={{0,2},{1,5},{4,0},{5,9},{8,4},{9,13},{12,8},{13,15},{14,12},{15,11... | collective-permute-start | bytes 786440 | tf_op jit(solution)/shard_map/ppermute | solution.py:300
  77.1 6.4 %collective-permute-start.13 = (bf16[128,1024]{1,0:T(8,128)(2,1)S(1)}, bf16[128,1024]{1,0:T(8,128)(2,1)S(1)}, u32[]{:S(2)}, u32[]{:S(2)}) collective-permute-start(bf16[128,1024]{1,0:T(8,128)(2,1)S(1)} %add_convert_fusion.4), channel_id=1, source_target_pairs={{0,2},{1,5},{4,0},{5,9},{8,4},{9,13},{12,8},{13,15},{14,12},{15,11... | collective-permute-start | bytes 786440 | tf_op jit(solution)/shard_map/ppermute | solution.py:300
  80.1 6.8 %collective-permute-start.18 = (bf16[128,1024]{1,0:T(8,128)(2,1)S(1)}, bf16[128,1024]{1,0:T(8,128)(2,1)S(1)}, u32[]{:S(2)}, u32[]{:S(2)}) collective-permute-start(bf16[128,1024]{1,0:T(8,128)(2,1)S(1)} %collective-permute-done.17), channel_id=1, source_target_pairs={{0,1},{1,0},{2,3},{3,2},{4,5},{5,4},{6,7},{7,6},{8,9},{9,8},{10,11... | collective-permute-start | bytes 786440 | tf_op jit(solution)/shard_map/ppermute | solution.py:300
  83.6 6.4 %collective-permute-start.14 = (bf16[128,1024]{1,0:T(8,128)(2,1)S(1)}, bf16[128,1024]{1,0:T(8,128)(2,1)S(1)}, u32[]{:S(2)}, u32[]{:S(2)}) collective-permute-start(bf16[128,1024]{1,0:T(8,128)(2,1)S(1)} %add_convert_fusion.3), channel_id=1, source_target_pairs={{0,2},{1,5},{4,0},{5,9},{8,4},{9,13},{12,8},{13,15},{14,12},{15,11... | collective-permute-start | bytes 786440 | tf_op jit(solution)/shard_map/ppermute | solution.py:300

commit v7 on v6

--- a/solution.py
+++ b/solution.py
@@ -238,7 +238,7 @@
         out_specs=[VMEM] * len(outs),
         scratch_shapes=scratch,
         compiler_params=pltpu.CompilerParams(vmem_limit_bytes=LIMIT),
-        cost_estimate=pl.CostEstimate(flops=0, bytes_accessed=0, transcendentals=0),
+        cost_estimate=pl.CostEstimate(flops=50000000, bytes_accessed=0, transcendentals=0),
     )(dense, rows, *weights)
 
 

time: 91.3 us -> 91.3 us (level)
  no operation moved by 1% of the time
where the time goes in v7:
time: 91.3 us; the launch traced here: 90.9 us
  starting transfers between devices  31.5 us (35%)
  waiting for transfers between devices  28.1 us (31%)
  Pallas kernels  27.5 us (30%)
  other arithmetic  3.41 us (4%)
    ppermute x19, starting transfers between devices, send(): return lax.ppermute(rows, 'ctx', way)  21.6 us
    pallas_call x9, Pallas kernels, expert(): pl.pallas_call(functools.partial(expert_kernel, chips, offset, flip, expe...  18.8 us
    ppermute x19, waiting for transfers between devices, send(): return lax.ppermute(rows, 'ctx', way)  13.3 us
    all_to_all x1, waiting for transfers between devices, scan_states(): sums = lax.all_to_all(sums, BOTH, split_axis=0, concat_axis=0, tiled=True)  7.56 us
    all_to_all x1, starting transfers between devices, scan_states(): lax.all_to_all(pieces, BOTH, split_axis=0, concat_axis=0, tiled=True)  7.3 us
    all_to_all x1, waiting for transfers between devices, scan_states(): lax.all_to_all(pieces, BOTH, split_axis=0, concat_axis=0, tiled=True)  7.25 us
    pallas_call x1, Pallas kernels, attend_inside(): pl.pallas_call(functools.partial(inside_kernel, count), out_shape=outs, i...  4.12 us
    all_to_all x1, starting transfers between devices, scan_states(): sums = lax.all_to_all(sums, BOTH, split_axis=0, concat_axis=0, tiled=True)  2.59 us
  transfers between devices with their start and end apart: 21, of which 14 were waited for; matrix products, arithmetic and copies ran while one was open for 3% of the time, Pallas kernels for 28%

profile of v7, /device:TPU:0, one launch (start us, length us, event | category | flops | bytes accessed | tf_op | source)
XLA Modules:
  0.0 90.9 jit_solution(12719616657443093539)
XLA Ops:
  0.0 2.0 %shard_map.118.refs_6_ = bf16[1024,128]{1,0:T(8,128)(2,1)} custom-call(bf16[128,1024]{1,0:T(8,128)(2,1)} %refs_1_.2, bf16[128,1024]{1,0:T(8,128)(2,1)} %refs_2_.2), custom_call_target="tpu_custom_call" | custom-call | tf_op jit(solution)/shard_map/pallas_call | solution.py:263
  2.0 7.3 %all-to-all-start = ((bf16[32,32,128]{2,1,0:T(8,128)(2,1)}), bf16[32,32,128]{2,1,0:T(8,128)(2,1)S(1)}, u32[]{:S(2)}, u32[]{:S(2)}) async-start(bf16[32,32,128]{2,1,0:T(8,128)(2,1)} %bitcast), calls=%async_computation | async-start | bytes 524288 | tf_op jit(solution)/shard_map/all_to_all | solution.py:135
  9.3 0.3 collective-permute-start
  9.6 0.3 collective-permute-start.1
  9.9 0.3 collective-permute-start.4
  10.2 0.7 convert_reduce_fusion
  10.9 0.7 convert_divide_fusion
  11.6 0.7 select_reduce_fusion
  12.4 7.3 %all-to-all-done.pieces_ref = bf16[32,32,128]{2,1,0:T(8,128)(2,1)S(1)} async-done(((bf16[32,32,128]{2,1,0:T(8,128)(2,1)}), bf16[32,32,128]{2,1,0:T(8,128)(2,1)S(1)}, u32[]{:S(2)}, u32[]{:S(2)}) %all-to-all-start) | async-done | bytes 262176 | tf_op jit(solution)/shard_map/all_to_all | solution.py:135
  19.6 0.8 shard_map.119
  20.4 2.6 %all-to-all-start.1 = ((bf16[32,40,128]{2,1,0:T(8,128)(2,1)}), bf16[32,40,128]{2,1,0:T(8,128)(2,1)S(1)}, u32[]{:S(2)}, u32[]{:S(2)}) async-start(bf16[32,40,128]{2,1,0:T(8,128)(2,1)} %shard_map.119), calls=%async_computation.1 | async-start | bytes 655360 | tf_op jit(solution)/shard_map/all_to_all | solution.py:149
  23.0 4.1 %shard_map.120 = (bf16[128,1024]{1,0:T(8,128)(2,1)S(1)}, bf16[128,1024]{1,0:T(8,128)(2,1)}, bf16[128,1024]{1,0:T(8,128)(2,1)}, bf16[1024,1024]{1,0:T(8,128)(2,1)...) custom-call(bf16[128,1024]{1,0:T(8,128)(2,1)} %refs_0_.2, bf16[128,1024]{1,0:T(8,128)(2,1)} %refs_1_.2, ...), custom_call_target="tpu_custom_call" | custom-call | tf_op jit(solution)/shard_map/pallas_call | solution.py:102
  27.1 7.6 %all-to-all-done.1.sums_ref = bf16[32,40,128]{2,1,0:T(8,128)(2,1)S(1)} async-done(((bf16[32,40,128]{2,1,0:T(8,128)(2,1)}), bf16[32,40,128]{2,1,0:T(8,128)(2,1)S(1)}, u32[]{:S(2)}, u32[]{:S(2)}) %all-to-all-start.1) | async-done | bytes 327712 | tf_op jit(solution)/shard_map/all_to_all | solution.py:149
  34.7 1.8 %shard_map.121 = (f32[128,1024]{1,0:T(8,128)S(1)}, bf16[128,1024]{1,0:T(8,128)(2,1)S(1)}) custom-call(bf16[32,40,128]{2,1,0:T(8,128)(2,1)S(1)} %all-to-all-done.1.sums_ref, bf16[128,1024]{1,0:T(8,128)(2,1)S(1)} %get-tuple-element.30.q_ref, bf16[1024,1024]{1,0:T(8,128)(2,1)S(1)} %get-tuple-element.31.proj_ref, f32[1,1024]{1,0:T(1,128)S(1)} %get-tuple-element.32.gain_ref, ...), custom_call_target="tpu_custom_call" | custom-call | tf_op jit(solution)/shard_map/pallas_call | solution.py:283
  36.4 0.1 collective-permute-start.7
  36.5 1.1 %collective-permute-start.2 = (bf16[128,1024]{1,0:T(8,128)(2,1)S(1)}, bf16[128,1024]{1,0:T(8,128)(2,1)S(1)}, u32[]{:S(2)}, u32[]{:S(2)}) collective-permute-start(bf16[128,1024]{1,0:T(8,128)(2,1)S(1)} %get-tuple-element.53.rows_ref), channel_id=1, source_target_pairs={{0,4},{1,3},{4,8},{5,1},{8,12},{9,5},{12,14},{13,9},{14,10},{15,13... | collective-permute-start | bytes 786440 | tf_op jit(solution)/shard_map/ppermute | solution.py:300
  37.7 0.4 collective-permute-done.7
  38.1 1.0 %collective-permute-start.8 = (bf16[128,1024]{1,0:T(8,128)(2,1)S(1)}, bf16[128,1024]{1,0:T(8,128)(2,1)S(1)}, u32[]{:S(2)}, u32[]{:S(2)}) collective-permute-start(bf16[128,1024]{1,0:T(8,128)(2,1)S(1)} %collective-permute-done.7), channel_id=1, source_target_pairs={{0,4},{1,3},{4,8},{5,1},{8,12},{9,5},{12,14},{13,9},{14,10},{15,13... | collective-permute-start | bytes 786440 | tf_op jit(solution)/shard_map/ppermute | solution.py:300
  39.1 0.1 copy.29
  39.2 0.0 collective-permute-done.refs_3_
  39.2 0.0 collective-permute-done.1.refs_4_
  39.2 3.7 %shard_map.122 = (f32[128,1024]{1,0:T(8,128)S(1)}, bf16[1,1024,896]{2,1,0:T(8,128)(2,1)S(1)}, bf16[1,1024,896]{2,1,0:T(8,128)(2,1)S(1)}, bf16[1,896,1024]{2,1,0:...) custom-call(f32[128,32]{1,0:T(8,128)S(1)} %bitcast.24, ...), custom_call_target="tpu_custom_call" | custom-call | flops 50000000 | tf_op jit(solution)/shard_map/pallas_call | solution.py:234
  43.0 0.0 collective-permute-done.2.rows_ref
  43.0 1.0 %collective-permute-start.3 = (bf16[128,1024]{1,0:T(8,128)(2,1)S(1)}, bf16[128,1024]{1,0:T(8,128)(2,1)S(1)}, u32[]{:S(2)}, u32[]{:S(2)}) collective-permute-start(bf16[128,1024]{1,0:T(8,128)(2,1)S(1)} %collective-permute-done.2.rows_ref), channel_id=1, source_target_pairs={{0,4},{1,3},{4,8},{5,1},{8,12},{9,5},{12,14},{13,9},{14,10},{15,13... | collective-permute-start | bytes 786440 | tf_op jit(solution)/shard_map/ppermute | solution.py:300
  44.0 1.8 %collective-permute-done.8.rows_ref = bf16[128,1024]{1,0:T(8,128)(2,1)S(1)} collective-permute-done((bf16[128,1024]{1,0:T(8,128)(2,1)S(1)}, bf16[128,1024]{1,0:T(8,128)(2,1)S(1)}, u32[]{:S(2)}, u32[]{:S(2)}) %collective-permute-start.8) | collective-permute-done | bytes 262176 | tf_op jit(solution)/shard_map/ppermute | solution.py:300
  45.8 1.0 %collective-permute-start.9 = (bf16[128,1024]{1,0:T(8,128)(2,1)S(1)}, bf16[128,1024]{1,0:T(8,128)(2,1)S(1)}, u32[]{:S(2)}, u32[]{:S(2)}) collective-permute-start(bf16[128,1024]{1,0:T(8,128)(2,1)S(1)} %collective-permute-done.8.rows_ref), channel_id=1, source_target_pairs={{0,4},{1,3},{4,8},{5,1},{8,12},{9,5},{12,14},{13,9},{14,10},{15,13... | collective-permute-start | bytes 786440 | tf_op jit(solution)/shard_map/ppermute | solution.py:300
  46.8 0.0 collective-permute-done.4.refs_5_
  46.8 2.6 %shard_map.123 = (f32[128,1024]{1,0:T(8,128)S(1)}, bf16[1,896,1024]{2,1,0:T(8,128)(2,1)S(1)}) custom-call(f32[128,32]{1,0:T(8,128)S(1)} %bitcast.25, bf16[128,1024]{1,0:T(8,128)(2,1)S(1)} %collective-permute-done.2.rows_ref, bf16[1,1024,896]{2,1,0:T(8,128)(2,1)S(1)} %get-tuple-element.39.refs_0_, bf16[1,1024,896]{2,1,0:T(8,128)(2,1)S(1)} %get-tuple-element.40.refs_1_, ...), custom_call_target="tpu_custom_call" | custom-call | flops 50000000 | tf_op jit(solution)/shard_map/pallas_call | solution.py:234
  49.4 0.0 collective-permute-done.3.rows_ref
  49.4 1.0 %collective-permute-start.5 = (bf16[128,1024]{1,0:T(8,128)(2,1)S(1)}, bf16[128,1024]{1,0:T(8,128)(2,1)S(1)}, u32[]{:S(2)}, u32[]{:S(2)}) collective-permute-start(bf16[128,1024]{1,0:T(8,128)(2,1)S(1)} %collective-permute-done.3.rows_ref), channel_id=1, source_target_pairs={{0,4},{1,3},{4,8},{5,1},{8,12},{9,5},{12,14},{13,9},{14,10},{15,13... | collective-permute-start | bytes 786440 | tf_op jit(solution)/shard_map/ppermute | solution.py:300
  50.4 1.9 %shard_map.125 = f32[128,1024]{1,0:T(8,128)S(1)} custom-call(f32[128,32]{1,0:T(8,128)S(1)} %bitcast.26, bf16[128,1024]{1,0:T(8,128)(2,1)S(1)} %collective-permute-done.8.rows_ref, bf16[1,1024,896]{2,1,0:T(8,128)(2,1)S(1)} %get-tuple-element.39.refs_0_, bf16[1,1024,896]{2,1,0:T(8,128)(2,1)S(1)} %get-tuple-element.40.refs_1_, ...), custom_call_target="tpu_custom_call" | custom-call | flops 50000000 | tf_op jit(solution)/shard_map/pallas_call | solution.py:234
  52.3 0.0 collective-permute-done.9.rows_ref
  52.3 1.1 %collective-permute-start.10 = (bf16[128,1024]{1,0:T(8,128)(2,1)S(1)}, bf16[128,1024]{1,0:T(8,128)(2,1)S(1)}, u32[]{:S(2)}, u32[]{:S(2)}) collective-permute-start(bf16[128,1024]{1,0:T(8,128)(2,1)S(1)} %collective-permute-done.9.rows_ref), channel_id=1, source_target_pairs={{0,4},{1,3},{4,8},{5,1},{8,12},{9,5},{12,14},{13,9},{14,10},{15,13... | collective-permute-start | bytes 786440 | tf_op jit(solution)/shard_map/ppermute | solution.py:300
  53.4 1.9 %shard_map.124 = f32[128,1024]{1,0:T(8,128)S(1)} custom-call(f32[128,32]{1,0:T(8,128)S(1)} %bitcast.27, bf16[128,1024]{1,0:T(8,128)(2,1)S(1)} %collective-permute-done.3.rows_ref, bf16[1,1024,896]{2,1,0:T(8,128)(2,1)S(1)} %get-tuple-element.39.refs_0_, bf16[1,1024,896]{2,1,0:T(8,128)(2,1)S(1)} %get-tuple-element.40.refs_1_, ...), custom_call_target="tpu_custom_call" | custom-call | flops 50000000 | tf_op jit(solution)/shard_map/pallas_call | solution.py:234
  55.3 0.5 collective-permute-done.5.rows_ref
  55.8 0.9 %collective-permute-start.6 = (bf16[128,1024]{1,0:T(8,128)(2,1)S(1)}, bf16[128,1024]{1,0:T(8,128)(2,1)S(1)}, u32[]{:S(2)}, u32[]{:S(2)}) collective-permute-start(bf16[128,1024]{1,0:T(8,128)(2,1)S(1)} %collective-permute-done.5.rows_ref), channel_id=1, source_target_pairs={{0,4},{1,3},{4,8},{5,1},{8,12},{9,5},{12,14},{13,9},{14,10},{15,13... | collective-permute-start | bytes 786440 | tf_op jit(solution)/shard_map/ppermute | solution.py:300
  56.7 1.9 %shard_map.126 = f32[128,1024]{1,0:T(8,128)S(1)} custom-call(f32[128,32]{1,0:T(8,128)S(1)} %bitcast.28, bf16[128,1024]{1,0:T(8,128)(2,1)S(1)} %collective-permute-done.9.rows_ref, bf16[1,1024,896]{2,1,0:T(8,128)(2,1)S(1)} %get-tuple-element.39.refs_0_, bf16[1,1024,896]{2,1,0:T(8,128)(2,1)S(1)} %get-tuple-element.40.refs_1_, ...), custom_call_target="tpu_custom_call" | custom-call | flops 50000000 | tf_op jit(solution)/shard_map/pallas_call | solution.py:234
  58.7 0.1 collective-permute-done.10.rows_ref
  58.7 1.9 %shard_map.127 = f32[128,1024]{1,0:T(8,128)S(1)} custom-call(f32[128,32]{1,0:T(8,128)S(1)} %bitcast.29, bf16[128,1024]{1,0:T(8,128)(2,1)S(1)} %collective-permute-done.10.rows_ref, bf16[1,1024,896]{2,1,0:T(8,128)(2,1)S(1)} %get-tuple-element.39.refs_0_, bf16[1,1024,896]{2,1,0:T(8,128)(2,1)S(1)} %get-tuple-element.40.refs_1_, ...), custom_call_target="tpu_custom_call" | custom-call | flops 50000000 | tf_op jit(solution)/shard_map/pallas_call | solution.py:234
  60.7 1.3 %collective-permute-start.15 = (bf16[128,1024]{1,0:T(8,128)(2,1)S(1)}, bf16[128,1024]{1,0:T(8,128)(2,1)S(1)}, u32[]{:S(2)}, u32[]{:S(2)}) collective-permute-start(bf16[128,1024]{1,0:T(8,128)(2,1)S(1)} %convert_element_type.75), channel_id=1, source_target_pairs={{0,2},{1,5},{4,0},{5,9},{8,4},{9,13},{12,8},{13,15},{14,12},{15,11... | collective-permute-start | bytes 786440 | tf_op jit(solution)/shard_map/ppermute | solution.py:300
  62.0 0.2 collective-permute-done.6.rows_ref
  62.2 1.9 %shard_map.128 = f32[128,1024]{1,0:T(8,128)S(1)} custom-call(f32[128,32]{1,0:T(8,128)S(1)} %bitcast.30, bf16[128,1024]{1,0:T(8,128)(2,1)S(1)} %collective-permute-done.6.rows_ref, bf16[1,1024,896]{2,1,0:T(8,128)(2,1)S(1)} %get-tuple-element.39.refs_0_, bf16[1,1024,896]{2,1,0:T(8,128)(2,1)S(1)} %get-tuple-element.40.refs_1_, ...), custom_call_target="tpu_custom_call" | custom-call | flops 50000000 | tf_op jit(solution)/shard_map/pallas_call | solution.py:234
  64.2 2.2 %collective-permute-start.11 = (bf16[128,1024]{1,0:T(8,128)(2,1)S(1)}, bf16[128,1024]{1,0:T(8,128)(2,1)S(1)}, u32[]{:S(2)}, u32[]{:S(2)}) collective-permute-start(bf16[128,1024]{1,0:T(8,128)(2,1)S(1)} %convert_element_type.67), channel_id=1, source_target_pairs={{0,2},{1,5},{4,0},{5,9},{8,4},{9,13},{12,8},{13,15},{14,12},{15,11... | collective-permute-start | bytes 786440 | tf_op jit(solution)/shard_map/ppermute | solution.py:300
  66.4 0.7 collective-permute-done.15
  67.1 0.1 add_convert_fusion.2
  67.2 1.3 %collective-permute-start.16 = (bf16[128,1024]{1,0:T(8,128)(2,1)S(1)}, bf16[128,1024]{1,0:T(8,128)(2,1)S(1)}, u32[]{:S(2)}, u32[]{:S(2)}) collective-permute-start(bf16[128,1024]{1,0:T(8,128)(2,1)S(1)} %add_convert_fusion.2), channel_id=1, source_target_pairs={{0,2},{1,5},{4,0},{5,9},{8,4},{9,13},{12,8},{13,15},{14,12},{15,11... | collective-permute-start | bytes 786440 | tf_op jit(solution)/shard_map/ppermute | solution.py:300
  68.5 1.9 %shard_map.129 = f32[128,1024]{1,0:T(8,128)S(1)} custom-call(f32[128,32]{1,0:T(8,128)S(1)} %bitcast.31, bf16[128,1024]{1,0:T(8,128)(2,1)S(1)} %collective-permute-done.5.rows_ref, bf16[1,1024,896]{2,1,0:T(8,128)(2,1)S(1)} %get-tuple-element.39.refs_0_, bf16[1,1024,896]{2,1,0:T(8,128)(2,1)S(1)} %get-tuple-element.40.refs_1_, ...), custom_call_target="tpu_custom_call" | custom-call | flops 50000000 | tf_op jit(solution)/shard_map/pallas_call | solution.py:234
  70.4 0.2 collective-permute-done.11
  70.6 0.1 add_convert_fusion.5
  70.6 2.2 %collective-permute-start.12 = (bf16[128,1024]{1,0:T(8,128)(2,1)S(1)}, bf16[128,1024]{1,0:T(8,128)(2,1)S(1)}, u32[]{:S(2)}, u32[]{:S(2)}) collective-permute-start(bf16[128,1024]{1,0:T(8,128)(2,1)S(1)} %add_convert_fusion.5), channel_id=1, source_target_pairs={{0,2},{1,5},{4,0},{5,9},{8,4},{9,13},{12,8},{13,15},{14,12},{15,11... | collective-permute-start | bytes 786440 | tf_op jit(solution)/shard_map/ppermute | solution.py:300
  72.9 0.7 collective-permute-done.16
  73.6 0.1 add_convert_fusion.1
  73.7 2.0 %collective-permute-start.17 = (bf16[128,1024]{1,0:T(8,128)(2,1)S(1)}, bf16[128,1024]{1,0:T(8,128)(2,1)S(1)}, u32[]{:S(2)}, u32[]{:S(2)}) collective-permute-start(bf16[128,1024]{1,0:T(8,128)(2,1)S(1)} %add_convert_fusion.1), channel_id=1, source_target_pairs={{0,2},{1,5},{4,0},{5,9},{8,4},{9,13},{12,8},{13,15},{14,12},{15,11... | collective-permute-start | bytes 786440 | tf_op jit(solution)/shard_map/ppermute | solution.py:300
  75.7 1.4 %collective-permute-done.12 = bf16[128,1024]{1,0:T(8,128)(2,1)S(1)} collective-permute-done((bf16[128,1024]{1,0:T(8,128)(2,1)S(1)}, bf16[128,1024]{1,0:T(8,128)(2,1)S(1)}, u32[]{:S(2)}, u32[]{:S(2)}) %collective-permute-start.12) | collective-permute-done | bytes 262176 | tf_op jit(solution)/shard_map/ppermute | solution.py:300
  77.1 0.1 add_convert_fusion.4
  77.1 2.2 %collective-permute-start.13 = (bf16[128,1024]{1,0:T(8,128)(2,1)S(1)}, bf16[128,1024]{1,0:T(8,128)(2,1)S(1)}, u32[]{:S(2)}, u32[]{:S(2)}) collective-permute-start(bf16[128,1024]{1,0:T(8,128)(2,1)S(1)} %add_convert_fusion.4), channel_id=1, source_target_pairs={{0,2},{1,5},{4,0},{5,9},{8,4},{9,13},{12,8},{13,15},{14,12},{15,11... | collective-permute-start | bytes 786440 | tf_op jit(solution)/shard_map/ppermute | solution.py:300
  79.4 0.7 collective-permute-done.17
  80.1 3.5 %collective-permute-done.13 = bf16[128,1024]{1,0:T(8,128)(2,1)S(1)} collective-permute-done((bf16[128,1024]{1,0:T(8,128)(2,1)S(1)}, bf16[128,1024]{1,0:T(8,128)(2,1)S(1)}, u32[]{:S(2)}, u32[]{:S(2)}) %collective-permute-start.13) | collective-permute-done | bytes 262176 | tf_op jit(solution)/shard_map/ppermute | solution.py:300
  83.6 0.1 add_convert_fusion.3
  83.6 2.2 %collective-permute-start.14 = (bf16[128,1024]{1,0:T(8,128)(2,1)S(1)}, bf16[128,1024]{1,0:T(8,128)(2,1)S(1)}, u32[]{:S(2)}, u32[]{:S(2)}) collective-permute-start(bf16[128,1024]{1,0:T(8,128)(2,1)S(1)} %add_convert_fusion.3), channel_id=1, source_target_pairs={{0,2},{1,5},{4,0},{5,9},{8,4},{9,13},{12,8},{13,15},{14,12},{15,11... | collective-permute-start | bytes 786440 | tf_op jit(solution)/shard_map/ppermute | solution.py:300
  85.8 1.0 %shard_map.130 = f32[128,1024]{1,0:T(8,128)S(1)} custom-call(f32[128,32]{1,0:T(8,128)S(1)} %bitcast.32, bf16[128,1024]{1,0:T(8,128)(2,1)S(1)} %get-tuple-element.53.rows_ref, bf16[1,1024,896]{2,1,0:T(8,128)(2,1)S(1)} %get-tuple-element.42.refs_3_.refs_0_, bf16[1,1024,896]{2,1,0:T(8,128)(2,1)S(1)} %get-tuple-element.43.refs_4_.refs_1_, ...), custom_call_target="tpu_custom_call" | custom-call | flops 50000000 | tf_op jit(solution)/shard_map/pallas_call | solution.py:234
  86.9 0.0 collective-permute-done.18
  86.9 3.1 %collective-permute-done.14 = bf16[128,1024]{1,0:T(8,128)(2,1)S(1)} collective-permute-done((bf16[128,1024]{1,0:T(8,128)(2,1)S(1)}, bf16[128,1024]{1,0:T(8,128)(2,1)S(1)}, u32[]{:S(2)}, u32[]{:S(2)}) %collective-permute-start.14) | collective-permute-done | bytes 262176 | tf_op jit(solution)/shard_map/ppermute | solution.py:300
  90.0 0.9 add_convert_fusion
  (12 shorter events, 0.2 us)
Async XLA Ops:
  2.0 17.6 %all-to-all-start = ((bf16[32,32,128]{2,1,0:T(8,128)(2,1)}), bf16[32,32,128]{2,1,0:T(8,128)(2,1)S(1)}, u32[]{:S(2)}, u32[]{:S(2)}) async-start(bf16[32,32,128]{2,1,0:T(8,128)(2,1)} %bitcast), calls=%async_computation | async-start | bytes 524288 | tf_op jit(solution)/shard_map/all_to_all | solution.py:135
  9.3 29.9 %collective-permute-start = (bf16[1,1024,896]{2,1,0:T(8,128)(2,1)}, bf16[1,1024,896]{2,1,0:T(8,128)(2,1)}, u32[]{:S(2)}, u32[]{:S(2)}) collective-permute-start(bf16[1,1024,896]{2,1,0:T(8,128)(2,1)} %refs_0_.3), channel_id=1, source_target_pairs={{0,1},{1,0},{2,3},{3,2},{4,5},{5,4},{6,7},{7,6},{8,9},{9,8},{10,11... | collective-permute-start | bytes 5505032 | tf_op jit(solution)/shard_map/ppermute | solution.py:300
  9.6 29.6 %collective-permute-start.1 = (bf16[1,1024,896]{2,1,0:T(8,128)(2,1)}, bf16[1,1024,896]{2,1,0:T(8,128)(2,1)}, u32[]{:S(2)}, u32[]{:S(2)}) collective-permute-start(bf16[1,1024,896]{2,1,0:T(8,128)(2,1)} %refs_1_.3), channel_id=1, source_target_pairs={{0,1},{1,0},{2,3},{3,2},{4,5},{5,4},{6,7},{7,6},{8,9},{9,8},{10,11... | collective-permute-start | bytes 5505032 | tf_op jit(solution)/shard_map/ppermute | solution.py:300
  9.9 36.9 %collective-permute-start.4 = (bf16[1,896,1024]{2,1,0:T(8,128)(2,1)}, bf16[1,896,1024]{2,1,0:T(8,128)(2,1)}, u32[]{:S(2)}, u32[]{:S(2)}) collective-permute-start(bf16[1,896,1024]{2,1,0:T(8,128)(2,1)} %refs_2_.3), channel_id=1, source_target_pairs={{0,1},{1,0},{2,3},{3,2},{4,5},{5,4},{6,7},{7,6},{8,9},{9,8},{10,11... | collective-permute-start | bytes 5505032 | tf_op jit(solution)/shard_map/ppermute | solution.py:300
  20.4 14.3 %all-to-all-start.1 = ((bf16[32,40,128]{2,1,0:T(8,128)(2,1)}), bf16[32,40,128]{2,1,0:T(8,128)(2,1)S(1)}, u32[]{:S(2)}, u32[]{:S(2)}) async-start(bf16[32,40,128]{2,1,0:T(8,128)(2,1)} %shard_map.119), calls=%async_computation.1 | async-start | bytes 655360 | tf_op jit(solution)/shard_map/all_to_all | solution.py:149
  36.4 1.6 %collective-permute-start.7 = (bf16[128,1024]{1,0:T(8,128)(2,1)S(1)}, bf16[128,1024]{1,0:T(8,128)(2,1)S(1)}, u32[]{:S(2)}, u32[]{:S(2)}) collective-permute-start(bf16[128,1024]{1,0:T(8,128)(2,1)S(1)} %get-tuple-element.53.rows_ref), channel_id=1, source_target_pairs={{0,1},{1,0},{2,3},{3,2},{4,5},{5,4},{6,7},{7,6},{8,9},{9,8},{10,11... | collective-permute-start | bytes 786440 | tf_op jit(solution)/shard_map/ppermute | solution.py:300
  36.5 6.5 %collective-permute-start.2 = (bf16[128,1024]{1,0:T(8,128)(2,1)S(1)}, bf16[128,1024]{1,0:T(8,128)(2,1)S(1)}, u32[]{:S(2)}, u32[]{:S(2)}) collective-permute-start(bf16[128,1024]{1,0:T(8,128)(2,1)S(1)} %get-tuple-element.53.rows_ref), channel_id=1, source_target_pairs={{0,4},{1,3},{4,8},{5,1},{8,12},{9,5},{12,14},{13,9},{14,10},{15,13... | collective-permute-start | bytes 786440 | tf_op jit(solution)/shard_map/ppermute | solution.py:300
  38.1 7.7 %collective-permute-start.8 = (bf16[128,1024]{1,0:T(8,128)(2,1)S(1)}, bf16[128,1024]{1,0:T(8,128)(2,1)S(1)}, u32[]{:S(2)}, u32[]{:S(2)}) collective-permute-start(bf16[128,1024]{1,0:T(8,128)(2,1)S(1)} %collective-permute-done.7), channel_id=1, source_target_pairs={{0,4},{1,3},{4,8},{5,1},{8,12},{9,5},{12,14},{13,9},{14,10},{15,13... | collective-permute-start | bytes 786440 | tf_op jit(solution)/shard_map/ppermute | solution.py:300
  43.0 6.4 %collective-permute-start.3 = (bf16[128,1024]{1,0:T(8,128)(2,1)S(1)}, bf16[128,1024]{1,0:T(8,128)(2,1)S(1)}, u32[]{:S(2)}, u32[]{:S(2)}) collective-permute-start(bf16[128,1024]{1,0:T(8,128)(2,1)S(1)} %collective-permute-done.2.rows_ref), channel_id=1, source_target_pairs={{0,4},{1,3},{4,8},{5,1},{8,12},{9,5},{12,14},{13,9},{14,10},{15,13... | collective-permute-start | bytes 786440 | tf_op jit(solution)/shard_map/ppermute | solution.py:300
  45.8 6.5 %collective-permute-start.9 = (bf16[128,1024]{1,0:T(8,128)(2,1)S(1)}, bf16[128,1024]{1,0:T(8,128)(2,1)S(1)}, u32[]{:S(2)}, u32[]{:S(2)}) collective-permute-start(bf16[128,1024]{1,0:T(8,128)(2,1)S(1)} %collective-permute-done.8.rows_ref), channel_id=1, source_target_pairs={{0,4},{1,3},{4,8},{5,1},{8,12},{9,5},{12,14},{13,9},{14,10},{15,13... | collective-permute-start | bytes 786440 | tf_op jit(solution)/shard_map/ppermute | solution.py:300
  49.4 6.4 %collective-permute-start.5 = (bf16[128,1024]{1,0:T(8,128)(2,1)S(1)}, bf16[128,1024]{1,0:T(8,128)(2,1)S(1)}, u32[]{:S(2)}, u32[]{:S(2)}) collective-permute-start(bf16[128,1024]{1,0:T(8,128)(2,1)S(1)} %collective-permute-done.3.rows_ref), channel_id=1, source_target_pairs={{0,4},{1,3},{4,8},{5,1},{8,12},{9,5},{12,14},{13,9},{14,10},{15,13... | collective-permute-start | bytes 786440 | tf_op jit(solution)/shard_map/ppermute | solution.py:300
  52.3 6.4 %collective-permute-start.10 = (bf16[128,1024]{1,0:T(8,128)(2,1)S(1)}, bf16[128,1024]{1,0:T(8,128)(2,1)S(1)}, u32[]{:S(2)}, u32[]{:S(2)}) collective-permute-start(bf16[128,1024]{1,0:T(8,128)(2,1)S(1)} %collective-permute-done.9.rows_ref), channel_id=1, source_target_pairs={{0,4},{1,3},{4,8},{5,1},{8,12},{9,5},{12,14},{13,9},{14,10},{15,13... | collective-permute-start | bytes 786440 | tf_op jit(solution)/shard_map/ppermute | solution.py:300
  55.8 6.4 %collective-permute-start.6 = (bf16[128,1024]{1,0:T(8,128)(2,1)S(1)}, bf16[128,1024]{1,0:T(8,128)(2,1)S(1)}, u32[]{:S(2)}, u32[]{:S(2)}) collective-permute-start(bf16[128,1024]{1,0:T(8,128)(2,1)S(1)} %collective-permute-done.5.rows_ref), channel_id=1, source_target_pairs={{0,4},{1,3},{4,8},{5,1},{8,12},{9,5},{12,14},{13,9},{14,10},{15,13... | collective-permute-start | bytes 786440 | tf_op jit(solution)/shard_map/ppermute | solution.py:300
  60.7 6.4 %collective-permute-start.15 = (bf16[128,1024]{1,0:T(8,128)(2,1)S(1)}, bf16[128,1024]{1,0:T(8,128)(2,1)S(1)}, u32[]{:S(2)}, u32[]{:S(2)}) collective-permute-start(bf16[128,1024]{1,0:T(8,128)(2,1)S(1)} %convert_element_type.75), channel_id=1, source_target_pairs={{0,2},{1,5},{4,0},{5,9},{8,4},{9,13},{12,8},{13,15},{14,12},{15,11... | collective-permute-start | bytes 786440 | tf_op jit(solution)/shard_map/ppermute | solution.py:300
  64.2 6.4 %collective-permute-start.11 = (bf16[128,1024]{1,0:T(8,128)(2,1)S(1)}, bf16[128,1024]{1,0:T(8,128)(2,1)S(1)}, u32[]{:S(2)}, u32[]{:S(2)}) collective-permute-start(bf16[128,1024]{1,0:T(8,128)(2,1)S(1)} %convert_element_type.67), channel_id=1, source_target_pairs={{0,2},{1,5},{4,0},{5,9},{8,4},{9,13},{12,8},{13,15},{14,12},{15,11... | collective-permute-start | bytes 786440 | tf_op jit(solution)/shard_map/ppermute | solution.py:300
  67.2 6.4 %collective-permute-start.16 = (bf16[128,1024]{1,0:T(8,128)(2,1)S(1)}, bf16[128,1024]{1,0:T(8,128)(2,1)S(1)}, u32[]{:S(2)}, u32[]{:S(2)}) collective-permute-start(bf16[128,1024]{1,0:T(8,128)(2,1)S(1)} %add_convert_fusion.2), channel_id=1, source_target_pairs={{0,2},{1,5},{4,0},{5,9},{8,4},{9,13},{12,8},{13,15},{14,12},{15,11... | collective-permute-start | bytes 786440 | tf_op jit(solution)/shard_map/ppermute | solution.py:300
  70.6 6.4 %collective-permute-start.12 = (bf16[128,1024]{1,0:T(8,128)(2,1)S(1)}, bf16[128,1024]{1,0:T(8,128)(2,1)S(1)}, u32[]{:S(2)}, u32[]{:S(2)}) collective-permute-start(bf16[128,1024]{1,0:T(8,128)(2,1)S(1)} %add_convert_fusion.5), channel_id=1, source_target_pairs={{0,2},{1,5},{4,0},{5,9},{8,4},{9,13},{12,8},{13,15},{14,12},{15,11... | collective-permute-start | bytes 786440 | tf_op jit(solution)/shard_map/ppermute | solution.py:300
  73.7 6.4 %collective-permute-start.17 = (bf16[128,1024]{1,0:T(8,128)(2,1)S(1)}, bf16[128,1024]{1,0:T(8,128)(2,1)S(1)}, u32[]{:S(2)}, u32[]{:S(2)}) collective-permute-start(bf16[128,1024]{1,0:T(8,128)(2,1)S(1)} %add_convert_fusion.1), channel_id=1, source_target_pairs={{0,2},{1,5},{4,0},{5,9},{8,4},{9,13},{12,8},{13,15},{14,12},{15,11... | collective-permute-start | bytes 786440 | tf_op jit(solution)/shard_map/ppermute | solution.py:300
  77.1 6.4 %collective-permute-start.13 = (bf16[128,1024]{1,0:T(8,128)(2,1)S(1)}, bf16[128,1024]{1,0:T(8,128)(2,1)S(1)}, u32[]{:S(2)}, u32[]{:S(2)}) collective-permute-start(bf16[128,1024]{1,0:T(8,128)(2,1)S(1)} %add_convert_fusion.4), channel_id=1, source_target_pairs={{0,2},{1,5},{4,0},{5,9},{8,4},{9,13},{12,8},{13,15},{14,12},{15,11... | collective-permute-start | bytes 786440 | tf_op jit(solution)/shard_map/ppermute | solution.py:300
  80.1 6.8 %collective-permute-start.18 = (bf16[128,1024]{1,0:T(8,128)(2,1)S(1)}, bf16[128,1024]{1,0:T(8,128)(2,1)S(1)}, u32[]{:S(2)}, u32[]{:S(2)}) collective-permute-start(bf16[128,1024]{1,0:T(8,128)(2,1)S(1)} %collective-permute-done.17), channel_id=1, source_target_pairs={{0,1},{1,0},{2,3},{3,2},{4,5},{5,4},{6,7},{7,6},{8,9},{9,8},{10,11... | collective-permute-start | bytes 786440 | tf_op jit(solution)/shard_map/ppermute | solution.py:300
  83.6 6.4 %collective-permute-start.14 = (bf16[128,1024]{1,0:T(8,128)(2,1)S(1)}, bf16[128,1024]{1,0:T(8,128)(2,1)S(1)}, u32[]{:S(2)}, u32[]{:S(2)}) collective-permute-start(bf16[128,1024]{1,0:T(8,128)(2,1)S(1)} %add_convert_fusion.3), channel_id=1, source_target_pairs={{0,2},{1,5},{4,0},{5,9},{8,4},{9,13},{12,8},{13,15},{14,12},{15,11... | collective-permute-start | bytes 786440 | tf_op jit(solution)/shard_map/ppermute | solution.py:300
